TPU v7x, 256 devices: a whole 4x4x8 slice. The times are simulated.
256 devices in a mesh: slab: 32 (over z, x_lo, core), depth: 8 (over y, x_hi).
Axes of the slice: x: 4 (x_hi: 2, x_lo: 2; x = x_hi * 2 + x_lo), y: 4, z: 8, core: 2. Of those that a mesh axis runs over, the one named last changes fastest.
Arguments:
- pressure: float32 [16, 2048, 2048], P('depth', 'slab'), may hold values from -6 to 6
- zone_labels: int32 [16, 2048, 2048], P('depth', 'slab'), may hold values from 0 to 15
- perm_table: float32 [16], replicated, may hold values from 0.02 to 1
- asig_table: float32 [16], replicated, may hold values from 0.5 to 2
- well_cells: int32 [512, 3], replicated, may hold values from 0 to 2047, as said below
- rate_levels: int32 [2, 512], replicated, may hold values from 0 to 7
- green_spectrum: float32 [2048, 2048], P(None, 'slab'), may hold values from -1 to 1, as said below
- seis_state: float32 [16, 2048, 2048], P('depth', 'slab'), may hold values from 0.3 to 3
Outputs:
- pressure_out: float32 [16, 2048, 2048], P('depth', 'slab')
- state_out: float32 [16, 2048, 2048], P('depth', 'slab')
- rate_map: float32 [2048, 2048], P('slab', 'depth')
Inputs may be any that keep to these rules, and one draw needn't show every extreme that they name: `well_cells`: column 0 lies below 16, column 1 below 2048, column 2 below 2048; several wells may share a cell. green_spectrum at (kx, ky) equals its value at ((2048 - kx) % 2048, (2048 - ky) % 2048).
All inputs are finite; a program needn't handle non-finite values.
Results may differ from a plain program's by a relative error of at most 0.00019.
Values sent between devices are 32-bit elements; how exact they have to be, the bound alone decides.
No kernel may reach another device: no remote copies, remote signals or barrier semaphores. Data moves between devices by JAX's collectives and lax.ppermute only.
A program may use at most 128 MiB of HBM per device.

v0:
```python
import functools
import math

import jax
import jax.numpy as jnp
import ml_dtypes
import numpy as np
from jax import lax
from jax.experimental import pallas as pl
from jax.experimental.pallas import tpu as pltpu
from jax.sharding import PartitionSpec as P

conduct = 0.15
rate_unit = 0.5
friction = 0.6
recovery = 0.6065306597126334

LANES = 128
SLABS = 32
DEPTHS = 8
N = 2048
ROWS = N // SLABS
TILES = N // LANES
PAIRS = TILES // 2
FREQS = LANES // SLABS
STEP = SLABS * FREQS
PARAMS = pltpu.CompilerParams(vmem_limit_bytes=48 * 1024 * 1024)
F32 = jnp.float32
BF16 = jnp.bfloat16


def blocks(theta):
    cos, sin = np.cos(theta), np.sin(theta)
    return np.stack([np.stack([cos, -sin]), np.stack([sin, cos])])


def halves(table):
    high = table.astype(ml_dtypes.bfloat16)
    low = (table - high.astype(np.float64)).astype(ml_dtypes.bfloat16)
    return high, low


def left_table(table):
    high, low = halves(table)
    return np.concatenate([high, high, low], 1)


def right_table(table):
    high, low = halves(table)
    return np.concatenate([high, high, low], 0)


@functools.lru_cache(maxsize=None)
def tables():
    two_pi = 2.0 * np.pi
    k2, n2 = np.arange(128)[:, None], np.arange(128)[None, :]
    fwd = blocks(-two_pi * ((k2 * n2) % 128) / 128)
    fwd = fwd.reshape(2, 2, SLABS, FREQS, 128).transpose(2, 0, 3, 1, 4).reshape(256, 256)
    inv = blocks(two_pi * ((k2 * n2) % 128) / 128)
    inv = inv.reshape(2, 2, 128, SLABS, FREQS).transpose(3, 1, 4, 0, 2).reshape(256, 256)
    s, k = np.arange(SLABS)[:, None], np.arange(SLABS)[None, :]
    eye = np.eye(FREQS)
    mid = blocks(-two_pi * ((s * k) % SLABS) / SLABS)
    mid = np.einsum("abks,ij->akisbj", mid, eye)
    mid = mid.reshape(256, 256)
    mid_inv = blocks(two_pi * ((s * k) % SLABS) / SLABS)
    mid_inv = np.einsum("absk,ij->saibkj", mid_inv, eye).reshape(256, 256)
    r, q = np.arange(ROWS)[:, None], np.arange(ROWS)[None, :]
    two = np.eye(2)
    inner = blocks(-two_pi * ((r * q) % ROWS) / ROWS)
    inner = np.einsum("abqr,ij->bjraiq", inner, two).reshape(256, 256)
    inner_inv = blocks(two_pi * ((r * q) % ROWS) / ROWS)
    inner_inv = np.einsum("abrq,ij->bjqair", inner_inv, two).reshape(256, 256)
    row_angle = -two_pi * ((np.arange(TILES)[:, None] * np.arange(128)[None, :]) % N) / N
    row_twist = np.stack([np.cos(row_angle), np.sin(row_angle)]).astype(np.float32)
    col_angle = -two_pi * ((np.arange(SLABS)[:, None] * np.arange(ROWS)[None, :]) % N) / N
    col_angle = np.tile(np.repeat(col_angle, FREQS, 0), (1, 2))
    col_twist = np.stack([np.cos(col_angle), np.sin(col_angle)]).astype(np.float32)
    return {
        "fwd": left_table(fwd),
        "inv": right_table(inv),
        "mid": left_table(mid),
        "mid_inv": left_table(mid_inv),
        "inner": right_table(inner),
        "inner_inv": right_table(inner_inv),
        "row_twist": row_twist,
        "col_twist": col_twist,
    }


def triple(value, axis):
    high = value.astype(BF16)
    low = (value - high.astype(F32)).astype(BF16)
    return jnp.concatenate([high, low, high], axis)


def matmul(left, right):
    return jnp.dot(left, right, preferred_element_type=F32)


def radix4(items, sign):
    (ar, ai), (br, bi), (cr, ci), (dr, di) = items
    pr, pi, mr, mi = ar + cr, ai + ci, ar - cr, ai - ci
    qr, qi, nr, ni = br + dr, bi + di, br - dr, bi - di
    tr, ti = (-ni, nr) if sign > 0 else (ni, -nr)
    return [(pr + qr, pi + qi), (mr + tr, mi + ti), (pr - qr, pi - qi), (mr - tr, mi - ti)]


def scale_by(item, angle):
    c, s = math.cos(angle), math.sin(angle)
    re, im = item
    if abs(s) < 1e-12:
        return (re, im) if c > 0 else (-re, -im)
    if abs(c) < 1e-12:
        return (-im, re) if s > 0 else (im, -re)
    return (re * c - im * s, re * s + im * c)


def dft16(items, sign):
    mids = [radix4([items[4 * b + a] for b in range(4)], sign) for a in range(4)]
    out = [None] * 16
    for k in range(4):
        column = [scale_by(mids[a][k], sign * 2.0 * math.pi * a * k / 16) for a in range(4)]
        for m, item in enumerate(radix4(column, sign)):
            out[k + 4 * m] = item
    return out


def pick(label, table, bit, base):
    if bit < 0:
        return table[base]
    mask = (label & (1 << bit)) != 0
    return jnp.where(mask, pick(label, table, bit - 1, base + (1 << bit)), pick(label, table, bit - 1, base))


def lookup_kernel(root_ref, inv_ref, label_ref, root_out, inv_out):
    width = 512

    def body(i, carry):
        for l in range(2):
            for c in range(N // width):
                rows, cols = pl.ds(pl.multiple_of(i * 8, 8), 8), pl.ds(c * width, width)
                label = label_ref[l, rows, cols]
                root_out[l, rows, cols] = pick(label, root_ref, 3, 0)
                inv_out[l, rows, cols] = pick(label, inv_ref, 3, 0)
        return carry

    lax.fori_loop(0, ROWS // 8, body, 0)


def wells_kernel(where_ref, amount_ref, col_ref, out_ref):
    row = lax.broadcasted_iota(jnp.int32, (128, 512), 0)
    hit = row == where_ref[...]
    left = [jnp.where(hit, amount_ref[s : s + 1, :], 0.0).astype(BF16) for s in range(2)]
    left = jnp.concatenate(left, 0)
    col_of = jnp.broadcast_to(col_ref[...], (512, 256))
    for c in range(N // 256):
        col = lax.broadcasted_iota(jnp.int32, (512, 256), 1) + c * 256
        right = jnp.where(col == col_of, 1.0, 0.0).astype(BF16)
        out_ref[:, c * 256 : (c + 1) * 256] = matmul(left, right)


def neighbours(padded, own, c, before, after, row, lane):
    left = jnp.where(lane == 0, pltpu.roll(padded[:, pl.ds(pl.multiple_of(c * 128, 128), 128)], 1, 1), pltpu.roll(own, 1, 1))
    right = jnp.where(
        lane == 127,
        pltpu.roll(padded[:, pl.ds(pl.multiple_of(c * 128 + 256, 128), 128)], 127, 1),
        pltpu.roll(own, 127, 1),
    )
    up = jnp.where(row == 0, before, pltpu.roll(own, 1, 0))
    down = jnp.where(row == ROWS - 1, after, pltpu.roll(own, ROWS - 1, 0))
    return (left + right) + (up + down)


def clear_ends(pad_ref):
    zero = jnp.zeros((ROWS, LANES), F32)
    for l in range(2):
        pad_ref[l, :, 0:128] = zero
        pad_ref[l, :, N + 128 : N + 256] = zero


def tile_at(c):
    return pl.ds(pl.multiple_of(c * 128, 128), 128)


def pad_at(c):
    return pl.ds(pl.multiple_of(c * 128 + 128, 128), 128)


def first_kernel(
    p_ref, q_ref, pb_ref, qb_ref, pa_ref, qa_ref, prb_ref, qrb_ref, pra_ref, qra_ref, src_ref,
    low_out, top_out, s_out, first_row, last_row, q_pad, u_pad,
):
    clear_ends(q_pad)
    clear_ends(u_pad)
    row = lax.broadcasted_iota(jnp.int32, (ROWS, LANES), 0)
    lane = lax.broadcasted_iota(jnp.int32, (ROWS, LANES), 1)

    def fill(c, carry):
        for l in range(2):
            q = q_ref[l, :, tile_at(c)]
            q_pad[l, :, pad_at(c)] = q
            u_pad[l, :, pad_at(c)] = q * p_ref[l, :, tile_at(c)]
        return carry

    lax.fori_loop(0, TILES, fill, 0)

    def body(c, carry):
        at = tile_at(c)
        for l in range(2):
            q, u = q_pad[l, :, pad_at(c)], u_pad[l, :, pad_at(c)]
            z_q, z_p = (qb_ref, pb_ref) if l == 0 else (qa_ref, pa_ref)
            zq = z_q[:, at]
            qrb, qra = qrb_ref[l, :, at], qra_ref[l, :, at]
            s = neighbours(q_pad.at[l], q, c, qrb, qra, row, lane)
            s = s + (zq + q_pad[1 - l, :, pad_at(c)])
            t = neighbours(u_pad.at[l], u, c, qrb * prb_ref[l, :, at], qra * pra_ref[l, :, at], row, lane)
            t = t + (zq * z_p[:, at] + u_pad[1 - l, :, pad_at(c)])
            p = p_ref[l, :, at]
            new = p + (conduct * q) * (t - p * s) + src_ref[l * ROWS : (l + 1) * ROWS, at]
            s_out[l, :, at] = s
            out = low_out if l == 0 else top_out
            out[:, at] = new
            first_row[l, :, at] = new[0:1]
            last_row[l, :, at] = new[ROWS - 1 : ROWS]
        return carry

    lax.fori_loop(0, TILES, body, 0)


def second_kernel(
    low_ref, top_ref, q_ref, s_ref, pb_ref, qb_ref, pa_ref, qa_ref, prb_ref, qrb_ref, pra_ref, qra_ref, src_ref,
    fwd_ref, twist_ref, p_out, spec_out, u_pad, mid_ref,
):
    clear_ends(u_pad)
    row = lax.broadcasted_iota(jnp.int32, (ROWS, LANES), 0)
    lane = lax.broadcasted_iota(jnp.int32, (ROWS, LANES), 1)

    def fill(c, carry):
        for l, ref in enumerate((low_ref, top_ref)):
            u_pad[l, :, pad_at(c)] = q_ref[l, :, tile_at(c)] * ref[:, tile_at(c)]
        return carry

    lax.fori_loop(0, TILES, fill, 0)

    def body(c, carry):
        at = tile_at(c)
        for l in range(2):
            u = u_pad[l, :, pad_at(c)]
            z_q, z_p = (qb_ref, pb_ref) if l == 0 else (qa_ref, pa_ref)
            t = neighbours(
                u_pad.at[l], u, c, qrb_ref[l, :, at] * prb_ref[l, :, at], qra_ref[l, :, at] * pra_ref[l, :, at], row, lane
            )
            t = t + (z_q[:, at] * z_p[:, at] + u_pad[1 - l, :, pad_at(c)])
            p = (low_ref if l == 0 else top_ref)[:, at]
            p_out[l, :, at] = (
                p + (conduct * q_ref[l, :, at]) * (t - p * s_ref[l, :, at]) + src_ref[l * ROWS : (l + 1) * ROWS, at]
            )
        return carry

    lax.fori_loop(0, TILES, body, 0)
    spectrum_of_rows(p_out, fwd_ref, twist_ref, spec_out, mid_ref)


def spectrum_of_rows(p_ref, fwd_ref, twist_ref, spec_out, mid_ref):
    def body(i, carry):
        rows = pl.ds(pl.multiple_of(i * 8, 8), 8)
        items = [(p_ref[0, rows, n * 128 : (n + 1) * 128], p_ref[1, rows, n * 128 : (n + 1) * 128]) for n in range(TILES)]
        for k, (re, im) in enumerate(dft16(items, -1)):
            if k:
                cos, sin = twist_ref[0, k : k + 1, :], twist_ref[1, k : k + 1, :]
                re, im = re * cos - im * sin, re * sin + im * cos
            at = pl.ds(pl.multiple_of(k * ROWS + i * 8, 8), 8)
            mid_ref[at, 0:128] = re
            mid_ref[at, 128:256] = im
        return carry

    lax.fori_loop(0, ROWS // 8, body, 0)
    for c in range(4):
        part = triple(mid_ref[c * 256 : (c + 1) * 256, :], 1)
        spec_out[:, c * 256 : (c + 1) * 256] = lax.dot_general(
            fwd_ref[...], part, (((1,), (1,)), ((), ())), preferred_element_type=F32
        )


def middle_kernel(spec_ref, green_ref, mid_ref, mid_inv_ref, inner_ref, inner_inv_ref, twist_ref, out_ref):
    cos, sin = twist_ref[0], twist_ref[1]
    for p in range(0, PAIRS, 2):
        at = slice(p * 128, (p + 2) * 128)
        spread = matmul(mid_ref[...], triple(spec_ref[:, at], 0))
        rows = []
        for h in range(2):
            re, im = spread[0:128, h * 128 : (h + 1) * 128], spread[128:256, h * 128 : (h + 1) * 128]
            rows.append(jnp.concatenate([re * cos - im * sin, re * sin + im * cos], 1))
        freq = matmul(triple(jnp.concatenate(rows, 0), 1), inner_ref[...])
        green = jnp.concatenate([green_ref[p], green_ref[p + 1]], 0)
        freq = freq * jnp.concatenate([green, green], 1)
        back = matmul(triple(freq, 1), inner_inv_ref[...])
        cols = []
        for h in range(2):
            re, im = back[h * 128 : (h + 1) * 128, 0:128], back[h * 128 : (h + 1) * 128, 128:256]
            cols.append(jnp.concatenate([re * cos + im * sin, im * cos - re * sin], 0))
        out_ref[:, at] = matmul(mid_inv_ref[...], triple(jnp.concatenate(cols, 1), 0))


def last_kernel(weight_ref, spec_ref, p_ref, inv_ref, seis_ref, table_ref, twist_ref, state_out, rate_out, mid_ref):
    for c in range(4):
        turned = jnp.transpose(spec_ref[:, c * 256 : (c + 1) * 256])
        mid_ref[c * 256 : (c + 1) * 256, :] = matmul(triple(turned, 1), table_ref[...])

    def body(i, carry):
        rows = pl.ds(pl.multiple_of(i * 8, 8), 8)
        items = []
        for k in range(TILES):
            at = pl.ds(pl.multiple_of(k * ROWS + i * 8, 8), 8)
            re, im = mid_ref[at, 0:128], mid_ref[at, 128:256]
            if k:
                cos, sin = twist_ref[0, k : k + 1, :], twist_ref[1, k : k + 1, :]
                re, im = re * cos + im * sin, im * cos - re * sin
            items.append((re, im))
        for n, stress in enumerate(dft16(items, 1)):
            at = slice(n * 128, (n + 1) * 128)
            total = None
            for l in range(2):
                coulomb = stress[l] + friction * p_ref[l, rows, at]
                grown = seis_ref[l, rows, at] * jnp.exp(-coulomb * inv_ref[l, rows, at])
                state = 1.0 + (grown - 1.0) * recovery
                state_out[l, rows, at] = state
                term = weight_ref[l] / state
                total = term if total is None else total + term
            rate_out[n // 2, rows, (n % 2) * 128 : (n % 2) * 128 + 128] = total
        return carry

    lax.fori_loop(0, ROWS // 8, body, 0)


def sum_kernel(part_ref, out_ref):
    total = part_ref[0]
    for d in range(1, DEPTHS):
        total = total + part_ref[d]
    out_ref[...] = total


def vec(*shape):
    return jax.ShapeDtypeStruct(shape, F32)


def in_vmem(count):
    return [pl.BlockSpec(memory_space=pltpu.VMEM)] * count


def in_smem(count):
    return [pl.BlockSpec(memory_space=pltpu.SMEM)] * count


def call(kernel, outs, smem, args, scratch=()):
    return pl.pallas_call(
        kernel,
        out_shape=outs,
        in_specs=in_smem(smem) + in_vmem(len(args) - smem),
        out_specs=tuple(in_vmem(len(outs))) if isinstance(outs, tuple) else in_vmem(1)[0],
        scratch_shapes=[pltpu.VMEM(s, F32) for s in scratch],
        compiler_params=PARAMS,
    )(*args)


def shift(value, axis, step):
    peers = lax.axis_size(axis)
    pairs = [(i, i + step) for i in range(peers) if 0 <= i + step < peers]
    return lax.ppermute(value, axis, pairs)


def shards(pressure, zone_labels, perm_table, asig_table, well_cells, rate_levels, green_spectrum, seis_state):
    tab = {name: jnp.asarray(value) for name, value in tables().items()}
    z_start = lax.axis_index("depth") * 2
    x_start = lax.axis_index("slab") * ROWS
    block = vec(2, ROWS, N)
    layer = vec(ROWS, N)
    edge = vec(2, 1, N)

    p_below = shift(pressure[1], "depth", 1)
    p_above = shift(pressure[0], "depth", -1)
    p_before = shift(pressure[:, ROWS - 1 :], "slab", 1)
    p_after = shift(pressure[:, :1], "slab", -1)

    root, inv = call(
        lookup_kernel, (block, block), 2, (jnp.sqrt(perm_table), 1.0 / asig_table, zone_labels)
    )
    q_below = shift(root[1], "depth", 1)
    q_above = shift(root[0], "depth", -1)
    q_before = shift(root[:, ROWS - 1 :], "slab", 1)
    q_after = shift(root[:, :1], "slab", -1)

    z_local = well_cells[:, 0] - z_start
    x_local = well_cells[:, 1] - x_start
    inside = (z_local >= 0) & (z_local < 2) & (x_local >= 0) & (x_local < ROWS)
    spot = jnp.where(inside, z_local * ROWS + x_local, -1)[None, :]
    amounts = rate_unit * rate_levels.astype(F32)
    sources = call(wells_kernel, vec(256, N), 0, (spot, amounts, well_cells[:, 2:3]))

    green = (green_spectrum * (1.0 / (N * N))).reshape(ROWS, SLABS, FREQS, PAIRS, 2)
    green = green.transpose(3, 1, 2, 4, 0).reshape(PAIRS, STEP, LANES)

    low, top, s_sum, first, last = call(
        first_kernel,
        (layer, layer, block, edge, edge),
        0,
        (pressure, root, p_below, q_below, p_above, q_above, p_before, q_before, p_after, q_after, sources[:128]),
        ((2, ROWS, N + 256), (2, ROWS, N + 256)),
    )
    p_below = shift(top, "depth", 1)
    p_above = shift(low, "depth", -1)
    p_before = shift(last, "slab", 1)
    p_after = shift(first, "slab", -1)
    press, spec = call(
        second_kernel,
        (block, vec(256, 1024)),
        0,
        (low, top, root, s_sum, p_below, q_below, p_above, q_above, p_before, q_before, p_after, q_after, sources[128:],
         tab["fwd"], tab["row_twist"]),
        ((2, ROWS, N + 256), (1024, 256)),
    )
    spec = lax.all_to_all(spec.reshape(SLABS, 8, 1024), "slab", 0, 0, tiled=True).reshape(256, 1024)
    spec = call(
        middle_kernel,
        vec(256, 1024),
        0,
        (spec, green, tab["mid"], tab["mid_inv"], tab["inner"], tab["inner_inv"], tab["col_twist"]),
    )
    spec = lax.all_to_all(spec.reshape(SLABS, 8, 1024), "slab", 0, 0, tiled=True).reshape(256, 1024)
    layer_pos = (z_start + jnp.arange(2, dtype=jnp.int32)).astype(F32)
    weights = (1.0 + 2.0 * layer_pos / (2 * DEPTHS - 1)) / (4.0 * DEPTHS)
    state, rate = call(
        last_kernel,
        (block, vec(DEPTHS, ROWS, 2 * LANES)),
        1,
        (weights, spec, press, inv, seis_state, tab["inv"], tab["row_twist"]),
        ((1024, 256),),
    )
    rate = lax.all_to_all(rate, "depth", 0, 0, tiled=True)
    rate_map = call(sum_kernel, vec(ROWS, 2 * LANES), 0, (rate,))
    return (press, state, rate_map)


def solution(mesh):
    in_specs = (
        P("depth", "slab", None),
        P("depth", "slab", None),
        P(),
        P(),
        P(),
        P(),
        P(None, "slab"),
        P("depth", "slab", None),
    )
    out_specs = (P("depth", "slab", None), P("depth", "slab", None), P("slab", "depth"))
    return jax.shard_map(shards, mesh=mesh, in_specs=in_specs, out_specs=out_specs, check_vma=False)
```

profile of v0, /device:TPU:2, one launch (start us, length us, event | category | flops | bytes accessed | tf_op | source)
XLA Modules:
  0.0 199.6 jit_solution(4646050197345679214)
XLA Ops:
  0.6 0.7 broadcast_divide_fusion.inv_ref
  1.4 0.7 sqrt.3.root_ref
  2.1 1.2 copy-done.8
  3.3 2.0 shard_map.175
  5.3 0.0 copy-start
  5.3 0.0 copy-start.21
  5.3 1.1 slice_bitcast_fusion
  6.4 4.0 %collective-permute-start.1 = (f32[64,2048]{1,0:T(8,128)}, f32[64,2048]{1,0:T(8,128)S(1)}, u32[]{:S(2)}, u32[]{:S(2)}) collective-permute-start(f32[64,2048]{1,0:T(8,128)} %get-tuple-element.32), channel_id=1, source_target_pairs={{0,1},{1,2},{2,3},{3,4},{4,5},{5,6},{6,7},{8,9},{9,10},{10,11},{11... | collective-permute-start | bytes 1572872 | tf_op jit(solution)/shard_map/ppermute | solution.py:370
  10.4 1.3 collective-permute-start.3
  11.8 1.9 collective-permute-start.5
  13.7 3.6 %collective-permute-start.7 = (f32[2,1,2048]{2,1,0:T(1,128)S(1)}, f32[2,1,2048]{2,1,0:T(1,128)S(1)}, u32[]{:S(2)}, u32[]{:S(2)}) collective-permute-start(f32[2,1,2048]{2,1,0:T(1,128)S(1)} %get-tuple-element.27), channel_id=1, source_target_pairs={{8,0},{16,8},{24,16},{32,24},{40,32},{48,40},{56,48},{64,56},{72,6... | collective-permute-start | bytes 49160 | tf_op jit(solution)/shard_map/ppermute | solution.py:370
  17.4 3.1 %collective-permute-start.4 = (f32[2,1,2048]{2,1,0:T(1,128)S(1)}, f32[2,1,2048]{2,1,0:T(1,128)S(1)}, u32[]{:S(2)}, u32[]{:S(2)}) collective-permute-start(f32[2,1,2048]{2,1,0:T(1,128)S(1)} %get-tuple-element.30), channel_id=1, source_target_pairs={{0,8},{8,16},{16,24},{24,32},{32,40},{40,48},{48,56},{56,64},{64,7... | collective-permute-start | bytes 49160 | tf_op jit(solution)/shard_map/ppermute | solution.py:370
  20.5 1.0 slice_bitcast_fusion.1
  21.6 0.1 copy.23.col_ref
  21.7 0.8 shard_map.176
  22.6 0.5 collective-permute-done.5.qrb_ref
  23.0 14.1 %collective-permute-start = (f32[64,2048]{1,0:T(8,128)S(1)}, f32[64,2048]{1,0:T(8,128)S(1)}, u32[]{:S(2)}, u32[]{:S(2)}) collective-permute-start(f32[64,2048]{1,0:T(8,128)S(1)} %copy-done.20), channel_id=1, source_target_pairs={{0,1},{1,2},{2,3},{3,4},{4,5},{5,6},{6,7},{8,9},{9,10},{10,11},{11... | collective-permute-start | bytes 1572872 | tf_op jit(solution)/shard_map/ppermute | solution.py:370
  37.1 1.3 collective-permute-start.2
  38.4 1.9 collective-permute-start.6
  40.4 1.5 fusion.1
  41.8 2.1 %collective-permute-done.6.pra_ref = f32[2,1,2048]{2,1,0:T(1,128)S(1)} collective-permute-done((f32[2,1,2048]{2,1,0:T(1,128)S(1)}, f32[2,1,2048]{2,1,0:T(1,128)S(1)}, u32[]{:S(2)}, u32[]{:S(2)}) %collective-permute-start.6) | collective-permute-done | bytes 16416 | tf_op jit(solution)/shard_map/ppermute | solution.py:370
  44.0 14.6 %collective-permute-done.2.pa_ref = f32[64,2048]{1,0:T(8,128)S(1)} collective-permute-done((f32[64,2048]{1,0:T(8,128)S(1)}, f32[64,2048]{1,0:T(8,128)S(1)}, u32[]{:S(2)}, u32[]{:S(2)}) %collective-permute-start.2) | collective-permute-done | bytes 524320 | tf_op jit(solution)/shard_map/ppermute | solution.py:370
  58.5 5.5 %shard_map.177 = (f32[64,2048]{1,0:T(8,128)S(1)}, f32[64,2048]{1,0:T(8,128)S(1)}, f32[2,64,2048]{2,1,0:T(8,128)S(1)}, f32[2,1,2048]{2,1,0:T(1,128)S(1)}, f32[2,1,2048]{2,1,0:T(1,128)S(1)}) custom-call(f32[2,64,2048]{2,1,0:T(8,128)S(1)} %copy-done.2, f32[2,64,2048]{2,1,0:T(8,128)} %copy-done, f32[64,2048]{1,0:T(8,128)S(1)} %collective-permute-done.pb_ref, ...), custom_call_target="tpu_custom_call" | custom-call | tf_op jit(solution)/shard_map/pallas_call | solution.py:357
  64.0 1.0 copy-done.7
  65.0 4.0 %collective-permute-start.8 = (f32[64,2048]{1,0:T(8,128)S(1)}, f32[64,2048]{1,0:T(8,128)S(1)}, u32[]{:S(2)}, u32[]{:S(2)}) collective-permute-start(f32[64,2048]{1,0:T(8,128)S(1)} %get-tuple-element.16.top_ref), channel_id=1, source_target_pairs={{0,1},{1,2},{2,3},{3,4},{4,5},{5,6},{6,7},{8,9},{9,10},{10,11},{11... | collective-permute-start | bytes 1572872 | tf_op jit(solution)/shard_map/ppermute | solution.py:370
  69.1 1.3 collective-permute-start.9
  70.4 1.9 collective-permute-start.10
  72.3 3.6 %collective-permute-start.11 = (f32[2,1,2048]{2,1,0:T(1,128)S(1)}, f32[2,1,2048]{2,1,0:T(1,128)S(1)}, u32[]{:S(2)}, u32[]{:S(2)}) collective-permute-start(f32[2,1,2048]{2,1,0:T(1,128)S(1)} %get-tuple-element.19), channel_id=1, source_target_pairs={{8,0},{16,8},{24,16},{32,24},{40,32},{48,40},{56,48},{64,56},{72,6... | collective-permute-start | bytes 49160 | tf_op jit(solution)/shard_map/ppermute | solution.py:370
  76.0 5.6 %collective-permute-done.10.prb_ref = f32[2,1,2048]{2,1,0:T(1,128)S(1)} collective-permute-done((f32[2,1,2048]{2,1,0:T(1,128)S(1)}, f32[2,1,2048]{2,1,0:T(1,128)S(1)}, u32[]{:S(2)}, u32[]{:S(2)}) %collective-permute-start.10) | collective-permute-done | bytes 16416 | tf_op jit(solution)/shard_map/ppermute | solution.py:370
  81.6 6.8 %collective-permute-done.9.pa_ref = f32[64,2048]{1,0:T(8,128)S(1)} collective-permute-done((f32[64,2048]{1,0:T(8,128)S(1)}, f32[64,2048]{1,0:T(8,128)S(1)}, u32[]{:S(2)}, u32[]{:S(2)}) %collective-permute-start.9) | collective-permute-done | bytes 524320 | tf_op jit(solution)/shard_map/ppermute | solution.py:370
  88.4 6.2 %shard_map.178 = (f32[2,64,2048]{2,1,0:T(8,128)}, f32[256,1024]{1,0:T(8,128)}) custom-call(f32[64,2048]{1,0:T(8,128)S(1)} %get-tuple-element.15.low_ref, f32[64,2048]{1,0:T(8,128)S(1)} %get-tuple-element.16.top_ref, f32[2,64,2048]{2,1,0:T(8,128)S(1)} %copy-done.1, f32[2,64,2048]{2,1,0:T(8,128)} %copy-done.7, f32[64,2048]{1,0:T(8,128)S(1)} %collective-permute-done.8.pb_ref, ...), custom_call_target="tpu_custom_call" | custom-call | tf_op jit(solution)/shard_map/pallas_call | solution.py:357
  94.6 12.5 %all-to-all-start = ((f32[32,8,1024]{2,1,0:T(8,128)}), f32[32,8,1024]{2,1,0:T(8,128)S(1)}, u32[]{:S(2)}, u32[]{:S(2)}) async-start(f32[32,8,1024]{2,1,0:T(8,128)} %bitcast.5), calls=%async_computation | async-start | bytes 2097152 | tf_op jit(solution)/shard_map/all_to_all | solution.py:423
  107.1 2.0 %reshape.93 = f32[64,32,4,8,2]{1,0,4,3,2:T(8,128)} reshape(f32[2048,64]{0,1:T(8,128)S(1)} %broadcast_multiply_fusion) | data formatting | bytes 1048576 | tf_op jit(solution)/shard_map/reshape | solution.py:401
  109.1 2.8 %copy.22 = f32[8,32,4,2,64]{4,3,2,1,0:T(2,128)} copy(f32[8,32,4,2,64]{1,4,3,0,2:T(8,128)} %bitcast.19) | data formatting | bytes 1048576 | tf_op jit(solution)/shard_map/transpose | solution.py:402
  112.0 1.8 reshape.94.green_ref
  113.8 22.2 %all-to-all-done = f32[32,8,1024]{2,1,0:T(8,128)S(1)} async-done(((f32[32,8,1024]{2,1,0:T(8,128)}), f32[32,8,1024]{2,1,0:T(8,128)S(1)}, u32[]{:S(2)}, u32[]{:S(2)}) %all-to-all-start) | async-done | bytes 1048608 | tf_op jit(solution)/shard_map/all_to_all | solution.py:423
  136.0 0.0 copy-start.15
  136.0 0.9 copy-done.15
  136.9 4.6 %shard_map.179 = f32[256,1024]{1,0:T(8,128)} custom-call(f32[256,1024]{1,0:T(8,128)S(1)} %bitcast.18, f32[8,128,128]{2,1,0:T(8,128)S(1)} %reshape.94.green_ref, bf16[256,768]{1,0:T(8,128)(2,1)S(1)} %copy-done.10, bf16[256,768]{1,0:T(8,128)(2,1)S(1)} %copy-done.11, bf16[768,256]{1,0:T(8,128)(2,1)S(1)} %copy-done.12, bf16[768,256]{1,0:T(8,128)(2,1)S(1)} %copy-done.13, ...), custom_call_target="tpu_custom_call" | custom-call | tf_op jit(solution)/shard_map/pallas_call | solution.py:357
  141.5 4.1 %all-to-all-start.1 = ((f32[32,8,1024]{2,1,0:T(8,128)}), f32[32,8,1024]{2,1,0:T(8,128)S(1)}, u32[]{:S(2)}, u32[]{:S(2)}) async-start(f32[32,8,1024]{2,1,0:T(8,128)} %bitcast.8), calls=%async_computation.1 | async-start | bytes 2097152 | tf_op jit(solution)/shard_map/all_to_all | solution.py:430
  145.7 0.5 add_multiply_fusion.weight_ref
  146.2 28.5 %all-to-all-done.1 = f32[32,8,1024]{2,1,0:T(8,128)S(1)} async-done(((f32[32,8,1024]{2,1,0:T(8,128)}), f32[32,8,1024]{2,1,0:T(8,128)S(1)}, u32[]{:S(2)}, u32[]{:S(2)}) %all-to-all-start.1) | async-done | bytes 1048608 | tf_op jit(solution)/shard_map/all_to_all | solution.py:430
  174.7 0.0 copy-start.6
  174.7 1.2 copy-done.6
  175.9 0.7 copy-done.17
  176.6 3.1 %shard_map.180 = (f32[2,64,2048]{2,1,0:T(8,128)}, f32[8,64,256]{2,1,0:T(8,128)S(1)}) custom-call(f32[2]{0:T(128)S(1)} %copy-done.17, f32[256,1024]{1,0:T(8,128)S(1)} %bitcast.17, f32[2,64,2048]{2,1,0:T(8,128)S(1)} %copy-done.6, f32[2,64,2048]{2,1,0:T(8,128)S(1)} %copy-done.5, f32[2,64,2048]{2,1,0:T(8,128)S(1)} %copy-done.3, bf16[768,256]{1,0:T(8,128)(2,1)S(1)} %copy-done.9, ...), custom_call_target="tpu_custom_call" | custom-call | tf_op jit(solution)/shard_map/pallas_call | solution.py:357
  179.7 19.2 %all_to_all.15.part_ref = f32[8,64,256]{2,1,0:T(8,128)S(1)} all-to-all(f32[8,64,256]{2,1,0:T(8,128)S(1)} %get-tuple-element.24), channel_id=1, replica_groups=mesh['slab'=32,'depth'=8] {'depth'}, dimensions={0} | all-to-all | bytes 1048576 | tf_op jit(solution)/shard_map/all_to_all | solution.py:440
  198.9 0.7 shard_map.181
  (49 shorter events, 0.2 us)
Async XLA Ops:
  0.6 16.7 %copy-start.2 = (f32[2,64,2048]{2,1,0:T(8,128)S(1)}, f32[2,64,2048]{2,1,0:T(8,128)}, u32[]{:S(2)}) copy-start(f32[2,64,2048]{2,1,0:T(8,128)} %p_ref.1) | copy-start | bytes 3145732
  2.0 1.2 copy-start.8
  5.3 5.2 %copy-start.4 = (f32[2,64,2048]{2,1,0:T(8,128)}, f32[2,64,2048]{2,1,0:T(8,128)S(1)}, u32[]{:S(2)}) copy-start(f32[2,64,2048]{2,1,0:T(8,128)S(1)} %get-tuple-element.22.inv_ref) | copy-start | bytes 3145732
  5.3 16.3 %copy-start = (f32[2,64,2048]{2,1,0:T(8,128)}, f32[2,64,2048]{2,1,0:T(8,128)S(1)}, u32[]{:S(2)}) copy-start(f32[2,64,2048]{2,1,0:T(8,128)S(1)} %get-tuple-element.14.q_ref) | copy-start | bytes 3145732
  5.3 16.3 %copy-start.21 = (s32[512,3]{0,1:T(4,128)S(1)}, s32[512,3]{0,1:T(4,128)}, u32[]{:S(2)}) copy-start(s32[512,3]{0,1:T(4,128)} %param.20) | copy-start | bytes 18436
  5.3 16.3 %copy-start.22 = (s32[2,512]{1,0:T(2,128)S(1)}, s32[2,512]{1,0:T(2,128)}, u32[]{:S(2)}) copy-start(s32[2,512]{1,0:T(2,128)} %param.21) | copy-start | bytes 12292
  6.4 37.6 %collective-permute-start.1 = (f32[64,2048]{1,0:T(8,128)}, f32[64,2048]{1,0:T(8,128)S(1)}, u32[]{:S(2)}, u32[]{:S(2)}) collective-permute-start(f32[64,2048]{1,0:T(8,128)} %get-tuple-element.32), channel_id=1, source_target_pairs={{0,1},{1,2},{2,3},{3,4},{4,5},{5,6},{6,7},{8,9},{9,10},{10,11},{11... | collective-permute-start | bytes 1572872 | tf_op jit(solution)/shard_map/ppermute | solution.py:370
  10.4 33.5 %collective-permute-start.3 = (f32[64,2048]{1,0:T(8,128)}, f32[64,2048]{1,0:T(8,128)S(1)}, u32[]{:S(2)}, u32[]{:S(2)}) collective-permute-start(f32[64,2048]{1,0:T(8,128)} %get-tuple-element.31), channel_id=1, source_target_pairs={{1,0},{2,1},{3,2},{4,3},{5,4},{6,5},{7,6},{9,8},{10,9},{11,10},{12... | collective-permute-start | bytes 1572872 | tf_op jit(solution)/shard_map/ppermute | solution.py:370
  11.8 11.3 %collective-permute-start.5 = (f32[2,1,2048]{2,1,0:T(1,128)S(1)}, f32[2,1,2048]{2,1,0:T(1,128)S(1)}, u32[]{:S(2)}, u32[]{:S(2)}) collective-permute-start(f32[2,1,2048]{2,1,0:T(1,128)S(1)} %get-tuple-element.28), channel_id=1, source_target_pairs={{0,8},{8,16},{16,24},{24,32},{32,40},{40,48},{48,56},{56,64},{64,7... | collective-permute-start | bytes 49160 | tf_op jit(solution)/shard_map/ppermute | solution.py:370
  13.7 23.4 %collective-permute-start.7 = (f32[2,1,2048]{2,1,0:T(1,128)S(1)}, f32[2,1,2048]{2,1,0:T(1,128)S(1)}, u32[]{:S(2)}, u32[]{:S(2)}) collective-permute-start(f32[2,1,2048]{2,1,0:T(1,128)S(1)} %get-tuple-element.27), channel_id=1, source_target_pairs={{8,0},{16,8},{24,16},{32,24},{40,32},{48,40},{56,48},{64,56},{72,6... | collective-permute-start | bytes 49160 | tf_op jit(solution)/shard_map/ppermute | solution.py:370
  17.4 21.0 %collective-permute-start.4 = (f32[2,1,2048]{2,1,0:T(1,128)S(1)}, f32[2,1,2048]{2,1,0:T(1,128)S(1)}, u32[]{:S(2)}, u32[]{:S(2)}) collective-permute-start(f32[2,1,2048]{2,1,0:T(1,128)S(1)} %get-tuple-element.30), channel_id=1, source_target_pairs={{0,8},{8,16},{16,24},{24,32},{32,40},{40,48},{48,56},{56,64},{64,7... | collective-permute-start | bytes 49160 | tf_op jit(solution)/shard_map/ppermute | solution.py:370
  21.5 15.6 %copy-start.19 = (f32[64,2048]{1,0:T(8,128)S(1)}, f32[64,2048]{1,0:T(8,128)}, u32[]{:S(2)}) copy-start(f32[64,2048]{1,0:T(8,128)} %get-tuple-element.33) | copy-start | bytes 1572868
  21.7 1.3 copy-start.20
  23.0 20.9 %collective-permute-start = (f32[64,2048]{1,0:T(8,128)S(1)}, f32[64,2048]{1,0:T(8,128)S(1)}, u32[]{:S(2)}, u32[]{:S(2)}) collective-permute-start(f32[64,2048]{1,0:T(8,128)S(1)} %copy-done.20), channel_id=1, source_target_pairs={{0,1},{1,2},{2,3},{3,4},{4,5},{5,6},{6,7},{8,9},{9,10},{10,11},{11... | collective-permute-start | bytes 1572872 | tf_op jit(solution)/shard_map/ppermute | solution.py:370
  37.1 21.4 %collective-permute-start.2 = (f32[64,2048]{1,0:T(8,128)S(1)}, f32[64,2048]{1,0:T(8,128)S(1)}, u32[]{:S(2)}, u32[]{:S(2)}) collective-permute-start(f32[64,2048]{1,0:T(8,128)S(1)} %copy-done.19), channel_id=1, source_target_pairs={{1,0},{2,1},{3,2},{4,3},{5,4},{6,5},{7,6},{9,8},{10,9},{11,10},{12... | collective-permute-start | bytes 1572872 | tf_op jit(solution)/shard_map/ppermute | solution.py:370
  38.4 5.5 %collective-permute-start.6 = (f32[2,1,2048]{2,1,0:T(1,128)S(1)}, f32[2,1,2048]{2,1,0:T(1,128)S(1)}, u32[]{:S(2)}, u32[]{:S(2)}) collective-permute-start(f32[2,1,2048]{2,1,0:T(1,128)S(1)} %get-tuple-element.29), channel_id=1, source_target_pairs={{8,0},{16,8},{24,16},{32,24},{40,32},{48,40},{56,48},{64,56},{72,6... | collective-permute-start | bytes 49160 | tf_op jit(solution)/shard_map/ppermute | solution.py:370
  58.5 29.8 %copy-start.1 = (f32[2,64,2048]{2,1,0:T(8,128)S(1)}, f32[2,64,2048]{2,1,0:T(8,128)}, u32[]{:S(2)}) copy-start(f32[2,64,2048]{2,1,0:T(8,128)} %copy-done) | copy-start | bytes 3145732
  58.5 29.8 %copy-start.14 = (bf16[256,768]{1,0:T(8,128)(2,1)S(1)}, bf16[256,768]{1,0:T(8,128)(2,1)}, u32[]{:S(2)}) copy-start(bf16[256,768]{1,0:T(8,128)(2,1)} %constant.50.clone.fwd_ref) | copy-start | bytes 1179652
  58.5 29.8 %copy-start.16 = (f32[2,16,128]{2,1,0:T(8,128)S(1)}, f32[2,16,128]{2,1,0:T(8,128)}, u32[]{:S(2)}) copy-start(f32[2,16,128]{2,1,0:T(8,128)} %constant.56.clone.twist_ref) | copy-start | bytes 49156
  64.0 1.0 copy-start.7
  65.0 16.5 %collective-permute-start.8 = (f32[64,2048]{1,0:T(8,128)S(1)}, f32[64,2048]{1,0:T(8,128)S(1)}, u32[]{:S(2)}, u32[]{:S(2)}) collective-permute-start(f32[64,2048]{1,0:T(8,128)S(1)} %get-tuple-element.16.top_ref), channel_id=1, source_target_pairs={{0,1},{1,2},{2,3},{3,4},{4,5},{5,6},{6,7},{8,9},{9,10},{10,11},{11... | collective-permute-start | bytes 1572872 | tf_op jit(solution)/shard_map/ppermute | solution.py:370
  69.1 19.3 %collective-permute-start.9 = (f32[64,2048]{1,0:T(8,128)S(1)}, f32[64,2048]{1,0:T(8,128)S(1)}, u32[]{:S(2)}, u32[]{:S(2)}) collective-permute-start(f32[64,2048]{1,0:T(8,128)S(1)} %get-tuple-element.15.low_ref), channel_id=1, source_target_pairs={{1,0},{2,1},{3,2},{4,3},{5,4},{6,5},{7,6},{9,8},{10,9},{11,10},{12... | collective-permute-start | bytes 1572872 | tf_op jit(solution)/shard_map/ppermute | solution.py:370
  70.4 11.2 %collective-permute-start.10 = (f32[2,1,2048]{2,1,0:T(1,128)S(1)}, f32[2,1,2048]{2,1,0:T(1,128)S(1)}, u32[]{:S(2)}, u32[]{:S(2)}) collective-permute-start(f32[2,1,2048]{2,1,0:T(1,128)S(1)} %get-tuple-element.18), channel_id=1, source_target_pairs={{0,8},{8,16},{16,24},{24,32},{32,40},{40,48},{48,56},{56,64},{64,7... | collective-permute-start | bytes 49160 | tf_op jit(solution)/shard_map/ppermute | solution.py:370
  72.3 9.3 %collective-permute-start.11 = (f32[2,1,2048]{2,1,0:T(1,128)S(1)}, f32[2,1,2048]{2,1,0:T(1,128)S(1)}, u32[]{:S(2)}, u32[]{:S(2)}) collective-permute-start(f32[2,1,2048]{2,1,0:T(1,128)S(1)} %get-tuple-element.19), channel_id=1, source_target_pairs={{8,0},{16,8},{24,16},{32,24},{40,32},{48,40},{56,48},{64,56},{72,6... | collective-permute-start | bytes 49160 | tf_op jit(solution)/shard_map/ppermute | solution.py:370
  94.6 12.5 %copy-start.18 = (f32[2048,64]{0,1:T(8,128)S(1)}, f32[2048,64]{0,1:T(8,128)}, u32[]{:S(2)}) copy-start(f32[2048,64]{0,1:T(8,128)} %param.22) | copy-start | bytes 1572868
  94.6 41.4 %all-to-all-start = ((f32[32,8,1024]{2,1,0:T(8,128)}), f32[32,8,1024]{2,1,0:T(8,128)S(1)}, u32[]{:S(2)}, u32[]{:S(2)}) async-start(f32[32,8,1024]{2,1,0:T(8,128)} %bitcast.5), calls=%async_computation | async-start | bytes 2097152 | tf_op jit(solution)/shard_map/all_to_all | solution.py:423
  109.1 26.9 %copy-start.10 = (bf16[256,768]{1,0:T(8,128)(2,1)S(1)}, bf16[256,768]{1,0:T(8,128)(2,1)}, u32[]{:S(2)}) copy-start(bf16[256,768]{1,0:T(8,128)(2,1)} %constant.52.clone.mid_ref) | copy-start | bytes 1179652
  109.1 26.9 %copy-start.11 = (bf16[256,768]{1,0:T(8,128)(2,1)S(1)}, bf16[256,768]{1,0:T(8,128)(2,1)}, u32[]{:S(2)}) copy-start(bf16[256,768]{1,0:T(8,128)(2,1)} %constant.53.clone.mid_inv_ref) | copy-start | bytes 1179652
  109.1 26.9 %copy-start.12 = (bf16[768,256]{1,0:T(8,128)(2,1)S(1)}, bf16[768,256]{1,0:T(8,128)(2,1)}, u32[]{:S(2)}) copy-start(bf16[768,256]{1,0:T(8,128)(2,1)} %constant.54.clone.inner_ref) | copy-start | bytes 1179652
  109.1 26.9 %copy-start.13 = (bf16[768,256]{1,0:T(8,128)(2,1)S(1)}, bf16[768,256]{1,0:T(8,128)(2,1)}, u32[]{:S(2)}) copy-start(bf16[768,256]{1,0:T(8,128)(2,1)} %constant.55.clone.inner_inv_ref) | copy-start | bytes 1179652
  136.0 0.9 copy-start.15
  136.9 37.8 %copy-start.9 = (bf16[768,256]{1,0:T(8,128)(2,1)S(1)}, bf16[768,256]{1,0:T(8,128)(2,1)}, u32[]{:S(2)}) copy-start(bf16[768,256]{1,0:T(8,128)(2,1)} %constant.51.clone.table_ref) | copy-start | bytes 1179652
  141.5 33.2 %copy-start.3 = (f32[2,64,2048]{2,1,0:T(8,128)S(1)}, f32[2,64,2048]{2,1,0:T(8,128)}, u32[]{:S(2)}) copy-start(f32[2,64,2048]{2,1,0:T(8,128)} %seis_ref.1) | copy-start | bytes 3145732
  141.5 33.2 %copy-start.5 = (f32[2,64,2048]{2,1,0:T(8,128)S(1)}, f32[2,64,2048]{2,1,0:T(8,128)}, u32[]{:S(2)}) copy-start(f32[2,64,2048]{2,1,0:T(8,128)} %copy-done.4) | copy-start | bytes 3145732
  141.5 33.2 %all-to-all-start.1 = ((f32[32,8,1024]{2,1,0:T(8,128)}), f32[32,8,1024]{2,1,0:T(8,128)S(1)}, u32[]{:S(2)}, u32[]{:S(2)}) async-start(f32[32,8,1024]{2,1,0:T(8,128)} %bitcast.8), calls=%async_computation.1 | async-start | bytes 2097152 | tf_op jit(solution)/shard_map/all_to_all | solution.py:430
  174.7 1.2 copy-start.6
  175.9 0.7 copy-start.17
where the time goes:
time: 200 us
  waiting for transfers between devices  80.3 us (40%)
  starting transfers between devices  58.8 us (29%)
  Pallas kernels  22.8 us (11%)
  blocking collectives  19.2 us (10%)
  local copies, waits for them, and re-layouts  16.2 us (8%)
    all_to_all x2, waiting for transfers between devices, shards(): lax.all_to_all(spec.reshape(SLABS, 8, 1024), 'slab', 0, 0, tiled=True)  50.7 us
    ppermute x12, starting transfers between devices, shift(): return lax.ppermute(value, axis, pairs)  42.2 us
    ppermute x12, waiting for transfers between devices, shift(): return lax.ppermute(value, axis, pairs)  29.5 us
    pallas_call x7, Pallas kernels, call(): pl.pallas_call(kernel, out_shape=outs, in_specs=in_smem(smem) + in_vmem(l...  22.8 us
    all_to_all x1, blocking collectives, shards(): rate = lax.all_to_all(rate, 'depth', 0, 0, tiled=True)  19.2 us
    all_to_all x2, starting transfers between devices, shards(): lax.all_to_all(spec.reshape(SLABS, 8, 1024), 'slab', 0, 0, tiled=True)  16.6 us
    unnamed x47, local copies, waits for them, and re-layouts  5.22 us
  transfers between devices with their start and end apart: 14, of which 7 were waited for; matrix products, arithmetic and copies ran while one was open for 5% of the time, Pallas kernels for 0%

commit v1 on v0

v1 whole, which is shorter than its diff:
```python
import functools
import math

import jax
import jax.numpy as jnp
import ml_dtypes
import numpy as np
from jax import lax
from jax.experimental import pallas as pl
from jax.experimental.pallas import tpu as pltpu
from jax.sharding import PartitionSpec as P

conduct = 0.15
rate_unit = 0.5
friction = 0.6
recovery = 0.6065306597126334

LANES = 128
SLABS = 32
DEPTHS = 8
N = 2048
ROWS = N // SLABS
TILES = N // LANES
FREQS = LANES // SLABS
STEP = SLABS * FREQS
F32 = jnp.float32
BF16 = jnp.bfloat16


def blocks(theta):
    cos, sin = np.cos(theta), np.sin(theta)
    return np.stack([np.stack([cos, -sin]), np.stack([sin, cos])])


def halves(table):
    high = table.astype(ml_dtypes.bfloat16)
    low = (table - high.astype(np.float64)).astype(ml_dtypes.bfloat16)
    return high, low


def left_table(table):
    high, low = halves(table)
    return np.concatenate([high, high, low], 1)


def right_table(table):
    high, low = halves(table)
    return np.concatenate([high, high, low], 0)


@functools.lru_cache(maxsize=None)
def tables():
    two_pi = 2.0 * np.pi
    k2, n2 = np.arange(128)[:, None], np.arange(128)[None, :]
    fwd = blocks(-two_pi * ((k2 * n2) % 128) / 128)
    fwd = fwd.reshape(2, 2, SLABS, FREQS, 128).transpose(2, 0, 3, 1, 4).reshape(256, 256)
    inv = blocks(two_pi * ((k2 * n2) % 128) / 128)
    inv = inv.reshape(2, 2, 128, SLABS, FREQS).transpose(3, 1, 4, 0, 2).reshape(256, 256)
    i, k = np.arange(SLABS)[:, None], np.arange(SLABS)[None, :]
    eye = np.eye(FREQS)
    angle = two_pi * ((i * k) % SLABS) / SLABS
    mid = np.einsum("absk,ij->akisbj", blocks(-angle), eye).reshape(256, 256)
    mid_inv = np.einsum("absk,ij->saibkj", blocks(angle), eye).reshape(256, 256)
    r, q = np.arange(8)[:, None], np.arange(8)[None, :]
    many = np.eye(TILES)
    angle = two_pi * ((r * q) % 8) / 8
    inner = np.einsum("abrq,ij->bjraiq", blocks(-angle), many).reshape(256, 256)
    inner_inv = np.einsum("abrq,ij->bjqair", blocks(angle), many).reshape(256, 256)
    row_angle = -two_pi * ((np.arange(TILES)[:, None] * np.arange(128)[None, :]) % N) / N
    row_twist = np.stack([np.cos(row_angle), np.sin(row_angle)]).astype(np.float32)
    row = (8 * np.arange(8)[:, None] + np.arange(8)[None, :])[:, None, :]
    col_angle = -two_pi * ((row * np.arange(SLABS)[None, :, None]) % N) / N
    col_angle = np.tile(np.repeat(col_angle, FREQS, 1), (1, 1, TILES))
    col_twist = np.stack([np.cos(col_angle), np.sin(col_angle)]).astype(np.float32)
    in_angle = np.tile(-two_pi * ((r * q) % 64) / 64, (1, TILES))
    in_twist = np.stack([np.cos(in_angle), np.sin(in_angle)]).astype(np.float32)
    return {
        "fwd": left_table(fwd),
        "inv": right_table(inv),
        "mid": left_table(mid),
        "mid_inv": left_table(mid_inv),
        "inner": right_table(inner),
        "inner_inv": right_table(inner_inv),
        "row_twist": row_twist,
        "col_twist": col_twist,
        "in_twist": in_twist,
    }


def triple(value, axis):
    high = value.astype(BF16)
    low = (value - high.astype(F32)).astype(BF16)
    return jnp.concatenate([high, low, high], axis)


def matmul(left, right):
    return jnp.dot(left, right, preferred_element_type=F32)


def radix4(items, sign):
    (ar, ai), (br, bi), (cr, ci), (dr, di) = items
    pr, pi, mr, mi = ar + cr, ai + ci, ar - cr, ai - ci
    qr, qi, nr, ni = br + dr, bi + di, br - dr, bi - di
    tr, ti = (-ni, nr) if sign > 0 else (ni, -nr)
    return [(pr + qr, pi + qi), (mr + tr, mi + ti), (pr - qr, pi - qi), (mr - tr, mi - ti)]


def scale_by(item, angle):
    c, s = math.cos(angle), math.sin(angle)
    re, im = item
    if abs(s) < 1e-12:
        return (re, im) if c > 0 else (-re, -im)
    if abs(c) < 1e-12:
        return (-im, re) if s > 0 else (im, -re)
    return (re * c - im * s, re * s + im * c)


def dft16(items, sign):
    mids = [radix4([items[4 * b + a] for b in range(4)], sign) for a in range(4)]
    out = [None] * 16
    for k in range(4):
        column = [scale_by(mids[a][k], sign * 2.0 * math.pi * a * k / 16) for a in range(4)]
        for m, item in enumerate(radix4(column, sign)):
            out[k + 4 * m] = item
    return out


def pick(label, table, bit, base):
    if bit < 0:
        return table[base]
    mask = (label & (1 << bit)) != 0
    return jnp.where(mask, pick(label, table, bit - 1, base + (1 << bit)), pick(label, table, bit - 1, base))


def lookup_kernel(root_ref, inv_ref, label_ref, root_out, inv_out):
    width = 512

    def body(i, carry):
        for l in range(2):
            for c in range(N // width):
                rows, cols = pl.ds(pl.multiple_of(i * 8, 8), 8), pl.ds(c * width, width)
                label = label_ref[l, rows, cols]
                root_out[l, rows, cols] = pick(label, root_ref, 3, 0)
                inv_out[l, rows, cols] = pick(label, inv_ref, 3, 0)
        return carry

    lax.fori_loop(0, ROWS // 8, body, 0)


def wells_kernel(where1_ref, where2_ref, amount_ref, col_ref, out1_ref, out2_ref):
    def hits(where_ref, rows, s):
        row = lax.broadcasted_iota(jnp.int32, (rows, 512), 0)
        return jnp.where(row == where_ref[...], amount_ref[s : s + 1, :], 0.0).astype(BF16)

    left = jnp.concatenate([hits(where1_ref, 256, 0), hits(where2_ref, 128, 1)], 0)
    col_of = jnp.broadcast_to(col_ref[...], (512, 256))
    for c in range(N // 256):
        at = slice(c * 256, (c + 1) * 256)
        col = lax.broadcasted_iota(jnp.int32, (512, 256), 1) + c * 256
        both = matmul(left, jnp.where(col == col_of, 1.0, 0.0).astype(BF16))
        out1_ref[:, at] = both[0:256]
        out2_ref[:, at] = both[256:384]


def pack_kernel(p_ref, q_ref, p_before, p_after, q_before, q_after, out_ref):
    width = 1024
    row = lax.broadcasted_iota(jnp.int32, (8, width), 0)
    for c in range(N // width):
        at = slice(c * width, (c + 1) * width)
        for v, (ref, before, after) in enumerate(((p_ref, p_before, p_after), (q_ref, q_before, q_after))):
            for d in range(DEPTHS):
                sides = []
                for l in range(2):
                    out_ref[d, v * 24 + l * 8 : v * 24 + l * 8 + 8, at] = ref[l, d * 8 : d * 8 + 8, at]
                    prev = ref[l, d * 8 - 8 : d * 8, at] if d else before[l, :, at]
                    then = ref[l, d * 8 + 8 : d * 8 + 16, at] if d < DEPTHS - 1 else after[l, :, at]
                    sides.append(jnp.where(row < 4, then, prev))
                both = jnp.where((row < 2) | (row >= 6), sides[0], pltpu.roll(sides[1], 4, 0))
                out_ref[d, v * 24 + 16 : v * 24 + 24, at] = both


def sideways(value, col):
    left = jnp.where(col == 0, 0.0, pltpu.roll(value, 1, 1))
    right = jnp.where(col == N - 1, 0.0, pltpu.roll(value, N - 1, 1))
    return left + right


def around(main, side, row):
    main_up, side_up = pltpu.roll(main, 1, 0), pltpu.roll(side, 1, 0)
    main_down, side_down = pltpu.roll(main, 7, 0), pltpu.roll(side, 7, 0)
    first, last = row == 0, row == 7
    of_main = jnp.where(first, side_up, main_up) + jnp.where(last, side_down, main_down)
    of_side = jnp.where(first, main_up, side_up) + jnp.where(last, main_down, side_down)
    return of_main, of_side


def diffuse_kernel(me_ref, msg_ref, src1_ref, src2_ref, fwd_ref, twist_ref, *rest):
    outs, spec_out, (q_ref, u_ref, w_ref, p_ref, s_ref, mid_ref) = rest[:8], rest[8], rest[9:]
    me = me_ref[0]
    zero = jnp.zeros((16, N), F32)
    for ref in (q_ref, u_ref, w_ref):
        ref[0] = zero
        ref[17] = zero
    row = lax.broadcasted_iota(jnp.int32, (8, N), 0)
    col = lax.broadcasted_iota(jnp.int32, (8, N), 1)

    def fill(d, carry):
        p_side, q_side = msg_ref[d, 16:24, :], msg_ref[d, 40:48, :]
        for l in range(2):
            z = d * 2 + l + 1
            q, p = msg_ref[d, 24 + l * 8 : 32 + l * 8, :], msg_ref[d, l * 8 : l * 8 + 8, :]
            q_ref[z, 0:8, :] = q
            u_ref[z, 0:8, :] = q * p
            q = q_side if l == 0 else pltpu.roll(q_side, 4, 0)
            p = p_side if l == 0 else pltpu.roll(p_side, 4, 0)
            q_ref[z, 8:16, :] = q
            u_ref[z, 8:16, :] = q * p
            p_ref[z - 1, 8:16, :] = p
        return carry

    lax.fori_loop(0, DEPTHS, fill, 0)

    def first(z, carry):
        d, l = z // 2, z % 2
        q, q_side = q_ref[z + 1, 0:8, :], q_ref[z + 1, 8:16, :]
        sums, sides = around(q, q_side, row)
        s = sums + sideways(q, col) + (q_ref[z, 0:8, :] + q_ref[z + 2, 0:8, :])
        s_side = sides + sideways(q_side, col) + (q_ref[z, 8:16, :] + q_ref[z + 2, 8:16, :])
        u, u_side = u_ref[z + 1, 0:8, :], u_ref[z + 1, 8:16, :]
        sums, sides = around(u, u_side, row)
        t = sums + sideways(u, col) + (u_ref[z, 0:8, :] + u_ref[z + 2, 0:8, :])
        t_side = sides + sideways(u_side, col) + (u_ref[z, 8:16, :] + u_ref[z + 2, 8:16, :])
        at = pl.ds(pl.multiple_of(z * 16, 16), 8)
        side_at = pl.ds(pl.multiple_of(z * 16 + 8, 8), 8)
        p = msg_ref[d, pl.ds(pl.multiple_of(l * 8, 8), 8), :]
        new = p + (conduct * q) * (t - p * s) + src1_ref[at, :]
        p_side = p_ref[z, 8:16, :]
        new_side = p_side + (conduct * q_side) * (t_side - p_side * s_side) + src1_ref[side_at, :]
        s_ref[z] = s
        p_ref[z, 0:8, :] = new
        w_ref[z + 1, 0:8, :] = q * new
        w_ref[z + 1, 8:16, :] = q_side * new_side
        return carry

    lax.fori_loop(0, 2 * DEPTHS, first, 0)

    for k in range(DEPTHS):
        d = lax.rem(me + k, DEPTHS)
        for l in range(2):
            z = d * 2 + l
            w = w_ref[z + 1, 0:8, :]
            sums, _ = around(w, w_ref[z + 1, 8:16, :], row)
            t = sums + sideways(w, col) + (w_ref[z, 0:8, :] + w_ref[z + 2, 0:8, :])
            p = p_ref[z, 0:8, :]
            at = pl.ds(pl.multiple_of(z * 8, 8), 8)
            new = p + (conduct * q_ref[z + 1, 0:8, :]) * (t - p * s_ref[z]) + src2_ref[at, :]
            outs[k][l] = new
        spectrum_of_rows(outs[k], twist_ref, mid_ref, d)
    for c in range(4):
        part = triple(mid_ref[c * 256 : (c + 1) * 256, :], 1)
        block = lax.dot_general(fwd_ref[...], part, (((1,), (1,)), ((), ())), preferred_element_type=F32)
        for h in range(2):
            spec_out[:, c * 2 + h] = block[:, h * 128 : (h + 1) * 128].reshape(SLABS, 8, 128)


def spectrum_of_rows(p_ref, twist_ref, mid_ref, d):
    items = [(p_ref[0, :, n * 128 : (n + 1) * 128], p_ref[1, :, n * 128 : (n + 1) * 128]) for n in range(TILES)]
    for k, (re, im) in enumerate(dft16(items, -1)):
        if k:
            cos, sin = twist_ref[0, k : k + 1, :], twist_ref[1, k : k + 1, :]
            re, im = re * cos - im * sin, re * sin + im * cos
        at = pl.ds(pl.multiple_of(d * 128 + k * 8, 8), 8)
        mid_ref[at, 0:128] = re
        mid_ref[at, 128:256] = im


def dft8(items, sign):
    even, odd = radix4(items[0::2], sign), radix4(items[1::2], sign)
    odd = [scale_by(item, sign * 2.0 * math.pi * k / 8) for k, item in enumerate(odd)]
    plus = [(a[0] + b[0], a[1] + b[1]) for a, b in zip(even, odd)]
    minus = [(a[0] - b[0], a[1] - b[1]) for a, b in zip(even, odd)]
    return plus + minus


def turn(item, cos, sin, sign):
    re, im = item
    if sign < 0:
        return re * cos - im * sin, re * sin + im * cos
    return re * cos + im * sin, im * cos - re * sin


def across(ref, sign, col_ref, in_ref):
    def body(i, carry):
        at = pl.ds(pl.multiple_of(i * 8, 8), 8)

        def by_block(items):
            return [turn(item, col_ref[0, d, at, :], col_ref[1, d, at, :], sign) for d, item in enumerate(items)]

        def by_digit(items):
            return [turn(item, in_ref[0, d : d + 1, :], in_ref[1, d : d + 1, :], sign) for d, item in enumerate(items)]

        items = [(ref[0, d, at, :], ref[1, d, at, :]) for d in range(DEPTHS)]
        items = by_block(items) if sign < 0 else by_digit(items)
        items = dft8(items, sign)
        items = by_digit(items) if sign < 0 else by_block(items)
        for d, (re, im) in enumerate(items):
            ref[0, d, at, :] = re
            ref[1, d, at, :] = im
        return carry

    lax.fori_loop(0, STEP // 8, body, 0)


def middle_kernel(
    spec_ref, green_ref, mid_ref, mid_inv_ref, inner_ref, inner_inv_ref, col_ref, in_ref, out_ref, work
):
    for d in range(0, DEPTHS, 2):
        part = jnp.concatenate([spec_ref[:, d + h].reshape(256, 128) for h in range(2)], 1)
        spread = matmul(mid_ref[...], triple(part, 0))
        for h in range(2):
            work[0, d + h] = spread[0:128, h * 128 : (h + 1) * 128]
            work[1, d + h] = spread[128:256, h * 128 : (h + 1) * 128]
    across(work, -1, col_ref, in_ref)
    for k in range(0, DEPTHS, 2):
        part = [jnp.concatenate([work[0, k + h], work[1, k + h]], 1) for h in range(2)]
        freq = matmul(triple(jnp.concatenate(part, 0), 1), inner_ref[...])
        green = jnp.concatenate([green_ref[k], green_ref[k + 1]], 0)
        freq = freq * jnp.concatenate([green, green], 1)
        back = matmul(triple(freq, 1), inner_inv_ref[...])
        for h in range(2):
            work[0, k + h] = back[h * 128 : (h + 1) * 128, 0:128]
            work[1, k + h] = back[h * 128 : (h + 1) * 128, 128:256]
    across(work, 1, col_ref, in_ref)
    for d in range(0, DEPTHS, 2):
        part = [jnp.concatenate([work[0, d + h], work[1, d + h]], 0) for h in range(2)]
        out_ref[:, d * 128 : (d + 2) * 128] = matmul(mid_inv_ref[...], triple(jnp.concatenate(part, 1), 0))


def last_kernel(me_ref, weight_ref, spec_ref, inv_ref, seis_ref, table_ref, twist_ref, *rest):
    parts, (p_out, state_out, rate_out, mid_ref) = rest[:DEPTHS], rest[DEPTHS:]
    me = me_ref[0]
    for c in range(4):
        turned = jnp.transpose(spec_ref[:, c * 256 : (c + 1) * 256])
        mid_ref[c * 256 : (c + 1) * 256, :] = matmul(triple(turned, 1), table_ref[...])
    for k in range(DEPTHS):
        d = lax.rem(me + (DEPTHS - k), DEPTHS)
        p_out[:, pl.ds(pl.multiple_of(d * 8, 8), 8), :] = parts[k][...]

    def body(i, carry):
        rows = pl.ds(pl.multiple_of(i * 8, 8), 8)
        items = []
        for k in range(TILES):
            at = pl.ds(pl.multiple_of(i * 128 + k * 8, 8), 8)
            re, im = mid_ref[at, 0:128], mid_ref[at, 128:256]
            if k:
                cos, sin = twist_ref[0, k : k + 1, :], twist_ref[1, k : k + 1, :]
                re, im = re * cos + im * sin, im * cos - re * sin
            items.append((re, im))
        for n, stress in enumerate(dft16(items, 1)):
            at = slice(n * 128, (n + 1) * 128)
            total = None
            for l in range(2):
                coulomb = stress[l] + friction * p_out[l, rows, at]
                grown = seis_ref[l, rows, at] * jnp.exp(-coulomb * inv_ref[l, rows, at])
                state = 1.0 + (grown - 1.0) * recovery
                state_out[l, rows, at] = state
                term = weight_ref[l] / state
                total = term if total is None else total + term
            rate_out[n // 2, rows, (n % 2) * 128 : (n % 2) * 128 + 128] = total
        return carry

    lax.fori_loop(0, ROWS // 8, body, 0)


def sum_kernel(part_ref, out_ref):
    total = part_ref[0]
    for d in range(1, DEPTHS):
        total = total + part_ref[d]
    out_ref[...] = total


def vec(*shape):
    return jax.ShapeDtypeStruct(shape, F32)


def in_vmem(count):
    return [pl.BlockSpec(memory_space=pltpu.VMEM)] * count


def in_smem(count):
    return [pl.BlockSpec(memory_space=pltpu.SMEM)] * count


def call(kernel, mib, outs, smem, args, scratch=()):
    return pl.pallas_call(
        kernel,
        out_shape=outs,
        in_specs=in_smem(smem) + in_vmem(len(args) - smem),
        out_specs=tuple(in_vmem(len(outs))) if isinstance(outs, tuple) else in_vmem(1)[0],
        scratch_shapes=[pltpu.VMEM(s, F32) for s in scratch],
        compiler_params=pltpu.CompilerParams(vmem_limit_bytes=mib * 1024 * 1024),
    )(*args)


def shift(value, axis, step):
    peers = lax.axis_size(axis)
    pairs = [(i, i + step) for i in range(peers) if 0 <= i + step < peers]
    return lax.ppermute(value, axis, pairs)


def shards(pressure, zone_labels, perm_table, asig_table, well_cells, rate_levels, green_spectrum, seis_state):
    tab = {name: jnp.asarray(value) for name, value in tables().items()}
    depth, slab = lax.axis_index("depth"), lax.axis_index("slab")
    me = depth.reshape(1)
    block = vec(2, ROWS, N)

    p_before = shift(pressure[:, ROWS - 8 :], "slab", 1)
    p_after = shift(pressure[:, :8], "slab", -1)
    root, inv = call(
        lookup_kernel, 12, (block, block), 2, (jnp.sqrt(perm_table), 1.0 / asig_table, zone_labels)
    )
    q_before = shift(root[:, ROWS - 8 :], "slab", 1)
    q_after = shift(root[:, :8], "slab", -1)

    offset = well_cells[:, 1] - (slab * ROWS + depth * 8)
    near = (offset >= -2) & (offset < 10)
    spot1 = jnp.where(near, well_cells[:, 0] * 16 + (offset & 15), -1)[None, :]
    own = (offset >= 0) & (offset < 8)
    spot2 = jnp.where(own, well_cells[:, 0] * 8 + offset, -1)[None, :]
    amounts = rate_unit * rate_levels.astype(F32)
    src1, src2 = call(wells_kernel, 12, (vec(256, N), vec(128, N)), 0, (spot1, spot2, amounts, well_cells[:, 2:3]))

    green = (green_spectrum * (1.0 / (N * N))).reshape(8, 8, SLABS, FREQS, TILES)
    green = green.transpose(1, 2, 3, 4, 0).reshape(8, STEP, LANES)

    msg = call(pack_kernel, 14, vec(DEPTHS, 48, N), 0, (pressure, root, p_before, p_after, q_before, q_after))
    msg = lax.all_to_all(msg, "depth", 0, 0, tiled=True)
    *parts, spec = call(
        diffuse_kernel,
        30,
        (vec(2, 8, N),) * DEPTHS + (vec(SLABS, DEPTHS, 8, LANES),),
        1,
        (me, msg, src1, src2, tab["fwd"], tab["row_twist"]),
        ((18, 16, N), (18, 16, N), (18, 16, N), (16, 16, N), (16, 8, N), (1024, 256)),
    )
    spec = lax.all_to_all(spec.reshape(SLABS * DEPTHS, 8, LANES), ("slab", "depth"), 0, 0, tiled=True)
    for k in range(1, DEPTHS):
        parts[k] = lax.ppermute(parts[k], "depth", [(i, (i + k) % DEPTHS) for i in range(DEPTHS)])
    spec = call(
        middle_kernel,
        24,
        vec(256, 1024),
        0,
        (spec.reshape(SLABS, DEPTHS, 8, LANES), green, tab["mid"], tab["mid_inv"], tab["inner"], tab["inner_inv"],
         tab["col_twist"], tab["in_twist"]),
        ((2, DEPTHS, STEP, LANES),),
    )
    spec = lax.all_to_all(spec.reshape(SLABS, 8, 1024), "slab", 0, 0, tiled=True).reshape(256, 1024)
    layer_pos = (depth * 2 + jnp.arange(2, dtype=jnp.int32)).astype(F32)
    weights = (1.0 + 2.0 * layer_pos / (2 * DEPTHS - 1)) / (4.0 * DEPTHS)
    press, state, rate = call(
        last_kernel,
        18,
        (block, block, vec(DEPTHS, ROWS, 2 * LANES)),
        2,
        (me, weights, spec, inv, seis_state, tab["inv"], tab["row_twist"], *parts),
        ((1024, 256),),
    )
    rate = lax.all_to_all(rate, "depth", 0, 0, tiled=True)
    rate_map = call(sum_kernel, 4, vec(ROWS, 2 * LANES), 0, (rate,))
    return (press, state, rate_map)


def solution(mesh):
    in_specs = (
        P("depth", "slab", None),
        P("depth", "slab", None),
        P(),
        P(),
        P(),
        P(),
        P(None, "slab"),
        P("depth", "slab", None),
    )
    out_specs = (P("depth", "slab", None), P("depth", "slab", None), P("slab", "depth"))
    return jax.shard_map(shards, mesh=mesh, in_specs=in_specs, out_specs=out_specs, check_vma=False)
```

time: 200 us -> 195 us (0.975)
  local copies, waits for them, and re-layouts: 16.2 us -> 39.2 us
  waiting for transfers between devices: 80.3 us -> 64.1 us
  Pallas kernels: 22.8 us -> 17.7 us
  starting transfers between devices: 58.8 us -> 53.7 us
  blocking collectives: 19.2 us -> 15.7 us
    all_to_all x0 -> x2, waiting for transfers between devices: none -> 48.3 us  [the longest x1 34.5 us: shards(): msg = lax.all_to_all(msg, 'depth', 0, 0, tiled=True)]
    all_to_all x2 -> x1, waiting for transfers between devices: 50.7 us -> 3.21 us  [shards(): lax.all_to_all(spec.reshape(SLABS, 8, 1024), 'slab', 0, 0, tiled=True)]
    ppermute x12 -> x4, starting transfers between devices: 42.2 us -> 11.1 us  [shift(): return lax.ppermute(value, axis, pairs)]
    ppermute x12 -> x4, waiting for transfers between devices: 29.5 us -> 2.48 us  [shift(): return lax.ppermute(value, axis, pairs)]
    all_to_all x0 -> x2, starting transfers between devices: none -> 22.2 us  [the longest x1 16 us: shards(): lax.all_to_all(spec.reshape(SLABS * DEPTHS, 8, LANES), ('slab', 'depth'),...]
    unnamed x47 -> x61, local copies, waits for them, and re-layouts: 5.22 us -> 22.6 us
    ppermute x0 -> x7, starting transfers between devices: none -> 15.2 us  [shards(): lax.ppermute(parts[k], 'depth', [(i, (i + k) % DEPTHS) for i in range(DEP...]
    all_to_all x2 -> x1, starting transfers between devices: 16.6 us -> 5.25 us  [shards(): lax.all_to_all(spec.reshape(SLABS, 8, 1024), 'slab', 0, 0, tiled=True)]
  transfers between devices with their start and end apart: 14 -> 14, of which waited for: 7 -> 8; matrix products, arithmetic and copies ran while one was open for 5% -> 9% of each run, Pallas kernels for 0% -> 1%
where the time goes in v1:
time: 195 us; the launch traced here: 194 us
  waiting for transfers between devices  64.1 us (33%)
  starting transfers between devices  53.7 us (28%)
  local copies, waits for them, and re-layouts  39.2 us (20%)
  Pallas kernels  17.7 us (9%)
  blocking collectives  15.7 us (8%)
  other arithmetic  2.27 us (1%)
    all_to_all x1, waiting for transfers between devices, shards(): msg = lax.all_to_all(msg, 'depth', 0, 0, tiled=True)  34.5 us
    unnamed x61, local copies, waits for them, and re-layouts  22.6 us
    pallas_call x7, Pallas kernels, call(): pl.pallas_call(kernel, out_shape=outs, in_specs=in_smem(smem) + in_vmem(l...  17.7 us
    all_to_all x1, starting transfers between devices, shards(): lax.all_to_all(spec.reshape(SLABS * DEPTHS, 8, LANES), ('slab', 'depth'),...  16 us
    all_to_all x1, blocking collectives, shards(): rate = lax.all_to_all(rate, 'depth', 0, 0, tiled=True)  15.7 us
    ppermute x7, starting transfers between devices, shards(): lax.ppermute(parts[k], 'depth', [(i, (i + k) % DEPTHS) for i in range(DEP...  15.2 us
    all_to_all x1, waiting for transfers between devices, shards(): lax.all_to_all(spec.reshape(SLABS * DEPTHS, 8, LANES), ('slab', 'depth'),...  13.9 us
    ppermute x4, starting transfers between devices, shift(): return lax.ppermute(value, axis, pairs)  11.1 us
  transfers between devices with their start and end apart: 14, of which 8 were waited for; matrix products, arithmetic and copies ran while one was open for 9% of the time, Pallas kernels for 1%

profile of v1, /device:TPU:2, one launch (start us, length us, event | category | flops | bytes accessed | tf_op | source)
XLA Modules:
  0.0 193.6 jit_solution(6866672556615131122)
XLA Ops:
  2.0 1.2 copy-done.8
  3.2 2.0 %shard_map.184 = (f32[2,64,2048]{2,1,0:T(8,128)S(1)}, f32[2,64,2048]{2,1,0:T(8,128)S(1)}) custom-call(f32[16]{0:T(128)S(1)} %sqrt.3.root_ref, f32[16]{0:T(128)S(1)} %broadcast_divide_fusion.inv_ref, s32[2,64,2048]{2,1,0:T(8,128)S(1)} %copy-done.8), custom_call_target="tpu_custom_call" | custom-call | tf_op jit(solution)/shard_map/pallas_call | solution.py:395
  5.2 1.9 collective-permute-start.2
  7.1 3.6 %collective-permute-start.3 = (f32[2,8,2048]{2,1,0:T(8,128)S(1)}, f32[2,8,2048]{2,1,0:T(8,128)S(1)}, u32[]{:S(2)}, u32[]{:S(2)}) collective-permute-start(f32[2,8,2048]{2,1,0:T(8,128)S(1)} %get-tuple-element.35), channel_id=1, source_target_pairs={{8,0},{16,8},{24,16},{32,24},{40,32},{48,40},{56,48},{64,56},{72,6... | collective-permute-start | bytes 393224 | tf_op jit(solution)/shard_map/ppermute | solution.py:408
  10.8 1.0 fusion.3
  11.8 2.2 %collective-permute-start = (f32[2,8,2048]{2,1,0:T(8,128)S(1)}, f32[2,8,2048]{2,1,0:T(8,128)S(1)}, u32[]{:S(2)}, u32[]{:S(2)}) collective-permute-start(f32[2,8,2048]{2,1,0:T(8,128)S(1)} %get-tuple-element.38), channel_id=1, source_target_pairs={{0,8},{8,16},{16,24},{24,32},{32,40},{40,48},{48,56},{56,64},{64,7... | collective-permute-start | bytes 393224 | tf_op jit(solution)/shard_map/ppermute | solution.py:408
  14.0 3.4 %collective-permute-start.1 = (f32[2,8,2048]{2,1,0:T(8,128)S(1)}, f32[2,8,2048]{2,1,0:T(8,128)S(1)}, u32[]{:S(2)}, u32[]{:S(2)}) collective-permute-start(f32[2,8,2048]{2,1,0:T(8,128)S(1)} %get-tuple-element.37), channel_id=1, source_target_pairs={{8,0},{16,8},{24,16},{32,24},{40,32},{48,40},{56,48},{64,56},{72,6... | collective-permute-start | bytes 393224 | tf_op jit(solution)/shard_map/ppermute | solution.py:408
  17.4 0.7 collective-permute-done.p_before
  18.1 1.8 collective-permute-done.1.p_after
  19.8 1.2 copy-done.3
  21.4 1.6 copy-done
  23.0 6.2 %all-to-all-start = ((f32[8,48,2048]{2,1,0:T(8,128)}), f32[8,48,2048]{2,1,0:T(8,128)S(1)}, u32[]{:S(2)}, u32[]{:S(2)}) async-start(f32[8,48,2048]{2,1,0:T(8,128)} %copy-done), calls=%async_computation | async-start | bytes 6291456 | tf_op jit(solution)/shard_map/all_to_all | solution.py:437
  29.4 1.1 shard_map.186
  30.5 1.3 copy-done.1
  31.8 1.0 copy-done.10
  32.8 34.5 %all-to-all-done.msg_ref = f32[8,48,2048]{2,1,0:T(8,128)S(1)} async-done(((f32[8,48,2048]{2,1,0:T(8,128)}), f32[8,48,2048]{2,1,0:T(8,128)S(1)}, u32[]{:S(2)}, u32[]{:S(2)}) %all-to-all-start) | async-done | bytes 3145760 | tf_op jit(solution)/shard_map/all_to_all | solution.py:437
  67.3 1.6 copy-done.2
  68.9 1.2 copy-done.11
  70.1 1.0 copy-done.17
  71.1 5.9 %shard_map.187 = (f32[2,8,2048]{2,1,0:T(8,128)S(1)}, f32[2,8,2048]{2,1,0:T(8,128)S(1)}, f32[2,8,2048]{2,1,0:T(8,128)S(1)}, f32[2,8,2048]{2,1,0:T(8,128)S(1)}, f3...) custom-call(s32[1]{0:T(128)} %bitcast.me_ref, ...), custom_call_target="tpu_custom_call" | custom-call | tf_op jit(solution)/shard_map/pallas_call | solution.py:395
  77.0 1.0 copy-done.9
  82.5 16.0 %all-to-all-start.1 = ((f32[256,8,128]{2,1,0:T(8,128)}), f32[256,8,128]{2,1,0:T(8,128)S(1)}, u32[]{:S(2)}, u32[]{:S(2)}) async-start(f32[256,8,128]{2,1,0:T(8,128)} %bitcast.16), calls=%async_computation.1 | async-start | bytes 2097152 | tf_op jit(solution)/shard_map/all_to_all | solution.py:446
  98.5 1.1 broadcast_multiply_fusion
  99.6 2.0 %reshape.121 = f32[8,8,32,4,16]{2,1,0,4,3:T(8,128)} reshape(f32[2048,64]{0,1:T(8,128)S(1)} %broadcast_multiply_fusion) | data formatting | bytes 1048576 | tf_op jit(solution)/shard_map/reshape | solution.py:433
  101.6 6.6 %copy.23 = f32[8,8,32,4,16]{0,4,3,2,1:T(8,128)} copy(f32[8,8,32,4,16]{2,1,0,4,3:T(8,128)} %reshape.121) | data formatting | bytes 1048576 | tf_op jit(solution)/shard_map/reshape | solution.py:433
  108.2 6.4 %reshape.122.green_ref = f32[8,128,128]{2,1,0:T(8,128)S(1)} reshape(f32[8,32,4,16,8]{4,3,2,1,0:T(8,128)} %bitcast.17) | data formatting | bytes 1048576 | tf_op jit(solution)/shard_map/reshape | solution.py:434
  114.6 13.9 %all-to-all-done.1 = f32[256,8,128]{2,1,0:T(8,128)S(1)} async-done(((f32[256,8,128]{2,1,0:T(8,128)}), f32[256,8,128]{2,1,0:T(8,128)S(1)}, u32[]{:S(2)}, u32[]{:S(2)}) %all-to-all-start.1) | async-done | bytes 1048608 | tf_op jit(solution)/shard_map/all_to_all | solution.py:446
  128.5 1.2 copy-done.7
  129.8 1.0 copy-done.14
  130.8 1.0 copy-done.15
  131.8 1.0 copy-done.16
  132.7 0.7 copy-done.19
  133.4 4.4 %shard_map.188 = f32[256,1024]{1,0:T(8,128)} custom-call(f32[32,8,8,128]{3,2,1,0:T(8,128)S(1)} %bitcast.15, f32[8,128,128]{2,1,0:T(8,128)S(1)} %reshape.122.green_ref, bf16[256,768]{1,0:T(8,128)(2,1)S(1)} %copy-done.13, bf16[256,768]{1,0:T(8,128)(2,1)S(1)} %copy-done.14, bf16[768,256]{1,0:T(8,128)(2,1)S(1)} %copy-done.15, bf16[768,256]{1,0:T(8,128)(2,1)S(1)} %copy-done.16, ...), custom_call_target="tpu_custom_call" | custom-call | tf_op jit(solution)/shard_map/pallas_call | solution.py:395
  137.8 5.3 %all-to-all-start.2 = ((f32[32,8,1024]{2,1,0:T(8,128)}), f32[32,8,1024]{2,1,0:T(8,128)S(1)}, u32[]{:S(2)}, u32[]{:S(2)}) async-start(f32[32,8,1024]{2,1,0:T(8,128)} %bitcast.6), calls=%async_computation.2 | async-start | bytes 2097152 | tf_op jit(solution)/shard_map/all_to_all | solution.py:458
  143.1 2.9 %collective-permute-start.10 = (f32[2,8,2048]{2,1,0:T(8,128)}, f32[2,8,2048]{2,1,0:T(8,128)S(1)}, u32[]{:S(2)}, u32[]{:S(2)}) collective-permute-start(f32[2,8,2048]{2,1,0:T(8,128)} %copy-done.27), channel_id=1, source_target_pairs={{0,7},{1,0},{2,1},{3,2},{4,3},{5,4},{6,5},{7,6},{8,15},{9,8},{10,9... | collective-permute-start | bytes 393224 | tf_op jit(solution)/shard_map/ppermute | solution.py:448
  146.0 0.7 collective-permute-start.4
  146.7 0.8 collective-permute-start.5
  147.5 2.8 %collective-permute-start.6 = (f32[2,8,2048]{2,1,0:T(8,128)}, f32[2,8,2048]{2,1,0:T(8,128)S(1)}, u32[]{:S(2)}, u32[]{:S(2)}) collective-permute-start(f32[2,8,2048]{2,1,0:T(8,128)} %copy-done.24), channel_id=1, source_target_pairs={{0,3},{1,4},{2,5},{3,6},{4,7},{5,0},{6,1},{7,2},{8,11},{9,12},{10,... | collective-permute-start | bytes 393224 | tf_op jit(solution)/shard_map/ppermute | solution.py:448
  150.3 3.0 %collective-permute-start.7 = (f32[2,8,2048]{2,1,0:T(8,128)}, f32[2,8,2048]{2,1,0:T(8,128)S(1)}, u32[]{:S(2)}, u32[]{:S(2)}) collective-permute-start(f32[2,8,2048]{2,1,0:T(8,128)} %copy-done.23), channel_id=1, source_target_pairs={{0,4},{1,5},{2,6},{3,7},{4,0},{5,1},{6,2},{7,3},{8,12},{9,13},{10,... | collective-permute-start | bytes 393224 | tf_op jit(solution)/shard_map/ppermute | solution.py:448
  153.3 2.3 %collective-permute-done.10.rest_7_ = f32[2,8,2048]{2,1,0:T(8,128)S(1)} collective-permute-done((f32[2,8,2048]{2,1,0:T(8,128)}, f32[2,8,2048]{2,1,0:T(8,128)S(1)}, u32[]{:S(2)}, u32[]{:S(2)}) %collective-permute-start.10) | collective-permute-done | bytes 131104 | tf_op jit(solution)/shard_map/ppermute | solution.py:448
  155.6 3.7 %collective-permute-start.8 = (f32[2,8,2048]{2,1,0:T(8,128)}, f32[2,8,2048]{2,1,0:T(8,128)S(1)}, u32[]{:S(2)}, u32[]{:S(2)}) collective-permute-start(f32[2,8,2048]{2,1,0:T(8,128)} %copy-done.22), channel_id=1, source_target_pairs={{0,5},{1,6},{2,7},{3,0},{4,1},{5,2},{6,3},{7,4},{8,13},{9,14},{10,... | collective-permute-start | bytes 393224 | tf_op jit(solution)/shard_map/ppermute | solution.py:448
  159.3 1.4 collective-permute-start.9
  161.1 5.6 %collective-permute-done.6.rest_3_ = f32[2,8,2048]{2,1,0:T(8,128)S(1)} collective-permute-done((f32[2,8,2048]{2,1,0:T(8,128)}, f32[2,8,2048]{2,1,0:T(8,128)S(1)}, u32[]{:S(2)}, u32[]{:S(2)}) %collective-permute-start.6) | collective-permute-done | bytes 131104 | tf_op jit(solution)/shard_map/ppermute | solution.py:448
  166.7 2.2 %collective-permute-done.8.rest_5_ = f32[2,8,2048]{2,1,0:T(8,128)S(1)} collective-permute-done((f32[2,8,2048]{2,1,0:T(8,128)}, f32[2,8,2048]{2,1,0:T(8,128)S(1)}, u32[]{:S(2)}, u32[]{:S(2)}) %collective-permute-start.8) | collective-permute-done | bytes 131104 | tf_op jit(solution)/shard_map/ppermute | solution.py:448
  168.9 3.2 %all-to-all-done.2 = f32[32,8,1024]{2,1,0:T(8,128)S(1)} async-done(((f32[32,8,1024]{2,1,0:T(8,128)}), f32[32,8,1024]{2,1,0:T(8,128)S(1)}, u32[]{:S(2)}, u32[]{:S(2)}) %all-to-all-start.2) | async-done | bytes 1048608 | tf_op jit(solution)/shard_map/all_to_all | solution.py:458
  172.1 1.2 copy-done.6
  174.0 3.4 %shard_map.189 = (f32[2,64,2048]{2,1,0:T(8,128)}, f32[2,64,2048]{2,1,0:T(8,128)}, f32[8,64,256]{2,1,0:T(8,128)S(1)}) custom-call(s32[1]{0:T(128)} %bitcast.me_ref, f32[2]{0:T(128)S(1)} %copy-done.20, f32[256,1024]{1,0:T(8,128)S(1)} %bitcast.14, f32[2,64,2048]{2,1,0:T(8,128)S(1)} %copy-done.6, f32[2,64,2048]{2,1,0:T(8,128)S(1)} %copy-done.4, ...), custom_call_target="tpu_custom_call" | custom-call | tf_op jit(solution)/shard_map/pallas_call | solution.py:395
  177.3 15.7 %all_to_all.20.part_ref = f32[8,64,256]{2,1,0:T(8,128)S(1)} all-to-all(f32[8,64,256]{2,1,0:T(8,128)S(1)} %get-tuple-element.34), channel_id=1, replica_groups=mesh['slab'=32,'depth'=8] {'depth'}, dimensions={0} | all-to-all | bytes 1048576 | tf_op jit(solution)/shard_map/all_to_all | solution.py:469
  (60 shorter events, 8.1 us)
Async XLA Ops:
  2.0 1.2 copy-start.8
  5.2 12.9 %copy-start.5 = (f32[2,64,2048]{2,1,0:T(8,128)}, f32[2,64,2048]{2,1,0:T(8,128)S(1)}, u32[]{:S(2)}) copy-start(f32[2,64,2048]{2,1,0:T(8,128)S(1)} %get-tuple-element.23.inv_ref) | copy-start | bytes 3145732
  5.2 12.2 %collective-permute-start.2 = (f32[2,8,2048]{2,1,0:T(8,128)S(1)}, f32[2,8,2048]{2,1,0:T(8,128)S(1)}, u32[]{:S(2)}, u32[]{:S(2)}) collective-permute-start(f32[2,8,2048]{2,1,0:T(8,128)S(1)} %get-tuple-element.36), channel_id=1, source_target_pairs={{0,8},{8,16},{16,24},{24,32},{32,40},{40,48},{48,56},{56,64},{64,7... | collective-permute-start | bytes 393224 | tf_op jit(solution)/shard_map/ppermute | solution.py:408
  7.1 10.2 %collective-permute-start.3 = (f32[2,8,2048]{2,1,0:T(8,128)S(1)}, f32[2,8,2048]{2,1,0:T(8,128)S(1)}, u32[]{:S(2)}, u32[]{:S(2)}) collective-permute-start(f32[2,8,2048]{2,1,0:T(8,128)S(1)} %get-tuple-element.35), channel_id=1, source_target_pairs={{8,0},{16,8},{24,16},{32,24},{40,32},{48,40},{56,48},{64,56},{72,6... | collective-permute-start | bytes 393224 | tf_op jit(solution)/shard_map/ppermute | solution.py:408
  11.8 6.3 %collective-permute-start = (f32[2,8,2048]{2,1,0:T(8,128)S(1)}, f32[2,8,2048]{2,1,0:T(8,128)S(1)}, u32[]{:S(2)}, u32[]{:S(2)}) collective-permute-start(f32[2,8,2048]{2,1,0:T(8,128)S(1)} %get-tuple-element.38), channel_id=1, source_target_pairs={{0,8},{8,16},{16,24},{24,32},{32,40},{40,48},{48,56},{56,64},{64,7... | collective-permute-start | bytes 393224 | tf_op jit(solution)/shard_map/ppermute | solution.py:408
  14.0 5.9 %collective-permute-start.1 = (f32[2,8,2048]{2,1,0:T(8,128)S(1)}, f32[2,8,2048]{2,1,0:T(8,128)S(1)}, u32[]{:S(2)}, u32[]{:S(2)}) collective-permute-start(f32[2,8,2048]{2,1,0:T(8,128)S(1)} %get-tuple-element.37), channel_id=1, source_target_pairs={{8,0},{16,8},{24,16},{32,24},{40,32},{48,40},{56,48},{64,56},{72,6... | collective-permute-start | bytes 393224 | tf_op jit(solution)/shard_map/ppermute | solution.py:408
  19.8 1.2 copy-start.3
  21.4 1.6 copy-start
  23.0 6.2 %copy-start.28 = (s32[512,3]{0,1:T(4,128)S(1)}, s32[512,3]{0,1:T(4,128)}, u32[]{:S(2)}) copy-start(s32[512,3]{0,1:T(4,128)} %param.21) | copy-start | bytes 18436
  23.0 6.4 %copy-start.29 = (s32[2,512]{1,0:T(2,128)S(1)}, s32[2,512]{1,0:T(2,128)}, u32[]{:S(2)}) copy-start(s32[2,512]{1,0:T(2,128)} %param.22) | copy-start | bytes 12292
  23.0 44.3 %copy-start.18 = (f32[2,16,128]{2,1,0:T(8,128)S(1)}, f32[2,16,128]{2,1,0:T(8,128)}, u32[]{:S(2)}) copy-start(f32[2,16,128]{2,1,0:T(8,128)} %constant.67.clone.twist_ref) | copy-start | bytes 49156
  23.0 44.3 %all-to-all-start = ((f32[8,48,2048]{2,1,0:T(8,128)}), f32[8,48,2048]{2,1,0:T(8,128)S(1)}, u32[]{:S(2)}, u32[]{:S(2)}) async-start(f32[8,48,2048]{2,1,0:T(8,128)} %copy-done), calls=%async_computation | async-start | bytes 6291456 | tf_op jit(solution)/shard_map/all_to_all | solution.py:437
  30.5 1.4 copy-start.1
  31.8 1.0 copy-start.10
  67.3 1.6 copy-start.2
  68.8 1.2 copy-start.11
  70.1 1.0 copy-start.17
  77.0 1.0 copy-start.9
  78.0 0.7 copy-start.21
  78.6 0.6 copy-start.22
  79.3 0.6 copy-start.23
  79.9 0.6 copy-start.24
  80.6 0.6 copy-start.25
  81.2 0.6 copy-start.26
  81.9 0.7 copy-start.27
  82.5 46.0 %all-to-all-start.1 = ((f32[256,8,128]{2,1,0:T(8,128)}), f32[256,8,128]{2,1,0:T(8,128)S(1)}, u32[]{:S(2)}, u32[]{:S(2)}) async-start(f32[256,8,128]{2,1,0:T(8,128)} %bitcast.16), calls=%async_computation.1 | async-start | bytes 2097152 | tf_op jit(solution)/shard_map/all_to_all | solution.py:446
  108.2 20.3 %copy-start.13 = (bf16[256,768]{1,0:T(8,128)(2,1)S(1)}, bf16[256,768]{1,0:T(8,128)(2,1)}, u32[]{:S(2)}) copy-start(bf16[256,768]{1,0:T(8,128)(2,1)} %constant.63.clone.mid_ref) | copy-start | bytes 1179652
  128.5 1.2 copy-start.7
  129.8 1.0 copy-start.14
  130.8 1.0 copy-start.15
  131.7 1.0 copy-start.16
  132.7 0.7 copy-start.19
  133.4 38.7 %copy-start.4 = (f32[2,64,2048]{2,1,0:T(8,128)S(1)}, f32[2,64,2048]{2,1,0:T(8,128)}, u32[]{:S(2)}) copy-start(f32[2,64,2048]{2,1,0:T(8,128)} %seis_ref.1) | copy-start | bytes 3145732
  133.4 38.7 %copy-start.12 = (bf16[768,256]{1,0:T(8,128)(2,1)S(1)}, bf16[768,256]{1,0:T(8,128)(2,1)}, u32[]{:S(2)}) copy-start(bf16[768,256]{1,0:T(8,128)(2,1)} %constant.62.clone.table_ref) | copy-start | bytes 1179652
  137.8 34.3 %all-to-all-start.2 = ((f32[32,8,1024]{2,1,0:T(8,128)}), f32[32,8,1024]{2,1,0:T(8,128)S(1)}, u32[]{:S(2)}, u32[]{:S(2)}) async-start(f32[32,8,1024]{2,1,0:T(8,128)} %bitcast.6), calls=%async_computation.2 | async-start | bytes 2097152 | tf_op jit(solution)/shard_map/all_to_all | solution.py:458
  143.1 12.5 %collective-permute-start.10 = (f32[2,8,2048]{2,1,0:T(8,128)}, f32[2,8,2048]{2,1,0:T(8,128)S(1)}, u32[]{:S(2)}, u32[]{:S(2)}) collective-permute-start(f32[2,8,2048]{2,1,0:T(8,128)} %copy-done.27), channel_id=1, source_target_pairs={{0,7},{1,0},{2,1},{3,2},{4,3},{5,4},{6,5},{7,6},{8,15},{9,8},{10,9... | collective-permute-start | bytes 393224 | tf_op jit(solution)/shard_map/ppermute | solution.py:448
  146.0 13.3 %collective-permute-start.4 = (f32[2,8,2048]{2,1,0:T(8,128)}, f32[2,8,2048]{2,1,0:T(8,128)S(1)}, u32[]{:S(2)}, u32[]{:S(2)}) collective-permute-start(f32[2,8,2048]{2,1,0:T(8,128)} %copy-done.26), channel_id=1, source_target_pairs={{0,1},{1,2},{2,3},{3,4},{4,5},{5,6},{6,7},{7,0},{8,9},{9,10},{10,1... | collective-permute-start | bytes 393224 | tf_op jit(solution)/shard_map/ppermute | solution.py:448
  146.7 14.4 %collective-permute-start.5 = (f32[2,8,2048]{2,1,0:T(8,128)}, f32[2,8,2048]{2,1,0:T(8,128)S(1)}, u32[]{:S(2)}, u32[]{:S(2)}) collective-permute-start(f32[2,8,2048]{2,1,0:T(8,128)} %copy-done.25), channel_id=1, source_target_pairs={{0,2},{1,3},{2,4},{3,5},{4,6},{5,7},{6,0},{7,1},{8,10},{9,11},{10,... | collective-permute-start | bytes 393224 | tf_op jit(solution)/shard_map/ppermute | solution.py:448
  147.5 19.2 %collective-permute-start.6 = (f32[2,8,2048]{2,1,0:T(8,128)}, f32[2,8,2048]{2,1,0:T(8,128)S(1)}, u32[]{:S(2)}, u32[]{:S(2)}) collective-permute-start(f32[2,8,2048]{2,1,0:T(8,128)} %copy-done.24), channel_id=1, source_target_pairs={{0,3},{1,4},{2,5},{3,6},{4,7},{5,0},{6,1},{7,2},{8,11},{9,12},{10,... | collective-permute-start | bytes 393224 | tf_op jit(solution)/shard_map/ppermute | solution.py:448
  150.3 16.4 %collective-permute-start.7 = (f32[2,8,2048]{2,1,0:T(8,128)}, f32[2,8,2048]{2,1,0:T(8,128)S(1)}, u32[]{:S(2)}, u32[]{:S(2)}) collective-permute-start(f32[2,8,2048]{2,1,0:T(8,128)} %copy-done.23), channel_id=1, source_target_pairs={{0,4},{1,5},{2,6},{3,7},{4,0},{5,1},{6,2},{7,3},{8,12},{9,13},{10,... | collective-permute-start | bytes 393224 | tf_op jit(solution)/shard_map/ppermute | solution.py:448
  155.6 13.3 %collective-permute-start.8 = (f32[2,8,2048]{2,1,0:T(8,128)}, f32[2,8,2048]{2,1,0:T(8,128)S(1)}, u32[]{:S(2)}, u32[]{:S(2)}) collective-permute-start(f32[2,8,2048]{2,1,0:T(8,128)} %copy-done.22), channel_id=1, source_target_pairs={{0,5},{1,6},{2,7},{3,0},{4,1},{5,2},{6,3},{7,4},{8,13},{9,14},{10,... | collective-permute-start | bytes 393224 | tf_op jit(solution)/shard_map/ppermute | solution.py:448
  159.3 9.7 %collective-permute-start.9 = (f32[2,8,2048]{2,1,0:T(8,128)}, f32[2,8,2048]{2,1,0:T(8,128)S(1)}, u32[]{:S(2)}, u32[]{:S(2)}) collective-permute-start(f32[2,8,2048]{2,1,0:T(8,128)} %copy-done.21), channel_id=1, source_target_pairs={{0,6},{1,7},{2,0},{3,1},{4,2},{5,3},{6,4},{7,5},{8,14},{9,15},{10,... | collective-permute-start | bytes 393224 | tf_op jit(solution)/shard_map/ppermute | solution.py:448
  172.1 1.2 copy-start.6
  173.4 0.6 copy-start.20

commit v2 on v1

--- a/solution.py
+++ b/solution.py
@@ -132,22 +132,36 @@
     return jnp.where(mask, pick(label, table, bit - 1, base + (1 << bit)), pick(label, table, bit - 1, base))
 
 
-def lookup_kernel(root_ref, inv_ref, label_ref, root_out, inv_out):
+def start(src, dst, sem):
+    copy = pltpu.make_async_copy(src, dst, sem)
+    copy.start()
+    return copy
+
+
+def rows_of(d):
+    return pl.ds(pl.multiple_of(d * 8, 8), 8)
+
+
+def lookup_kernel(root_ref, inv_ref, label_hbm, p_hbm, root_out, inv_out, p_out, label, sems):
+    copy = start(p_hbm, p_out, sems.at[8])
+    loads = [start(label_hbm.at[:, rows_of(d), :], label.at[:, rows_of(d), :], sems.at[d]) for d in range(DEPTHS)]
     width = 512
-
-    def body(i, carry):
-        for l in range(2):
-            for c in range(N // width):
-                rows, cols = pl.ds(pl.multiple_of(i * 8, 8), 8), pl.ds(c * width, width)
-                label = label_ref[l, rows, cols]
-                root_out[l, rows, cols] = pick(label, root_ref, 3, 0)
-                inv_out[l, rows, cols] = pick(label, inv_ref, 3, 0)
-        return carry
-
-    lax.fori_loop(0, ROWS // 8, body, 0)
-
-
-def wells_kernel(where1_ref, where2_ref, amount_ref, col_ref, out1_ref, out2_ref):
+    for d in range(DEPTHS):
+        loads[d].wait()
+
+        def body(c, carry, d=d):
+            cols = pl.ds(pl.multiple_of(c * width, width), width)
+            for l in range(2):
+                zone = label[l, rows_of(d), cols]
+                root_out[l, rows_of(d), cols] = pick(zone, root_ref, 3, 0)
+                inv_out[l, rows_of(d), cols] = pick(zone, inv_ref, 3, 0)
+            return carry
+
+        lax.fori_loop(0, N // width, body, 0)
+    copy.wait()
+
+
+def wells_kernel(where1_ref, where2_ref, amount_ref, col_ref, out1_ref, out2_ref, buf, sems):
     def hits(where_ref, rows, s):
         row = lax.broadcasted_iota(jnp.int32, (rows, 512), 0)
         return jnp.where(row == where_ref[...], amount_ref[s : s + 1, :], 0.0).astype(BF16)
@@ -157,26 +171,45 @@
     for c in range(N // 256):
         at = slice(c * 256, (c + 1) * 256)
         col = lax.broadcasted_iota(jnp.int32, (512, 256), 1) + c * 256
-        both = matmul(left, jnp.where(col == col_of, 1.0, 0.0).astype(BF16))
-        out1_ref[:, at] = both[0:256]
-        out2_ref[:, at] = both[256:384]
-
-
-def pack_kernel(p_ref, q_ref, p_before, p_after, q_before, q_after, out_ref):
-    width = 1024
-    row = lax.broadcasted_iota(jnp.int32, (8, width), 0)
-    for c in range(N // width):
-        at = slice(c * width, (c + 1) * width)
-        for v, (ref, before, after) in enumerate(((p_ref, p_before, p_after), (q_ref, q_before, q_after))):
-            for d in range(DEPTHS):
-                sides = []
-                for l in range(2):
-                    out_ref[d, v * 24 + l * 8 : v * 24 + l * 8 + 8, at] = ref[l, d * 8 : d * 8 + 8, at]
-                    prev = ref[l, d * 8 - 8 : d * 8, at] if d else before[l, :, at]
-                    then = ref[l, d * 8 + 8 : d * 8 + 16, at] if d < DEPTHS - 1 else after[l, :, at]
-                    sides.append(jnp.where(row < 4, then, prev))
-                both = jnp.where((row < 2) | (row >= 6), sides[0], pltpu.roll(sides[1], 4, 0))
-                out_ref[d, v * 24 + 16 : v * 24 + 24, at] = both
+        buf[:, at] = matmul(left, jnp.where(col == col_of, 1.0, 0.0).astype(BF16))
+    copies = [start(buf.at[0:256, :], out1_ref, sems.at[0]), start(buf.at[256:384, :], out2_ref, sems.at[1])]
+    for copy in copies:
+        copy.wait()
+
+
+def pack_kernel(root_ref, p_ref, q_ref, before_ref, after_ref, out_hbm, edge_ref, out_ref, sems):
+    width = 512
+
+    def outside(c, carry):
+        cols = pl.ds(pl.multiple_of(c * width, width), width)
+        for i, ref in enumerate((before_ref, after_ref)):
+            for l in range(2):
+                zone = ref[1, l, :, cols].astype(jnp.int32)
+                edge_ref[i, l, :, cols] = jnp.where(zone > 0, pick(zone - 1, root_ref, 3, 0), 0.0)
+        return carry
+
+    lax.fori_loop(0, N // width, outside, 0)
+    row = lax.broadcasted_iota(jnp.int32, (8, N), 0)
+    copies = []
+    for d in range(DEPTHS):
+        for v, ref in enumerate((p_ref, q_ref)):
+            sides = []
+            for l in range(2):
+                out_ref[d, v * 24 + l * 8 : v * 24 + l * 8 + 8, :] = ref[l, d * 8 : d * 8 + 8, :]
+                if d:
+                    prev = ref[l, d * 8 - 8 : d * 8, :]
+                else:
+                    prev = edge_ref[0, l] if v else before_ref[0, l]
+                if d < DEPTHS - 1:
+                    then = ref[l, d * 8 + 8 : d * 8 + 16, :]
+                else:
+                    then = edge_ref[1, l] if v else after_ref[0, l]
+                sides.append(jnp.where(row < 4, then, prev))
+            both = jnp.where((row < 2) | (row >= 6), sides[0], pltpu.roll(sides[1], 4, 0))
+            out_ref[d, v * 24 + 16 : v * 24 + 24, :] = both
+        copies.append(start(out_ref.at[d], out_hbm.at[d], sems.at[d]))
+    for copy in copies:
+        copy.wait()
 
 
 def sideways(value, col):
@@ -194,9 +227,13 @@
     return of_main, of_side
 
 
-def diffuse_kernel(me_ref, msg_ref, src1_ref, src2_ref, fwd_ref, twist_ref, *rest):
-    outs, spec_out, (q_ref, u_ref, w_ref, p_ref, s_ref, mid_ref) = rest[:8], rest[8], rest[9:]
+def diffuse_kernel(me_ref, msg_ref, src1_hbm, src2_hbm, fwd_hbm, twist_ref, *rest):
+    outs, spec_hbm = rest[:8], rest[8]
+    q_ref, u_ref, w_ref, p_ref, s_ref, mid_ref, new_ref, spec_out, src1_ref, src2_ref, fwd_ref, sems = rest[9:]
     me = me_ref[0]
+    src1_load = start(src1_hbm, src1_ref, sems.at[0, 0])
+    src2_load = start(src2_hbm, src2_ref, sems.at[0, 1])
+    fwd_load = start(fwd_hbm, fwd_ref, sems.at[0, 2])
     zero = jnp.zeros((16, N), F32)
     for ref in (q_ref, u_ref, w_ref):
         ref[0] = zero
@@ -219,9 +256,9 @@
         return carry
 
     lax.fori_loop(0, DEPTHS, fill, 0)
+    src1_load.wait()
 
     def first(z, carry):
-        d, l = z // 2, z % 2
         q, q_side = q_ref[z + 1, 0:8, :], q_ref[z + 1, 8:16, :]
         sums, sides = around(q, q_side, row)
         s = sums + sideways(q, col) + (q_ref[z, 0:8, :] + q_ref[z + 2, 0:8, :])
@@ -232,7 +269,7 @@
         t_side = sides + sideways(u_side, col) + (u_ref[z, 8:16, :] + u_ref[z + 2, 8:16, :])
         at = pl.ds(pl.multiple_of(z * 16, 16), 8)
         side_at = pl.ds(pl.multiple_of(z * 16 + 8, 8), 8)
-        p = msg_ref[d, pl.ds(pl.multiple_of(l * 8, 8), 8), :]
+        p = msg_ref[z // 2, pl.ds(pl.multiple_of(z % 2 * 8, 8), 8), :]
         new = p + (conduct * q) * (t - p * s) + src1_ref[at, :]
         p_side = p_ref[z, 8:16, :]
         new_side = p_side + (conduct * q_side) * (t_side - p_side * s_side) + src1_ref[side_at, :]
@@ -244,7 +281,9 @@
 
     lax.fori_loop(0, 2 * DEPTHS, first, 0)
 
-    for k in range(DEPTHS):
+    src2_load.wait()
+    copies = []
+    for k in (1, 2, 3, 4, 5, 6, 7, 0):
         d = lax.rem(me + k, DEPTHS)
         for l in range(2):
             z = d * 2 + l
@@ -252,15 +291,20 @@
             sums, _ = around(w, w_ref[z + 1, 8:16, :], row)
             t = sums + sideways(w, col) + (w_ref[z, 0:8, :] + w_ref[z + 2, 0:8, :])
             p = p_ref[z, 0:8, :]
-            at = pl.ds(pl.multiple_of(z * 8, 8), 8)
-            new = p + (conduct * q_ref[z + 1, 0:8, :]) * (t - p * s_ref[z]) + src2_ref[at, :]
-            outs[k][l] = new
-        spectrum_of_rows(outs[k], twist_ref, mid_ref, d)
+            new = p + (conduct * q_ref[z + 1, 0:8, :]) * (t - p * s_ref[z]) + src2_ref[rows_of(z), :]
+            new_ref[k, l] = new
+        copies.append(start(new_ref.at[k], outs[k], sems.at[1, k]))
+        spectrum_of_rows(new_ref.at[k], twist_ref, mid_ref, d)
+    fwd_load.wait()
     for c in range(4):
         part = triple(mid_ref[c * 256 : (c + 1) * 256, :], 1)
         block = lax.dot_general(fwd_ref[...], part, (((1,), (1,)), ((), ())), preferred_element_type=F32)
         for h in range(2):
-            spec_out[:, c * 2 + h] = block[:, h * 128 : (h + 1) * 128].reshape(SLABS, 8, 128)
+            at = c * 2 + h
+            spec_out[:, at] = block[:, h * 128 : (h + 1) * 128].reshape(SLABS, 8, 128)
+            copies.append(start(spec_out.at[:, at], spec_hbm.at[:, at], sems.at[2, at]))
+    for copy in copies:
+        copy.wait()
 
 
 def spectrum_of_rows(p_ref, twist_ref, mid_ref, d):
@@ -312,14 +356,23 @@
 
 
 def middle_kernel(
-    spec_ref, green_ref, mid_ref, mid_inv_ref, inner_ref, inner_inv_ref, col_ref, in_ref, out_ref, work
+    spec_ref, green_ref, mid_hbm, mid_inv_hbm, inner_hbm, inner_inv_hbm, col_hbm, in_ref, out_hbm,
+    work, out_ref, mid_ref, mid_inv_ref, inner_ref, inner_inv_ref, col_ref, sems,
 ):
+    pairs = (
+        (mid_hbm, mid_ref), (col_hbm, col_ref), (inner_hbm, inner_ref), (inner_inv_hbm, inner_inv_ref),
+        (mid_inv_hbm, mid_inv_ref),
+    )
+    loads = [start(src, dst, sems.at[i]) for i, (src, dst) in enumerate(pairs)]
+    loads[0].wait()
     for d in range(0, DEPTHS, 2):
         part = jnp.concatenate([spec_ref[:, d + h].reshape(256, 128) for h in range(2)], 1)
         spread = matmul(mid_ref[...], triple(part, 0))
         for h in range(2):
             work[0, d + h] = spread[0:128, h * 128 : (h + 1) * 128]
             work[1, d + h] = spread[128:256, h * 128 : (h + 1) * 128]
+    for copy in loads[1:]:
+        copy.wait()
     across(work, -1, col_ref, in_ref)
     for k in range(0, DEPTHS, 2):
         part = [jnp.concatenate([work[0, k + h], work[1, k + h]], 1) for h in range(2)]
@@ -331,45 +384,64 @@
             work[0, k + h] = back[h * 128 : (h + 1) * 128, 0:128]
             work[1, k + h] = back[h * 128 : (h + 1) * 128, 128:256]
     across(work, 1, col_ref, in_ref)
+    copies = []
     for d in range(0, DEPTHS, 2):
         part = [jnp.concatenate([work[0, d + h], work[1, d + h]], 0) for h in range(2)]
-        out_ref[:, d * 128 : (d + 2) * 128] = matmul(mid_inv_ref[...], triple(jnp.concatenate(part, 1), 0))
-
-
-def last_kernel(me_ref, weight_ref, spec_ref, inv_ref, seis_ref, table_ref, twist_ref, *rest):
-    parts, (p_out, state_out, rate_out, mid_ref) = rest[:DEPTHS], rest[DEPTHS:]
+        at = slice(d * 128, (d + 2) * 128)
+        out_ref[:, at] = matmul(mid_inv_ref[...], triple(jnp.concatenate(part, 1), 0))
+        copies.append(start(out_ref.at[:, at], out_hbm.at[:, at], sems.at[5 + d]))
+    for copy in copies:
+        copy.wait()
+
+
+def last_kernel(me_ref, weight_ref, spec_ref, inv_hbm, seis_hbm, table_hbm, twist_ref, *rest):
+    parts, rest = rest[:DEPTHS], rest[DEPTHS:]
+    p_out, state_out, rate_out, rest = rest[0], rest[1], rest[2], rest[3:]
+    p_ref, inv_ref, seis_ref, table_ref, state_ref, rate_ref, mid_ref, sems = rest
     me = me_ref[0]
+    table_load = start(table_hbm, table_ref, sems.at[4, 0])
+    loads = [start(inv_hbm, inv_ref, sems.at[4, 1]), start(seis_hbm, seis_ref, sems.at[4, 2])]
+    copies = []
+    for k in range(DEPTHS):
+        d = lax.rem(me + (DEPTHS - k), DEPTHS)
+        loads.append(start(parts[k], p_ref.at[:, rows_of(d), :], sems.at[0, k]))
+    table_load.wait()
     for c in range(4):
         turned = jnp.transpose(spec_ref[:, c * 256 : (c + 1) * 256])
         mid_ref[c * 256 : (c + 1) * 256, :] = matmul(triple(turned, 1), table_ref[...])
-    for k in range(DEPTHS):
-        d = lax.rem(me + (DEPTHS - k), DEPTHS)
-        p_out[:, pl.ds(pl.multiple_of(d * 8, 8), 8), :] = parts[k][...]
+    for copy in loads:
+        copy.wait()
+    copies.append(start(p_ref, p_out, sems.at[1, 0]))
 
     def body(i, carry):
-        rows = pl.ds(pl.multiple_of(i * 8, 8), 8)
+        rows = rows_of(i)
         items = []
         for k in range(TILES):
             at = pl.ds(pl.multiple_of(i * 128 + k * 8, 8), 8)
-            re, im = mid_ref[at, 0:128], mid_ref[at, 128:256]
+            item = (mid_ref[at, 0:128], mid_ref[at, 128:256])
             if k:
-                cos, sin = twist_ref[0, k : k + 1, :], twist_ref[1, k : k + 1, :]
-                re, im = re * cos + im * sin, im * cos - re * sin
-            items.append((re, im))
+                item = turn(item, twist_ref[0, k : k + 1, :], twist_ref[1, k : k + 1, :], 1)
+            items.append(item)
         for n, stress in enumerate(dft16(items, 1)):
             at = slice(n * 128, (n + 1) * 128)
             total = None
             for l in range(2):
-                coulomb = stress[l] + friction * p_out[l, rows, at]
+                coulomb = stress[l] + friction * p_ref[l, rows, at]
                 grown = seis_ref[l, rows, at] * jnp.exp(-coulomb * inv_ref[l, rows, at])
                 state = 1.0 + (grown - 1.0) * recovery
-                state_out[l, rows, at] = state
+                state_ref[i, l, :, at] = state
                 term = weight_ref[l] / state
                 total = term if total is None else total + term
-            rate_out[n // 2, rows, (n % 2) * 128 : (n % 2) * 128 + 128] = total
+            rate_ref[n // 2, rows, (n % 2) * 128 : (n % 2) * 128 + 128] = total
+        pltpu.make_async_copy(state_ref.at[i], state_out.at[:, rows, :], sems.at[2, i]).start()
         return carry
 
-    lax.fori_loop(0, ROWS // 8, body, 0)
+    lax.fori_loop(0, DEPTHS, body, 0)
+    copies.append(start(rate_ref, rate_out, sems.at[3, 0]))
+    for i in range(DEPTHS):
+        pltpu.make_async_copy(state_ref.at[i], state_out.at[:, rows_of(i), :], sems.at[2, i]).wait()
+    for copy in copies:
+        copy.wait()
 
 
 def sum_kernel(part_ref, out_ref):
@@ -383,23 +455,24 @@
     return jax.ShapeDtypeStruct(shape, F32)
 
 
-def in_vmem(count):
-    return [pl.BlockSpec(memory_space=pltpu.VMEM)] * count
-
-
-def in_smem(count):
-    return [pl.BlockSpec(memory_space=pltpu.SMEM)] * count
-
-
-def call(kernel, mib, outs, smem, args, scratch=()):
+SMEM, VMEM, ANY, HBM = pltpu.SMEM, pltpu.VMEM, pl.ANY, pltpu.HBM
+DMA = pltpu.SemaphoreType.DMA
+
+
+def call(kernel, mib, args, outs, scratch=()):
+    values = [pltpu.with_memory_space_constraint(value, space) if space is HBM else value for space, value in args]
     return pl.pallas_call(
         kernel,
-        out_shape=outs,
-        in_specs=in_smem(smem) + in_vmem(len(args) - smem),
-        out_specs=tuple(in_vmem(len(outs))) if isinstance(outs, tuple) else in_vmem(1)[0],
-        scratch_shapes=[pltpu.VMEM(s, F32) for s in scratch],
+        out_shape=[HBM(shape, F32) if space is HBM else vec(*shape) for space, shape in outs],
+        in_specs=[pl.BlockSpec(memory_space=space) for space, _ in args],
+        out_specs=[pl.BlockSpec(memory_space=space) for space, _ in outs],
+        scratch_shapes=scratch,
         compiler_params=pltpu.CompilerParams(vmem_limit_bytes=mib * 1024 * 1024),
-    )(*args)
+    )(*values)
+
+
+def buf(*shape, dtype=F32):
+    return pltpu.VMEM(shape, dtype)
 
 
 def shift(value, axis, step):
@@ -408,19 +481,29 @@
     return lax.ppermute(value, axis, pairs)
 
 
+def rotate(values):
+    moved = [lax.ppermute(v, "depth", [(i, (i + k) % DEPTHS) for i in range(DEPTHS)]) for k, v in enumerate(values) if k]
+    return [values[0]] + moved
+
+
 def shards(pressure, zone_labels, perm_table, asig_table, well_cells, rate_levels, green_spectrum, seis_state):
     tab = {name: jnp.asarray(value) for name, value in tables().items()}
     depth, slab = lax.axis_index("depth"), lax.axis_index("slab")
-    me = depth.reshape(1)
-    block = vec(2, ROWS, N)
-
-    p_before = shift(pressure[:, ROWS - 8 :], "slab", 1)
-    p_after = shift(pressure[:, :8], "slab", -1)
-    root, inv = call(
-        lookup_kernel, 12, (block, block), 2, (jnp.sqrt(perm_table), 1.0 / asig_table, zone_labels)
-    )
-    q_before = shift(root[:, ROWS - 8 :], "slab", 1)
-    q_after = shift(root[:, :8], "slab", -1)
+    me = (SMEM, depth.reshape(1))
+    rows, block = (2, 8, N), (2, ROWS, N)
+
+    def edge(at):
+        return jnp.stack([pressure[:, at], (zone_labels[:, at] + 1).astype(F32)])
+
+    before, after = shift(edge(slice(ROWS - 8, ROWS)), "slab", 1), shift(edge(slice(0, 8)), "slab", -1)
+    root_table = (SMEM, jnp.sqrt(perm_table))
+    root, inv, p_copy = call(
+        lookup_kernel,
+        12,
+        (root_table, (SMEM, 1.0 / asig_table), (HBM, zone_labels), (HBM, pressure)),
+        [(VMEM, block)] * 3,
+        [buf(*block, dtype=jnp.int32), DMA((9,))],
+    )
 
     offset = well_cells[:, 1] - (slab * ROWS + depth * 8)
     near = (offset >= -2) & (offset < 10)
@@ -428,32 +511,43 @@
     own = (offset >= 0) & (offset < 8)
     spot2 = jnp.where(own, well_cells[:, 0] * 8 + offset, -1)[None, :]
     amounts = rate_unit * rate_levels.astype(F32)
-    src1, src2 = call(wells_kernel, 12, (vec(256, N), vec(128, N)), 0, (spot1, spot2, amounts, well_cells[:, 2:3]))
+    src1, src2 = call(
+        wells_kernel,
+        12,
+        ((VMEM, spot1), (VMEM, spot2), (VMEM, amounts), (VMEM, well_cells[:, 2:3])),
+        [(HBM, (256, N)), (HBM, (128, N))],
+        [buf(384, N), DMA((2,))],
+    )
 
     green = (green_spectrum * (1.0 / (N * N))).reshape(8, 8, SLABS, FREQS, TILES)
     green = green.transpose(1, 2, 3, 4, 0).reshape(8, STEP, LANES)
 
-    msg = call(pack_kernel, 14, vec(DEPTHS, 48, N), 0, (pressure, root, p_before, p_after, q_before, q_after))
+    (msg,) = call(
+        pack_kernel,
+        16,
+        (root_table, (VMEM, p_copy), (VMEM, root), (VMEM, before), (VMEM, after)),
+        [(HBM, (DEPTHS, 48, N))],
+        [buf(2, *rows), buf(DEPTHS, 48, N), DMA((8,))],
+    )
     msg = lax.all_to_all(msg, "depth", 0, 0, tiled=True)
     *parts, spec = call(
         diffuse_kernel,
         30,
-        (vec(2, 8, N),) * DEPTHS + (vec(SLABS, DEPTHS, 8, LANES),),
-        1,
-        (me, msg, src1, src2, tab["fwd"], tab["row_twist"]),
-        ((18, 16, N), (18, 16, N), (18, 16, N), (16, 16, N), (16, 8, N), (1024, 256)),
+        (me, (VMEM, msg), (HBM, src1), (HBM, src2), (HBM, tab["fwd"]), (VMEM, tab["row_twist"])),
+        [(HBM, rows)] * DEPTHS + [(HBM, (SLABS, DEPTHS, 8, LANES))],
+        [buf(18, 16, N), buf(18, 16, N), buf(18, 16, N), buf(16, 16, N), buf(16, 8, N), buf(1024, 256),
+         buf(8, *rows), buf(SLABS, DEPTHS, 8, LANES), buf(256, N), buf(128, N), buf(256, 768, dtype=BF16), DMA((3, 8))],
     )
     spec = lax.all_to_all(spec.reshape(SLABS * DEPTHS, 8, LANES), ("slab", "depth"), 0, 0, tiled=True)
-    for k in range(1, DEPTHS):
-        parts[k] = lax.ppermute(parts[k], "depth", [(i, (i + k) % DEPTHS) for i in range(DEPTHS)])
-    spec = call(
+    parts = rotate(parts)
+    (spec,) = call(
         middle_kernel,
-        24,
-        vec(256, 1024),
-        0,
-        (spec.reshape(SLABS, DEPTHS, 8, LANES), green, tab["mid"], tab["mid_inv"], tab["inner"], tab["inner_inv"],
-         tab["col_twist"], tab["in_twist"]),
-        ((2, DEPTHS, STEP, LANES),),
+        16,
+        ((VMEM, spec.reshape(SLABS, DEPTHS, 8, LANES)), (VMEM, green), (HBM, tab["mid"]), (HBM, tab["mid_inv"]),
+         (HBM, tab["inner"]), (HBM, tab["inner_inv"]), (HBM, tab["col_twist"]), (VMEM, tab["in_twist"])),
+        [(HBM, (256, 1024))],
+        [buf(2, DEPTHS, STEP, LANES), buf(256, 1024), buf(256, 768, dtype=BF16), buf(256, 768, dtype=BF16),
+         buf(768, 256, dtype=BF16), buf(768, 256, dtype=BF16), buf(2, 8, STEP, LANES), DMA((12,))],
     )
     spec = lax.all_to_all(spec.reshape(SLABS, 8, 1024), "slab", 0, 0, tiled=True).reshape(256, 1024)
     layer_pos = (depth * 2 + jnp.arange(2, dtype=jnp.int32)).astype(F32)
@@ -461,13 +555,14 @@
     press, state, rate = call(
         last_kernel,
         18,
-        (block, block, vec(DEPTHS, ROWS, 2 * LANES)),
-        2,
-        (me, weights, spec, inv, seis_state, tab["inv"], tab["row_twist"], *parts),
-        ((1024, 256),),
+        (me, (SMEM, weights), (VMEM, spec), (HBM, inv), (HBM, seis_state), (HBM, tab["inv"]), (VMEM, tab["row_twist"]),
+         *[(ANY, v) for v in parts]),
+        [(HBM, block)] * 2 + [(HBM, (DEPTHS, ROWS, 2 * LANES))],
+        [buf(*block), buf(*block), buf(*block), buf(768, 256, dtype=BF16), buf(8, *rows),
+         buf(DEPTHS, ROWS, 2 * LANES), buf(1024, 256), DMA((5, 8))],
     )
     rate = lax.all_to_all(rate, "depth", 0, 0, tiled=True)
-    rate_map = call(sum_kernel, 4, vec(ROWS, 2 * LANES), 0, (rate,))
+    (rate_map,) = call(sum_kernel, 4, [(VMEM, rate)], [(VMEM, (ROWS, 2 * LANES))])
     return (press, state, rate_map)
 
 

time: 195 us -> 175 us (0.90)
  local copies, waits for them, and re-layouts: 39.2 us -> 16.3 us
  starting transfers between devices: 53.7 us -> 39.3 us
  Pallas kernels: 17.7 us -> 27.4 us
  waiting for transfers between devices: 64.1 us -> 70.6 us
    unnamed x61 -> x27, local copies, waits for them, and re-layouts: 22.6 us -> 1.22 us
    pallas_call x7, Pallas kernels: 17.7 us -> 27.4 us  [call(): pl.pallas_call(kernel, out_shape=[HBM(shape, F32) if space is HBM else ve...]
    ppermute x4 -> x2, starting transfers between devices: 11.1 us -> 5.56 us  [shift(): return lax.ppermute(value, axis, pairs)]
    all_to_all x1, starting transfers between devices: 16 us -> 11.3 us  [shards(): lax.all_to_all(spec.reshape(SLABS * DEPTHS, 8, LANES), ('slab', 'depth'),...]
    ppermute x7, waiting for transfers between devices: 10.1 us -> 14.6 us  [rotate(): lax.ppermute(v, 'depth', [(i, (i + k) % DEPTHS) for i in range(DEPTHS)])]
    ppermute x7, starting transfers between devices: 15.2 us -> 10.9 us  [rotate(): lax.ppermute(v, 'depth', [(i, (i + k) % DEPTHS) for i in range(DEPTHS)])]
    all_to_all x1, waiting for transfers between devices: 34.5 us -> 38 us  [shards(): msg = lax.all_to_all(msg, 'depth', 0, 0, tiled=True)]
    ppermute x4 -> x2, waiting for transfers between devices: 2.48 us -> 0.01 us  [shift(): return lax.ppermute(value, axis, pairs)]
  transfers between devices with their start and end apart: 14 -> 12, of which waited for: 8 -> 7; matrix products, arithmetic and copies ran while one was open for 9% -> 10% of each run, Pallas kernels for 1% -> 4%
where the time goes in v2:
time: 175 us; the launch traced here: 174 us
  waiting for transfers between devices  70.6 us (40%)
  starting transfers between devices  39.3 us (22%)
  Pallas kernels  27.4 us (16%)
  local copies, waits for them, and re-layouts  16.3 us (9%)
  blocking collectives  15.9 us (9%)
  other arithmetic  3.59 us (2%)
    all_to_all x1, waiting for transfers between devices, shards(): msg = lax.all_to_all(msg, 'depth', 0, 0, tiled=True)  38 us
    pallas_call x7, Pallas kernels, call(): pl.pallas_call(kernel, out_shape=[HBM(shape, F32) if space is HBM else ve...  27.4 us
    all_to_all x1, blocking collectives, shards(): rate = lax.all_to_all(rate, 'depth', 0, 0, tiled=True)  15.9 us
    all_to_all x1, waiting for transfers between devices, shards(): lax.all_to_all(spec.reshape(SLABS * DEPTHS, 8, LANES), ('slab', 'depth'),...  14.6 us
    ppermute x7, waiting for transfers between devices, rotate(): lax.ppermute(v, 'depth', [(i, (i + k) % DEPTHS) for i in range(DEPTHS)])  14.6 us
    all_to_all x1, starting transfers between devices, shards(): lax.all_to_all(spec.reshape(SLABS * DEPTHS, 8, LANES), ('slab', 'depth'),...  11.3 us
    ppermute x7, starting transfers between devices, rotate(): lax.ppermute(v, 'depth', [(i, (i + k) % DEPTHS) for i in range(DEPTHS)])  10.9 us
    reshape x2, local copies, waits for them, and re-layouts, shards(): (green_spectrum * (1.0 / (N * N))).reshape(8, 8, SLABS, FREQS, TILES)  7.07 us
  transfers between devices with their start and end apart: 12, of which 7 were waited for; matrix products, arithmetic and copies ran while one was open for 10% of the time, Pallas kernels for 4%

profile of v2, /device:TPU:2, one launch (start us, length us, event | category | flops | bytes accessed | tf_op | source)
XLA Modules:
  0.0 174.0 jit_solution(9370188261886883253)
XLA Ops:
  0.6 1.0 slice_bitcast_fusion
  1.6 1.0 convert_bitcast_fusion
  2.6 1.9 %collective-permute-start = (f32[2,2,8,2048]{3,2,1,0:T(8,128)S(1)}, f32[2,2,8,2048]{3,2,1,0:T(8,128)S(1)}, u32[]{:S(2)}, u32[]{:S(2)}) collective-permute-start(f32[2,2,8,2048]{3,2,1,0:T(8,128)S(1)} %pad_maximum_fusion), channel_id=1, source_target_pairs={{0,8},{8,16},{16,24},{24,32},{32,40},{40,48},{48,56},{56,64},{64,7... | collective-permute-start | bytes 786440 | tf_op jit(solution)/shard_map/ppermute | solution.py:481
  4.6 3.6 %collective-permute-start.1 = (f32[2,2,8,2048]{3,2,1,0:T(8,128)S(1)}, f32[2,2,8,2048]{3,2,1,0:T(8,128)S(1)}, u32[]{:S(2)}, u32[]{:S(2)}) collective-permute-start(f32[2,2,8,2048]{3,2,1,0:T(8,128)S(1)} %pad_maximum_fusion.1), channel_id=1, source_target_pairs={{8,0},{16,8},{24,16},{32,24},{40,32},{48,40},{56,48},{64,56},{72,6... | collective-permute-start | bytes 786440 | tf_op jit(solution)/shard_map/ppermute | solution.py:481
  8.2 0.7 sqrt.3.root_ref
  8.9 0.7 broadcast_divide_fusion.inv_ref
  9.6 3.4 %shard_map.184 = (f32[2,64,2048]{2,1,0:T(8,128)S(1)}, f32[2,64,2048]{2,1,0:T(8,128)S(1)}, f32[2,64,2048]{2,1,0:T(8,128)S(1)}) custom-call(f32[16]{0:T(128)S(1)} %sqrt.3.root_ref, f32[16]{0:T(128)S(1)} %broadcast_divide_fusion.inv_ref, s32[2,64,2048]{2,1,0:T(8,128)} %label_hbm.1, f32[2,64,2048]{2,1,0:T(8,128)} %p_hbm.1), custom_call_target="tpu_custom_call" | custom-call | tf_op jit(solution)/shard_map/pallas_call | solution.py:464
  13.0 1.0 copy-done
  14.0 0.0 collective-permute-done.before_ref
  14.0 0.0 collective-permute-done.1.after_ref
  14.0 2.6 %shard_map.185 = f32[8,48,2048]{2,1,0:T(8,128)} custom-call(f32[16]{0:T(128)S(1)} %sqrt.3.root_ref, f32[2,64,2048]{2,1,0:T(8,128)S(1)} %get-tuple-element.20.p_ref, f32[2,64,2048]{2,1,0:T(8,128)S(1)} %get-tuple-element.21.q_ref, f32[2,2,8,2048]{3,2,1,0:T(8,128)S(1)} %collective-permute-done.before_ref, f32[2,2,8,2048]{3,2,1,0:T(8,128)S(1)} %collective-permute-done.1.after_ref), custom_call_target="tpu_custom_call" | custom-call | tf_op jit(solution)/shard_map/pallas_call | solution.py:464
  16.6 0.0 copy-start.4
  16.6 0.0 copy-start.5
  16.6 0.0 copy-start.2
  16.7 6.2 %all-to-all-start = ((f32[8,48,2048]{2,1,0:T(8,128)}), f32[8,48,2048]{2,1,0:T(8,128)S(1)}, u32[]{:S(2)}, u32[]{:S(2)}) async-start(f32[8,48,2048]{2,1,0:T(8,128)} %shard_map.185), calls=%async_computation | async-start | bytes 6291456 | tf_op jit(solution)/shard_map/all_to_all | solution.py:532
  22.8 0.0 copy-done.4
  22.9 0.1 copy.24.col_ref
  23.0 2.8 %shard_map.186 = (f32[256,2048]{1,0:T(8,128)}, f32[128,2048]{1,0:T(8,128)}) custom-call(s32[1,512]{1,0:T(1,128)S(1)} %get-tuple-element.43.where1_ref, s32[1,512]{1,0:T(1,128)S(1)} %get-tuple-element.42.where2_ref, f32[2,512]{1,0:T(2,128)S(1)} %convert_multiply_fusion.amount_ref, s32[512,1]{1,0:T(8,128)S(1)} %copy.24.col_ref), custom_call_target="tpu_custom_call" | custom-call | tf_op jit(solution)/shard_map/pallas_call | solution.py:464
  25.8 38.0 %all-to-all-done.msg_ref = f32[8,48,2048]{2,1,0:T(8,128)S(1)} async-done(((f32[8,48,2048]{2,1,0:T(8,128)}), f32[8,48,2048]{2,1,0:T(8,128)S(1)}, u32[]{:S(2)}, u32[]{:S(2)}) %all-to-all-start) | async-done | bytes 3145760 | tf_op jit(solution)/shard_map/all_to_all | solution.py:532
  63.8 8.2 %shard_map.187 = (f32[2,8,2048]{2,1,0:T(8,128)}, f32[2,8,2048]{2,1,0:T(8,128)}, f32[2,8,2048]{2,1,0:T(8,128)}, f32[2,8,2048]{2,1,0:T(8,128)}, f32[2,8,2048]{2,1,...) custom-call(s32[1]{0:T(128)} %bitcast.me_ref, ...), custom_call_target="tpu_custom_call" | custom-call | tf_op jit(solution)/shard_map/pallas_call | solution.py:464
  72.0 11.3 %all-to-all-start.1 = ((f32[256,8,128]{2,1,0:T(8,128)}), f32[256,8,128]{2,1,0:T(8,128)S(1)}, u32[]{:S(2)}, u32[]{:S(2)}) async-start(f32[256,8,128]{2,1,0:T(8,128)} %bitcast.26), calls=%async_computation.1 | async-start | bytes 2097152 | tf_op jit(solution)/shard_map/all_to_all | solution.py:541
  83.3 1.9 %broadcast_multiply_fusion = f32[2048,64]{0,1:T(8,128)} fusion(f32[2048,64]{0,1:T(8,128)} %param.23), kind=kLoop, calls=%fused_computation.2 | loop fusion | flops 131072 | bytes 1048576 | tf_op jit(solution)/shard_map/mul | solution.py:522
  85.2 1.8 %reshape.121 = f32[8,8,32,4,16]{2,1,0,4,3:T(8,128)S(1)} reshape(f32[2048,64]{0,1:T(8,128)} %broadcast_multiply_fusion) | data formatting | bytes 1048576 | tf_op jit(solution)/shard_map/reshape | solution.py:522
  87.0 5.3 %copy.23 = f32[8,8,32,4,16]{0,4,3,2,1:T(8,128)} copy(f32[8,8,32,4,16]{2,1,0,4,3:T(8,128)S(1)} %reshape.121) | data formatting | bytes 1048576 | tf_op jit(solution)/shard_map/reshape | solution.py:522
  92.3 6.4 %reshape.122.green_ref = f32[8,128,128]{2,1,0:T(8,128)S(1)} reshape(f32[8,32,4,16,8]{4,3,2,1,0:T(8,128)} %bitcast.24) | data formatting | bytes 1048576 | tf_op jit(solution)/shard_map/reshape | solution.py:523
  98.7 14.6 %all-to-all-done.1 = f32[256,8,128]{2,1,0:T(8,128)S(1)} async-done(((f32[256,8,128]{2,1,0:T(8,128)}), f32[256,8,128]{2,1,0:T(8,128)S(1)}, u32[]{:S(2)}, u32[]{:S(2)}) %all-to-all-start.1) | async-done | bytes 1048608 | tf_op jit(solution)/shard_map/all_to_all | solution.py:541
  113.3 0.0 copy-done.3
  113.4 5.5 %shard_map.188 = f32[256,1024]{1,0:T(8,128)} custom-call(f32[32,8,8,128]{3,2,1,0:T(8,128)S(1)} %bitcast.23, f32[8,128,128]{2,1,0:T(8,128)S(1)} %reshape.122.green_ref, bf16[256,768]{1,0:T(8,128)(2,1)} %constant.65.clone.mid_hbm, bf16[256,768]{1,0:T(8,128)(2,1)} %constant.66.clone.mid_inv_hbm, bf16[768,256]{1,0:T(8,128)(2,1)} %constant.67.clone.inner_hbm, ...), custom_call_target="tpu_custom_call" | custom-call | tf_op jit(solution)/shard_map/pallas_call | solution.py:464
  118.9 5.3 %all-to-all-start.2 = ((f32[32,8,1024]{2,1,0:T(8,128)}), f32[32,8,1024]{2,1,0:T(8,128)S(1)}, u32[]{:S(2)}, u32[]{:S(2)}) async-start(f32[32,8,1024]{2,1,0:T(8,128)} %bitcast.25), calls=%async_computation.2 | async-start | bytes 2097152 | tf_op jit(solution)/shard_map/all_to_all | solution.py:552
  124.1 1.6 collective-permute-start.2
  125.8 0.7 collective-permute-start.3
  126.5 2.8 %collective-permute-start.4 = (f32[2,8,2048]{2,1,0:T(8,128)S(1)}, f32[2,8,2048]{2,1,0:T(8,128)S(1)}, u32[]{:S(2)}, u32[]{:S(2)}) collective-permute-start(f32[2,8,2048]{2,1,0:T(8,128)S(1)} %copy-done.10), channel_id=1, source_target_pairs={{0,3},{1,4},{2,5},{3,6},{4,7},{5,0},{6,1},{7,2},{8,11},{9,12},{10,... | collective-permute-start | bytes 393224 | tf_op jit(solution)/shard_map/ppermute | solution.py:485
  129.3 2.8 %collective-permute-start.5 = (f32[2,8,2048]{2,1,0:T(8,128)S(1)}, f32[2,8,2048]{2,1,0:T(8,128)S(1)}, u32[]{:S(2)}, u32[]{:S(2)}) collective-permute-start(f32[2,8,2048]{2,1,0:T(8,128)S(1)} %copy-done.9), channel_id=1, source_target_pairs={{0,4},{1,5},{2,6},{3,7},{4,0},{5,1},{6,2},{7,3},{8,12},{9,13},{10,... | collective-permute-start | bytes 393224 | tf_op jit(solution)/shard_map/ppermute | solution.py:485
  132.2 0.0 copy-done.8
  132.2 2.8 %collective-permute-start.6 = (f32[2,8,2048]{2,1,0:T(8,128)S(1)}, f32[2,8,2048]{2,1,0:T(8,128)S(1)}, u32[]{:S(2)}, u32[]{:S(2)}) collective-permute-start(f32[2,8,2048]{2,1,0:T(8,128)S(1)} %copy-done.8), channel_id=1, source_target_pairs={{0,5},{1,6},{2,7},{3,0},{4,1},{5,2},{6,3},{7,4},{8,13},{9,14},{10,... | collective-permute-start | bytes 393224 | tf_op jit(solution)/shard_map/ppermute | solution.py:485
  135.0 3.9 %collective-permute-done.2.rest_1_ = f32[2,8,2048]{2,1,0:T(8,128)S(1)} collective-permute-done((f32[2,8,2048]{2,1,0:T(8,128)S(1)}, f32[2,8,2048]{2,1,0:T(8,128)S(1)}, u32[]{:S(2)}, u32[]{:S(2)}) %collective-permute-start.2) | collective-permute-done | bytes 131104 | tf_op jit(solution)/shard_map/ppermute | solution.py:485
  138.9 0.0 collective-permute-start.7
  138.9 0.0 collective-permute-done.3.rest_2_
  138.9 0.1 collective-permute-start.8
  139.0 2.0 %collective-permute-done.4.rest_3_ = f32[2,8,2048]{2,1,0:T(8,128)S(1)} collective-permute-done((f32[2,8,2048]{2,1,0:T(8,128)S(1)}, f32[2,8,2048]{2,1,0:T(8,128)S(1)}, u32[]{:S(2)}, u32[]{:S(2)}) %collective-permute-start.4) | collective-permute-done | bytes 131104 | tf_op jit(solution)/shard_map/ppermute | solution.py:485
  141.0 0.0 collective-permute-done.5.rest_4_
  141.0 6.1 %collective-permute-done.6.rest_5_ = f32[2,8,2048]{2,1,0:T(8,128)S(1)} collective-permute-done((f32[2,8,2048]{2,1,0:T(8,128)S(1)}, f32[2,8,2048]{2,1,0:T(8,128)S(1)}, u32[]{:S(2)}, u32[]{:S(2)}) %collective-permute-start.6) | collective-permute-done | bytes 131104 | tf_op jit(solution)/shard_map/ppermute | solution.py:485
  147.1 0.0 collective-permute-done.7.rest_6_
  147.1 2.6 %collective-permute-done.8.rest_7_ = f32[2,8,2048]{2,1,0:T(8,128)S(1)} collective-permute-done((f32[2,8,2048]{2,1,0:T(8,128)S(1)}, f32[2,8,2048]{2,1,0:T(8,128)S(1)}, u32[]{:S(2)}, u32[]{:S(2)}) %collective-permute-start.8) | collective-permute-done | bytes 131104 | tf_op jit(solution)/shard_map/ppermute | solution.py:485
  149.7 3.5 %all-to-all-done.2 = f32[32,8,1024]{2,1,0:T(8,128)S(1)} async-done(((f32[32,8,1024]{2,1,0:T(8,128)}), f32[32,8,1024]{2,1,0:T(8,128)S(1)}, u32[]{:S(2)}, u32[]{:S(2)}) %all-to-all-start.2) | async-done | bytes 1048608 | tf_op jit(solution)/shard_map/all_to_all | solution.py:552
  153.2 4.3 %shard_map.189 = (f32[2,64,2048]{2,1,0:T(8,128)}, f32[2,64,2048]{2,1,0:T(8,128)}, f32[8,64,256]{2,1,0:T(8,128)}) custom-call(s32[1]{0:T(128)} %bitcast.me_ref, f32[2]{0:T(128)S(1)} %add_multiply_fusion.weight_ref, f32[256,1024]{1,0:T(8,128)S(1)} %bitcast.22, f32[2,64,2048]{2,1,0:T(8,128)} %copy-done, f32[2,64,2048]{2,1,0:T(8,128)} %seis_hbm.1, ...), custom_call_target="tpu_custom_call" | custom-call | tf_op jit(solution)/shard_map/pallas_call | solution.py:464
  157.5 15.9 %all_to_all.20.part_ref = f32[8,64,256]{2,1,0:T(8,128)S(1)} all-to-all(f32[8,64,256]{2,1,0:T(8,128)} %get-tuple-element.36), channel_id=1, replica_groups=mesh['slab'=32,'depth'=8] {'depth'}, dimensions={0} | all-to-all | bytes 1048576 | tf_op jit(solution)/shard_map/all_to_all | solution.py:564
  173.3 0.7 shard_map.190
  (24 shorter events, 0.1 us)
Async XLA Ops:
  2.6 11.4 %collective-permute-start = (f32[2,2,8,2048]{3,2,1,0:T(8,128)S(1)}, f32[2,2,8,2048]{3,2,1,0:T(8,128)S(1)}, u32[]{:S(2)}, u32[]{:S(2)}) collective-permute-start(f32[2,2,8,2048]{3,2,1,0:T(8,128)S(1)} %pad_maximum_fusion), channel_id=1, source_target_pairs={{0,8},{8,16},{16,24},{24,32},{32,40},{40,48},{48,56},{56,64},{64,7... | collective-permute-start | bytes 786440 | tf_op jit(solution)/shard_map/ppermute | solution.py:481
  4.6 9.5 %collective-permute-start.1 = (f32[2,2,8,2048]{3,2,1,0:T(8,128)S(1)}, f32[2,2,8,2048]{3,2,1,0:T(8,128)S(1)}, u32[]{:S(2)}, u32[]{:S(2)}) collective-permute-start(f32[2,2,8,2048]{3,2,1,0:T(8,128)S(1)} %pad_maximum_fusion.1), channel_id=1, source_target_pairs={{8,0},{16,8},{24,16},{32,24},{40,32},{48,40},{56,48},{64,56},{72,6... | collective-permute-start | bytes 786440 | tf_op jit(solution)/shard_map/ppermute | solution.py:481
  13.0 1.0 copy-start
  16.6 6.2 %copy-start.4 = (s32[512,3]{0,1:T(4,128)S(1)}, s32[512,3]{0,1:T(4,128)}, u32[]{:S(2)}) copy-start(s32[512,3]{0,1:T(4,128)} %param.21) | copy-start | bytes 18436
  16.6 6.4 %copy-start.5 = (s32[2,512]{1,0:T(2,128)S(1)}, s32[2,512]{1,0:T(2,128)}, u32[]{:S(2)}) copy-start(s32[2,512]{1,0:T(2,128)} %param.22) | copy-start | bytes 12292
  16.6 47.1 %copy-start.2 = (f32[2,16,128]{2,1,0:T(8,128)S(1)}, f32[2,16,128]{2,1,0:T(8,128)}, u32[]{:S(2)}) copy-start(f32[2,16,128]{2,1,0:T(8,128)} %constant.69.clone.twist_ref) | copy-start | bytes 49156
  16.7 47.1 %all-to-all-start = ((f32[8,48,2048]{2,1,0:T(8,128)}), f32[8,48,2048]{2,1,0:T(8,128)S(1)}, u32[]{:S(2)}, u32[]{:S(2)}) async-start(f32[8,48,2048]{2,1,0:T(8,128)} %shard_map.185), calls=%async_computation | async-start | bytes 6291456 | tf_op jit(solution)/shard_map/all_to_all | solution.py:532
  72.0 41.3 %all-to-all-start.1 = ((f32[256,8,128]{2,1,0:T(8,128)}), f32[256,8,128]{2,1,0:T(8,128)S(1)}, u32[]{:S(2)}, u32[]{:S(2)}) async-start(f32[256,8,128]{2,1,0:T(8,128)} %bitcast.26), calls=%async_computation.1 | async-start | bytes 2097152 | tf_op jit(solution)/shard_map/all_to_all | solution.py:541
  92.3 21.0 %copy-start.3 = (f32[2,8,128]{2,1,0:T(8,128)S(1)}, f32[2,8,128]{2,1,0:T(8,128)}, u32[]{:S(2)}) copy-start(f32[2,8,128]{2,1,0:T(8,128)} %constant.71.clone.in_ref) | copy-start | bytes 24580
  113.3 10.8 %copy-start.12 = (f32[2,8,2048]{2,1,0:T(8,128)S(1)}, f32[2,8,2048]{2,1,0:T(8,128)}, u32[]{:S(2)}) copy-start(f32[2,8,2048]{2,1,0:T(8,128)} %get-tuple-element.27) | copy-start | bytes 393220
  113.3 12.5 %copy-start.11 = (f32[2,8,2048]{2,1,0:T(8,128)S(1)}, f32[2,8,2048]{2,1,0:T(8,128)}, u32[]{:S(2)}) copy-start(f32[2,8,2048]{2,1,0:T(8,128)} %get-tuple-element.28) | copy-start | bytes 393220
  113.3 13.2 %copy-start.10 = (f32[2,8,2048]{2,1,0:T(8,128)S(1)}, f32[2,8,2048]{2,1,0:T(8,128)}, u32[]{:S(2)}) copy-start(f32[2,8,2048]{2,1,0:T(8,128)} %get-tuple-element.29) | copy-start | bytes 393220
  113.3 16.0 %copy-start.9 = (f32[2,8,2048]{2,1,0:T(8,128)S(1)}, f32[2,8,2048]{2,1,0:T(8,128)}, u32[]{:S(2)}) copy-start(f32[2,8,2048]{2,1,0:T(8,128)} %get-tuple-element.30) | copy-start | bytes 393220
  113.3 18.8 %copy-start.8 = (f32[2,8,2048]{2,1,0:T(8,128)S(1)}, f32[2,8,2048]{2,1,0:T(8,128)}, u32[]{:S(2)}) copy-start(f32[2,8,2048]{2,1,0:T(8,128)} %get-tuple-element.31) | copy-start | bytes 393220
  113.3 25.6 %copy-start.7 = (f32[2,8,2048]{2,1,0:T(8,128)S(1)}, f32[2,8,2048]{2,1,0:T(8,128)}, u32[]{:S(2)}) copy-start(f32[2,8,2048]{2,1,0:T(8,128)} %get-tuple-element.32) | copy-start | bytes 393220
  113.3 25.6 %copy-start.6 = (f32[2,8,2048]{2,1,0:T(8,128)S(1)}, f32[2,8,2048]{2,1,0:T(8,128)}, u32[]{:S(2)}) copy-start(f32[2,8,2048]{2,1,0:T(8,128)} %get-tuple-element.33) | copy-start | bytes 393220
  113.4 39.8 %copy-start.1 = (f32[2,8,2048]{2,1,0:T(8,128)S(1)}, f32[2,8,2048]{2,1,0:T(8,128)}, u32[]{:S(2)}) copy-start(f32[2,8,2048]{2,1,0:T(8,128)} %get-tuple-element.26.rest_0_) | copy-start | bytes 393220
  118.9 34.3 %all-to-all-start.2 = ((f32[32,8,1024]{2,1,0:T(8,128)}), f32[32,8,1024]{2,1,0:T(8,128)S(1)}, u32[]{:S(2)}, u32[]{:S(2)}) async-start(f32[32,8,1024]{2,1,0:T(8,128)} %bitcast.25), calls=%async_computation.2 | async-start | bytes 2097152 | tf_op jit(solution)/shard_map/all_to_all | solution.py:552
  124.1 14.7 %collective-permute-start.2 = (f32[2,8,2048]{2,1,0:T(8,128)S(1)}, f32[2,8,2048]{2,1,0:T(8,128)S(1)}, u32[]{:S(2)}, u32[]{:S(2)}) collective-permute-start(f32[2,8,2048]{2,1,0:T(8,128)S(1)} %copy-done.12), channel_id=1, source_target_pairs={{0,1},{1,2},{2,3},{3,4},{4,5},{5,6},{6,7},{7,0},{8,9},{9,10},{10,1... | collective-permute-start | bytes 393224 | tf_op jit(solution)/shard_map/ppermute | solution.py:485
  125.8 13.1 %collective-permute-start.3 = (f32[2,8,2048]{2,1,0:T(8,128)S(1)}, f32[2,8,2048]{2,1,0:T(8,128)S(1)}, u32[]{:S(2)}, u32[]{:S(2)}) collective-permute-start(f32[2,8,2048]{2,1,0:T(8,128)S(1)} %copy-done.11), channel_id=1, source_target_pairs={{0,2},{1,3},{2,4},{3,5},{4,6},{5,7},{6,0},{7,1},{8,10},{9,11},{10,... | collective-permute-start | bytes 393224 | tf_op jit(solution)/shard_map/ppermute | solution.py:485
  126.5 14.5 %collective-permute-start.4 = (f32[2,8,2048]{2,1,0:T(8,128)S(1)}, f32[2,8,2048]{2,1,0:T(8,128)S(1)}, u32[]{:S(2)}, u32[]{:S(2)}) collective-permute-start(f32[2,8,2048]{2,1,0:T(8,128)S(1)} %copy-done.10), channel_id=1, source_target_pairs={{0,3},{1,4},{2,5},{3,6},{4,7},{5,0},{6,1},{7,2},{8,11},{9,12},{10,... | collective-permute-start | bytes 393224 | tf_op jit(solution)/shard_map/ppermute | solution.py:485
  129.3 11.7 %collective-permute-start.5 = (f32[2,8,2048]{2,1,0:T(8,128)S(1)}, f32[2,8,2048]{2,1,0:T(8,128)S(1)}, u32[]{:S(2)}, u32[]{:S(2)}) collective-permute-start(f32[2,8,2048]{2,1,0:T(8,128)S(1)} %copy-done.9), channel_id=1, source_target_pairs={{0,4},{1,5},{2,6},{3,7},{4,0},{5,1},{6,2},{7,3},{8,12},{9,13},{10,... | collective-permute-start | bytes 393224 | tf_op jit(solution)/shard_map/ppermute | solution.py:485
  132.2 14.9 %collective-permute-start.6 = (f32[2,8,2048]{2,1,0:T(8,128)S(1)}, f32[2,8,2048]{2,1,0:T(8,128)S(1)}, u32[]{:S(2)}, u32[]{:S(2)}) collective-permute-start(f32[2,8,2048]{2,1,0:T(8,128)S(1)} %copy-done.8), channel_id=1, source_target_pairs={{0,5},{1,6},{2,7},{3,0},{4,1},{5,2},{6,3},{7,4},{8,13},{9,14},{10,... | collective-permute-start | bytes 393224 | tf_op jit(solution)/shard_map/ppermute | solution.py:485
  138.9 8.2 %collective-permute-start.7 = (f32[2,8,2048]{2,1,0:T(8,128)S(1)}, f32[2,8,2048]{2,1,0:T(8,128)S(1)}, u32[]{:S(2)}, u32[]{:S(2)}) collective-permute-start(f32[2,8,2048]{2,1,0:T(8,128)S(1)} %copy-done.7), channel_id=1, source_target_pairs={{0,6},{1,7},{2,0},{3,1},{4,2},{5,3},{6,4},{7,5},{8,14},{9,15},{10,... | collective-permute-start | bytes 393224 | tf_op jit(solution)/shard_map/ppermute | solution.py:485
  138.9 10.8 %collective-permute-start.8 = (f32[2,8,2048]{2,1,0:T(8,128)S(1)}, f32[2,8,2048]{2,1,0:T(8,128)S(1)}, u32[]{:S(2)}, u32[]{:S(2)}) collective-permute-start(f32[2,8,2048]{2,1,0:T(8,128)S(1)} %copy-done.6), channel_id=1, source_target_pairs={{0,7},{1,0},{2,1},{3,2},{4,3},{5,4},{6,5},{7,6},{8,15},{9,8},{10,9... | collective-permute-start | bytes 393224 | tf_op jit(solution)/shard_map/ppermute | solution.py:485

commit v3 on v2

--- a/solution.py
+++ b/solution.py
@@ -142,159 +142,220 @@
     return pl.ds(pl.multiple_of(d * 8, 8), 8)
 
 
-def lookup_kernel(root_ref, inv_ref, label_hbm, p_hbm, root_out, inv_out, p_out, label, sems):
-    copy = start(p_hbm, p_out, sems.at[8])
+def edge_kernel(perm_hbm, p_hbm, label_hbm, first_out, last_out, perm_ref, label, sems):
+    table = start(perm_hbm, perm_ref, sems.at[4])
+    first, last = slice(0, 8), slice(ROWS - 8, ROWS)
+    loads = [
+        start(label_hbm.at[:, first, :], label.at[0], sems.at[0]),
+        start(label_hbm.at[:, last, :], label.at[1], sems.at[1]),
+        start(p_hbm.at[:, first, :], first_out.at[0], sems.at[2]),
+        start(p_hbm.at[:, last, :], last_out.at[0], sems.at[3]),
+    ]
+    table.wait()
+    for copy in loads:
+        copy.wait()
+    width = 1024
+
+    def body(c, carry):
+        cols = pl.ds(pl.multiple_of(c * width, width), width)
+        for l in range(2):
+            first_out[1, l, :, cols] = jnp.sqrt(pick(label[0, l, :, cols], perm_ref, 3, 0))
+            last_out[1, l, :, cols] = jnp.sqrt(pick(label[1, l, :, cols], perm_ref, 3, 0))
+        return carry
+
+    lax.fori_loop(0, N // width, body, 0)
+
+
+def each_part(label_hbm, label, sems, work, done):
     loads = [start(label_hbm.at[:, rows_of(d), :], label.at[:, rows_of(d), :], sems.at[d]) for d in range(DEPTHS)]
-    width = 512
+    width = 1024
     for d in range(DEPTHS):
         loads[d].wait()
 
         def body(c, carry, d=d):
             cols = pl.ds(pl.multiple_of(c * width, width), width)
             for l in range(2):
-                zone = label[l, rows_of(d), cols]
-                root_out[l, rows_of(d), cols] = pick(zone, root_ref, 3, 0)
-                inv_out[l, rows_of(d), cols] = pick(zone, inv_ref, 3, 0)
+                work(label[l, rows_of(d), cols], (l, rows_of(d), cols))
             return carry
 
         lax.fori_loop(0, N // width, body, 0)
-    copy.wait()
-
-
-def wells_kernel(where1_ref, where2_ref, amount_ref, col_ref, out1_ref, out2_ref, buf, sems):
+        done(d)
+
+
+def lookup_kernel(perm_hbm, label_hbm, p_hbm, root_out, p_out, msg_hbm, perm_ref, label, sems, msg_sems):
+    table = start(perm_hbm, perm_ref, sems.at[8])
+    loads = [start(p_hbm.at[:, rows_of(d), :], p_out.at[:, rows_of(d), :], msg_sems.at[2, d]) for d in range(DEPTHS)]
+    copies = []
+
+    def work(zone, at):
+        root_out[at] = jnp.sqrt(pick(zone, perm_ref, 3, 0))
+
+    def done(d):
+        loads[d].wait()
+        copies.append(start(p_out.at[:, rows_of(d), :], msg_hbm.at[d, 0:2], msg_sems.at[1, d]))
+        copies.append(start(root_out.at[:, rows_of(d), :], msg_hbm.at[d, 3:5], msg_sems.at[0, d]))
+
+    table.wait()
+    each_part(label_hbm, label, sems, work, done)
+    for copy in copies:
+        copy.wait()
+
+
+def strength_kernel(asig_hbm, label_hbm, inv_hbm, asig_ref, label, inv, sems, inv_sems):
+    start(asig_hbm, asig_ref, sems.at[8]).wait()
+    copies = []
+
+    def work(zone, at):
+        inv[at] = 1.0 / pick(zone, asig_ref, 3, 0)
+
+    def done(d):
+        copies.append(start(inv.at[:, rows_of(d), :], inv_hbm.at[:, rows_of(d), :], inv_sems.at[d]))
+
+    each_part(label_hbm, label, sems, work, done)
+    for copy in copies:
+        copy.wait()
+
+
+def wells_kernel(where1_ref, where2_ref, amount_ref, col_ref, out1_ref, out2_ref, both, sems):
     def hits(where_ref, rows, s):
         row = lax.broadcasted_iota(jnp.int32, (rows, 512), 0)
         return jnp.where(row == where_ref[...], amount_ref[s : s + 1, :], 0.0).astype(BF16)
 
-    left = jnp.concatenate([hits(where1_ref, 256, 0), hits(where2_ref, 128, 1)], 0)
+    left = jnp.concatenate([hits(where1_ref, 192, 0), hits(where2_ref, 128, 1)], 0)
     col_of = jnp.broadcast_to(col_ref[...], (512, 256))
     for c in range(N // 256):
         at = slice(c * 256, (c + 1) * 256)
         col = lax.broadcasted_iota(jnp.int32, (512, 256), 1) + c * 256
-        buf[:, at] = matmul(left, jnp.where(col == col_of, 1.0, 0.0).astype(BF16))
-    copies = [start(buf.at[0:256, :], out1_ref, sems.at[0]), start(buf.at[256:384, :], out2_ref, sems.at[1])]
+        both[:, at] = matmul(left, jnp.where(col == col_of, 1.0, 0.0).astype(BF16))
+    copies = [start(both.at[0:192, :], out1_ref, sems.at[0]), start(both.at[192:320, :], out2_ref, sems.at[1])]
     for copy in copies:
         copy.wait()
 
 
-def pack_kernel(root_ref, p_ref, q_ref, before_ref, after_ref, out_hbm, edge_ref, out_ref, sems):
-    width = 512
-
-    def outside(c, carry):
-        cols = pl.ds(pl.multiple_of(c * width, width), width)
-        for i, ref in enumerate((before_ref, after_ref)):
-            for l in range(2):
-                zone = ref[1, l, :, cols].astype(jnp.int32)
-                edge_ref[i, l, :, cols] = jnp.where(zone > 0, pick(zone - 1, root_ref, 3, 0), 0.0)
-        return carry
-
-    lax.fori_loop(0, N // width, outside, 0)
+def pack_kernel(p_ref, q_ref, before_ref, after_ref, msg_hbm, out_hbm, side_ref, sems):
     row = lax.broadcasted_iota(jnp.int32, (8, N), 0)
     copies = []
     for d in range(DEPTHS):
         for v, ref in enumerate((p_ref, q_ref)):
             sides = []
             for l in range(2):
-                out_ref[d, v * 24 + l * 8 : v * 24 + l * 8 + 8, :] = ref[l, d * 8 : d * 8 + 8, :]
-                if d:
-                    prev = ref[l, d * 8 - 8 : d * 8, :]
-                else:
-                    prev = edge_ref[0, l] if v else before_ref[0, l]
-                if d < DEPTHS - 1:
-                    then = ref[l, d * 8 + 8 : d * 8 + 16, :]
-                else:
-                    then = edge_ref[1, l] if v else after_ref[0, l]
+                prev = ref[l, d * 8 - 8 : d * 8, :] if d else before_ref[v, l]
+                then = ref[l, d * 8 + 8 : d * 8 + 16, :] if d < DEPTHS - 1 else after_ref[v, l]
                 sides.append(jnp.where(row < 4, then, prev))
-            both = jnp.where((row < 2) | (row >= 6), sides[0], pltpu.roll(sides[1], 4, 0))
-            out_ref[d, v * 24 + 16 : v * 24 + 24, :] = both
-        copies.append(start(out_ref.at[d], out_hbm.at[d], sems.at[d]))
+            side_ref[d, v] = jnp.where((row < 2) | (row >= 6), sides[0], pltpu.roll(sides[1], 4, 0))
+            copies.append(start(side_ref.at[d, v], out_hbm.at[d, v * 3 + 2], sems.at[v, d]))
     for copy in copies:
         copy.wait()
 
 
-def sideways(value, col):
-    left = jnp.where(col == 0, 0.0, pltpu.roll(value, 1, 1))
-    right = jnp.where(col == N - 1, 0.0, pltpu.roll(value, N - 1, 1))
-    return left + right
-
-
-def around(main, side, row):
-    main_up, side_up = pltpu.roll(main, 1, 0), pltpu.roll(side, 1, 0)
-    main_down, side_down = pltpu.roll(main, 7, 0), pltpu.roll(side, 7, 0)
+class Tiles:
+    def __init__(self, load):
+        self.load, self.kept, self.turned = load, {}, {}
+
+    def __getitem__(self, c):
+        if c not in self.kept:
+            self.kept[c] = self.load(c)
+        return self.kept[c]
+
+    def roll(self, c, by):
+        if (c, by) not in self.turned:
+            self.turned[c, by] = pltpu.roll(self[c], by, 1)
+        return self.turned[c, by]
+
+    def beside(self, c, lane):
+        left = self.roll(c - 1, 1) if c else 0.0
+        right = self.roll(c + 1, 127) if c < TILES - 1 else 0.0
+        return jnp.where(lane == 0, left, self.roll(c, 1)) + jnp.where(lane == 127, right, self.roll(c, 127))
+
+
+def of_rows(main0, main1, side, row):
     first, last = row == 0, row == 7
-    of_main = jnp.where(first, side_up, main_up) + jnp.where(last, side_down, main_down)
-    of_side = jnp.where(first, main_up, side_up) + jnp.where(last, main_down, side_down)
-    return of_main, of_side
+    up0 = jnp.where(first, pltpu.roll(side, 1, 0), pltpu.roll(main0, 1, 0))
+    down0 = jnp.where(last, pltpu.roll(side, 7, 0), pltpu.roll(main0, 7, 0))
+    up1 = jnp.where(first, pltpu.roll(side, 5, 0), pltpu.roll(main1, 1, 0))
+    down1 = jnp.where(last, pltpu.roll(side, 3, 0), pltpu.roll(main1, 7, 0))
+    return up0 + down0, up1 + down1
+
+
+def of_side_rows(main0, main1, side, row):
+    up = jnp.where(row == 0, pltpu.roll(main0, 1, 0), jnp.where(row == 4, pltpu.roll(main1, 5, 0), pltpu.roll(side, 1, 0)))
+    down = jnp.where(row == 7, pltpu.roll(main0, 7, 0), jnp.where(row == 3, pltpu.roll(main1, 3, 0), pltpu.roll(side, 7, 0)))
+    return up + down
+
+
+def tile(c):
+    return slice(c * LANES, (c + 1) * LANES)
 
 
 def diffuse_kernel(me_ref, msg_ref, src1_hbm, src2_hbm, fwd_hbm, twist_ref, *rest):
     outs, spec_hbm = rest[:8], rest[8]
-    q_ref, u_ref, w_ref, p_ref, s_ref, mid_ref, new_ref, spec_out, src1_ref, src2_ref, fwd_ref, sems = rest[9:]
+    w_ref, p_ref, s_ref, mid_ref, new_ref, spec_out, src1_ref, src2_ref, fwd_ref, sems = rest[9:]
     me = me_ref[0]
-    src1_load = start(src1_hbm, src1_ref, sems.at[0, 0])
+    for d in range(DEPTHS):
+        start(src1_hbm.at[d], src1_ref.at[d], sems.at[3, d])
     src2_load = start(src2_hbm, src2_ref, sems.at[0, 1])
     fwd_load = start(fwd_hbm, fwd_ref, sems.at[0, 2])
-    zero = jnp.zeros((16, N), F32)
-    for ref in (q_ref, u_ref, w_ref):
-        ref[0] = zero
-        ref[17] = zero
-    row = lax.broadcasted_iota(jnp.int32, (8, N), 0)
-    col = lax.broadcasted_iota(jnp.int32, (8, N), 1)
-
-    def fill(d, carry):
-        p_side, q_side = msg_ref[d, 16:24, :], msg_ref[d, 40:48, :]
-        for l in range(2):
-            z = d * 2 + l + 1
-            q, p = msg_ref[d, 24 + l * 8 : 32 + l * 8, :], msg_ref[d, l * 8 : l * 8 + 8, :]
-            q_ref[z, 0:8, :] = q
-            u_ref[z, 0:8, :] = q * p
-            q = q_side if l == 0 else pltpu.roll(q_side, 4, 0)
-            p = p_side if l == 0 else pltpu.roll(p_side, 4, 0)
-            q_ref[z, 8:16, :] = q
-            u_ref[z, 8:16, :] = q * p
-            p_ref[z - 1, 8:16, :] = p
+    w_ref[0] = jnp.zeros((3, 8, N), F32)
+    w_ref[DEPTHS + 1] = jnp.zeros((3, 8, N), F32)
+    row = lax.broadcasted_iota(jnp.int32, (8, LANES), 0)
+    lane = lax.broadcasted_iota(jnp.int32, (8, LANES), 1)
+    of_second = (row >= 2) & (row < 6)
+
+    def first(d, carry):
+        below, above = jnp.maximum(d - 1, 0), jnp.minimum(d + 1, DEPTHS - 1)
+        has_below, has_above = (d > 0).astype(F32), (d < DEPTHS - 1).astype(F32)
+        pltpu.make_async_copy(src1_hbm.at[d], src1_ref.at[d], sems.at[3, d]).wait()
+        q = [Tiles(lambda c, i=i: msg_ref[d, 3 + i, :, tile(c)]) for i in range(3)]
+        p = [Tiles(lambda c, i=i: msg_ref[d, i, :, tile(c)]) for i in range(3)]
+        u = [Tiles(lambda c, i=i: q[i][c] * p[i][c]) for i in range(3)]
+        for c in range(TILES):
+            at = tile(c)
+            q_below = [msg_ref[below, 3 + i, :, at] * has_below for i in (1, 2)]
+            q_above = [msg_ref[above, 3 + i, :, at] * has_above for i in (0, 2)]
+            u_below = [x * msg_ref[below, i, :, at] for x, i in zip(q_below, (1, 2))]
+            u_above = [x * msg_ref[above, i, :, at] for x, i in zip(q_above, (0, 2))]
+            sums = []
+            for own, low, high in ((q, q_below, q_above), (u, u_below, u_above)):
+                x0, x1, side = own[0][c], own[1][c], own[2][c]
+                sum0, sum1 = of_rows(x0, x1, side, row)
+                depth = pltpu.roll(side + jnp.where(of_second, low[1], high[1]), 4, 0)
+                sums.append((
+                    sum0 + own[0].beside(c, lane) + (low[0] + x1),
+                    sum1 + own[1].beside(c, lane) + (x0 + high[0]),
+                    of_side_rows(x0, x1, side, row) + own[2].beside(c, lane) + depth,
+                ))
+            for i in range(3):
+                s, t = sums[0][i], sums[1][i]
+                new = p[i][c] + (conduct * q[i][c]) * (t - p[i][c] * s) + src1_ref[d, i, :, at]
+                w_ref[d + 1, i, :, at] = q[i][c] * new
+                if i < 2:
+                    s_ref[d, i, :, at] = s
+                    p_ref[d, i, :, at] = new
         return carry
 
-    lax.fori_loop(0, DEPTHS, fill, 0)
-    src1_load.wait()
-
-    def first(z, carry):
-        q, q_side = q_ref[z + 1, 0:8, :], q_ref[z + 1, 8:16, :]
-        sums, sides = around(q, q_side, row)
-        s = sums + sideways(q, col) + (q_ref[z, 0:8, :] + q_ref[z + 2, 0:8, :])
-        s_side = sides + sideways(q_side, col) + (q_ref[z, 8:16, :] + q_ref[z + 2, 8:16, :])
-        u, u_side = u_ref[z + 1, 0:8, :], u_ref[z + 1, 8:16, :]
-        sums, sides = around(u, u_side, row)
-        t = sums + sideways(u, col) + (u_ref[z, 0:8, :] + u_ref[z + 2, 0:8, :])
-        t_side = sides + sideways(u_side, col) + (u_ref[z, 8:16, :] + u_ref[z + 2, 8:16, :])
-        at = pl.ds(pl.multiple_of(z * 16, 16), 8)
-        side_at = pl.ds(pl.multiple_of(z * 16 + 8, 8), 8)
-        p = msg_ref[z // 2, pl.ds(pl.multiple_of(z % 2 * 8, 8), 8), :]
-        new = p + (conduct * q) * (t - p * s) + src1_ref[at, :]
-        p_side = p_ref[z, 8:16, :]
-        new_side = p_side + (conduct * q_side) * (t_side - p_side * s_side) + src1_ref[side_at, :]
-        s_ref[z] = s
-        p_ref[z, 0:8, :] = new
-        w_ref[z + 1, 0:8, :] = q * new
-        w_ref[z + 1, 8:16, :] = q_side * new_side
+    lax.fori_loop(0, DEPTHS, first, 0)
+    src2_load.wait()
+
+    def second(n, carry):
+        k = lax.rem(n + 1, DEPTHS)
+        d = lax.rem(me + k, DEPTHS)
+        w = [Tiles(lambda c, i=i: w_ref[d + 1, i, :, tile(c)]) for i in range(3)]
+        for c in range(TILES):
+            at = tile(c)
+            x0, x1 = w[0][c], w[1][c]
+            sum0, sum1 = of_rows(x0, x1, w[2][c], row)
+            t0 = sum0 + w[0].beside(c, lane) + (w_ref[d, 1, :, at] + x1)
+            t1 = sum1 + w[1].beside(c, lane) + (x0 + w_ref[d + 2, 0, :, at])
+            for l, t in ((0, t0), (1, t1)):
+                p = p_ref[d, l, :, at]
+                new_ref[k, l, :, at] = (
+                    p + (conduct * msg_ref[d, 3 + l, :, at]) * (t - p * s_ref[d, l, :, at]) + src2_ref[d, l, :, at]
+                )
+        spectrum_of_rows(new_ref.at[k], twist_ref, mid_ref, d)
         return carry
 
-    lax.fori_loop(0, 2 * DEPTHS, first, 0)
-
-    src2_load.wait()
-    copies = []
-    for k in (1, 2, 3, 4, 5, 6, 7, 0):
-        d = lax.rem(me + k, DEPTHS)
-        for l in range(2):
-            z = d * 2 + l
-            w = w_ref[z + 1, 0:8, :]
-            sums, _ = around(w, w_ref[z + 1, 8:16, :], row)
-            t = sums + sideways(w, col) + (w_ref[z, 0:8, :] + w_ref[z + 2, 0:8, :])
-            p = p_ref[z, 0:8, :]
-            new = p + (conduct * q_ref[z + 1, 0:8, :]) * (t - p * s_ref[z]) + src2_ref[rows_of(z), :]
-            new_ref[k, l] = new
-        copies.append(start(new_ref.at[k], outs[k], sems.at[1, k]))
-        spectrum_of_rows(new_ref.at[k], twist_ref, mid_ref, d)
+    lax.fori_loop(0, DEPTHS, second, 0)
+    copies = [start(new_ref.at[k], outs[k], sems.at[1, k]) for k in range(DEPTHS)]
     fwd_load.wait()
     for c in range(4):
         part = triple(mid_ref[c * 256 : (c + 1) * 256, :], 1)
@@ -459,7 +520,7 @@
 DMA = pltpu.SemaphoreType.DMA
 
 
-def call(kernel, mib, args, outs, scratch=()):
+def call(kernel, mib, args, outs, scratch=(), aliases={}):
     values = [pltpu.with_memory_space_constraint(value, space) if space is HBM else value for space, value in args]
     return pl.pallas_call(
         kernel,
@@ -467,6 +528,7 @@
         in_specs=[pl.BlockSpec(memory_space=space) for space, _ in args],
         out_specs=[pl.BlockSpec(memory_space=space) for space, _ in outs],
         scratch_shapes=scratch,
+        input_output_aliases=aliases,
         compiler_params=pltpu.CompilerParams(vmem_limit_bytes=mib * 1024 * 1024),
     )(*values)
 
@@ -492,31 +554,43 @@
     me = (SMEM, depth.reshape(1))
     rows, block = (2, 8, N), (2, ROWS, N)
 
-    def edge(at):
-        return jnp.stack([pressure[:, at], (zone_labels[:, at] + 1).astype(F32)])
-
-    before, after = shift(edge(slice(ROWS - 8, ROWS)), "slab", 1), shift(edge(slice(0, 8)), "slab", -1)
-    root_table = (SMEM, jnp.sqrt(perm_table))
-    root, inv, p_copy = call(
+    table = pltpu.SMEM((perm_table.shape[0],), F32)
+    first, last = call(
+        edge_kernel,
+        4,
+        ((HBM, perm_table), (HBM, pressure), (HBM, zone_labels)),
+        [(VMEM, (2,) + rows)] * 2,
+        [table, buf(2, *rows, dtype=jnp.int32), DMA((5,))],
+    )
+    before, after = shift(last, "slab", 1), shift(first, "slab", -1)
+    root, p_copy, msg = call(
         lookup_kernel,
-        12,
-        (root_table, (SMEM, 1.0 / asig_table), (HBM, zone_labels), (HBM, pressure)),
-        [(VMEM, block)] * 3,
-        [buf(*block, dtype=jnp.int32), DMA((9,))],
-    )
-
-    offset = well_cells[:, 1] - (slab * ROWS + depth * 8)
+        8,
+        ((HBM, perm_table), (HBM, zone_labels), (HBM, pressure)),
+        [(VMEM, block)] * 2 + [(HBM, (DEPTHS, 6, 8, N))],
+        [table, buf(*block, dtype=jnp.int32), DMA((9,)), DMA((3, 8))],
+    )
+    (inv,) = call(
+        strength_kernel,
+        8,
+        ((HBM, asig_table), (HBM, zone_labels)),
+        [(HBM, block)],
+        [table, buf(*block, dtype=jnp.int32), buf(*block), DMA((9,)), DMA((8,))],
+    )
+
+    layer, offset = well_cells[:, 0], well_cells[:, 1] - (slab * ROWS + depth * 8)
+    own = (offset >= 0) & (offset < 8)
     near = (offset >= -2) & (offset < 10)
-    spot1 = jnp.where(near, well_cells[:, 0] * 16 + (offset & 15), -1)[None, :]
-    own = (offset >= 0) & (offset < 8)
-    spot2 = jnp.where(own, well_cells[:, 0] * 8 + offset, -1)[None, :]
+    inner = jnp.where(own, layer % 2 * 8 + offset, 16 + (offset + layer % 2 * 4) % 8)
+    spot1 = jnp.where(near, layer // 2 * 24 + inner, -1)[None, :]
+    spot2 = jnp.where(own, layer * 8 + offset, -1)[None, :]
     amounts = rate_unit * rate_levels.astype(F32)
     src1, src2 = call(
         wells_kernel,
         12,
         ((VMEM, spot1), (VMEM, spot2), (VMEM, amounts), (VMEM, well_cells[:, 2:3])),
-        [(HBM, (256, N)), (HBM, (128, N))],
-        [buf(384, N), DMA((2,))],
+        [(HBM, (192, N)), (HBM, (128, N))],
+        [buf(320, N), DMA((2,))],
     )
 
     green = (green_spectrum * (1.0 / (N * N))).reshape(8, 8, SLABS, FREQS, TILES)
@@ -524,19 +598,21 @@
 
     (msg,) = call(
         pack_kernel,
-        16,
-        (root_table, (VMEM, p_copy), (VMEM, root), (VMEM, before), (VMEM, after)),
-        [(HBM, (DEPTHS, 48, N))],
-        [buf(2, *rows), buf(DEPTHS, 48, N), DMA((8,))],
+        8,
+        ((VMEM, p_copy), (VMEM, root), (VMEM, before), (VMEM, after), (HBM, msg)),
+        [(HBM, (DEPTHS, 6, 8, N))],
+        [buf(DEPTHS, *rows), DMA((2, 8))],
+        {4: 0},
     )
     msg = lax.all_to_all(msg, "depth", 0, 0, tiled=True)
     *parts, spec = call(
         diffuse_kernel,
-        30,
-        (me, (VMEM, msg), (HBM, src1), (HBM, src2), (HBM, tab["fwd"]), (VMEM, tab["row_twist"])),
+        24,
+        (me, (VMEM, msg), (HBM, src1.reshape(DEPTHS, 3, 8, N)), (HBM, src2.reshape(DEPTHS, 2, 8, N)), (HBM, tab["fwd"]),
+         (VMEM, tab["row_twist"])),
         [(HBM, rows)] * DEPTHS + [(HBM, (SLABS, DEPTHS, 8, LANES))],
-        [buf(18, 16, N), buf(18, 16, N), buf(18, 16, N), buf(16, 16, N), buf(16, 8, N), buf(1024, 256),
-         buf(8, *rows), buf(SLABS, DEPTHS, 8, LANES), buf(256, N), buf(128, N), buf(256, 768, dtype=BF16), DMA((3, 8))],
+        [buf(DEPTHS + 2, 3, 8, N), buf(DEPTHS, *rows), buf(DEPTHS, *rows), buf(1024, 256), buf(DEPTHS, *rows),
+         buf(SLABS, DEPTHS, 8, LANES), buf(DEPTHS, 3, 8, N), buf(DEPTHS, *rows), buf(256, 768, dtype=BF16), DMA((4, 8))],
     )
     spec = lax.all_to_all(spec.reshape(SLABS * DEPTHS, 8, LANES), ("slab", "depth"), 0, 0, tiled=True)
     parts = rotate(parts)

time: 175 us -> 171 us (0.977)
  waiting for transfers between devices: 70.6 us -> 65.7 us
  starting transfers between devices: 39.3 us -> 43 us
  local copies, waits for them, and re-layouts: 16.3 us -> 13.7 us
  Pallas kernels: 27.4 us -> 29.4 us
    all_to_all x1, starting transfers between devices: 11.3 us -> 14.9 us  [shards(): lax.all_to_all(spec.reshape(SLABS * DEPTHS, 8, LANES), ('slab', 'depth'),...]
    ppermute x7, waiting for transfers between devices: 14.6 us -> 11.2 us  [rotate(): lax.ppermute(v, 'depth', [(i, (i + k) % DEPTHS) for i in range(DEPTHS)])]
    pallas_call x7 -> x9, Pallas kernels: 27.4 us -> 29.4 us  [call(): pl.pallas_call(kernel, out_shape=[HBM(shape, F32) if space is HBM else ve...]
  transfers between devices with their start and end apart: 12 -> 12, of which waited for: 7 -> 6; matrix products, arithmetic and copies ran while one was open for 10% -> 9% of each run, Pallas kernels for 4% -> 6%
where the time goes in v3:
time: 171 us; the launch traced here: 170 us
  waiting for transfers between devices  65.7 us (38%)
  starting transfers between devices  43 us (25%)
  Pallas kernels  29.4 us (17%)
  blocking collectives  15.9 us (9%)
  local copies, waits for them, and re-layouts  13.7 us (8%)
  other arithmetic  1.93 us (1%)
    all_to_all x1, waiting for transfers between devices, shards(): msg = lax.all_to_all(msg, 'depth', 0, 0, tiled=True)  36.4 us
    pallas_call x9, Pallas kernels, call(): pl.pallas_call(kernel, out_shape=[HBM(shape, F32) if space is HBM else ve...  29.4 us
    all_to_all x1, blocking collectives, shards(): rate = lax.all_to_all(rate, 'depth', 0, 0, tiled=True)  15.9 us
    all_to_all x1, starting transfers between devices, shards(): lax.all_to_all(spec.reshape(SLABS * DEPTHS, 8, LANES), ('slab', 'depth'),...  14.9 us
    all_to_all x1, waiting for transfers between devices, shards(): lax.all_to_all(spec.reshape(SLABS * DEPTHS, 8, LANES), ('slab', 'depth'),...  14.6 us
    ppermute x7, waiting for transfers between devices, rotate(): lax.ppermute(v, 'depth', [(i, (i + k) % DEPTHS) for i in range(DEPTHS)])  11.2 us
    ppermute x7, starting transfers between devices, rotate(): lax.ppermute(v, 'depth', [(i, (i + k) % DEPTHS) for i in range(DEPTHS)])  10.9 us
    reshape x2, local copies, waits for them, and re-layouts, shards(): (green_spectrum * (1.0 / (N * N))).reshape(8, 8, SLABS, FREQS, TILES)  7.07 us
  transfers between devices with their start and end apart: 12, of which 6 were waited for; matrix products, arithmetic and copies ran while one was open for 9% of the time, Pallas kernels for 6%

profile of v3, /device:TPU:2, one launch (start us, length us, event | category | flops | bytes accessed | tf_op | source)
XLA Modules:
  0.0 170.5 jit_solution(14983754478756660696)
XLA Ops:
  0.6 1.4 shard_map.185
  2.1 1.9 %collective-permute-start = (f32[2,2,8,2048]{3,2,1,0:T(8,128)S(1)}, f32[2,2,8,2048]{3,2,1,0:T(8,128)S(1)}, u32[]{:S(2)}, u32[]{:S(2)}) collective-permute-start(f32[2,2,8,2048]{3,2,1,0:T(8,128)S(1)} %get-tuple-element.24), channel_id=1, source_target_pairs={{0,8},{8,16},{16,24},{24,32},{32,40},{40,48},{48,56},{56,64},{64,7... | collective-permute-start | bytes 786440 | tf_op jit(solution)/shard_map/ppermute | solution.py:543
  4.0 3.6 %collective-permute-start.1 = (f32[2,2,8,2048]{3,2,1,0:T(8,128)S(1)}, f32[2,2,8,2048]{3,2,1,0:T(8,128)S(1)}, u32[]{:S(2)}, u32[]{:S(2)}) collective-permute-start(f32[2,2,8,2048]{3,2,1,0:T(8,128)S(1)} %get-tuple-element.25), channel_id=1, source_target_pairs={{8,0},{16,8},{24,16},{32,24},{40,32},{48,40},{56,48},{64,56},{72,6... | collective-permute-start | bytes 786440 | tf_op jit(solution)/shard_map/ppermute | solution.py:543
  7.6 4.0 %shard_map.184 = (f32[2,64,2048]{2,1,0:T(8,128)S(1)}, f32[2,64,2048]{2,1,0:T(8,128)S(1)}, f32[8,6,8,2048]{3,2,1,0:T(8,128)}) custom-call(f32[16]{0:T(128)} %perm_hbm.3, s32[2,64,2048]{2,1,0:T(8,128)} %label_hbm.5, f32[2,64,2048]{2,1,0:T(8,128)} %p_hbm.3), custom_call_target="tpu_custom_call" | custom-call | tf_op jit(solution)/shard_map/pallas_call | solution.py:525
  11.7 0.0 collective-permute-done.before_ref
  11.7 0.0 collective-permute-done.1.after_ref
  11.7 1.1 shard_map.186
  12.8 0.0 copy-start.3
  12.8 0.0 copy-start.4
  12.9 0.0 copy-start.1
  12.9 6.2 %all-to-all-start = ((f32[8,6,8,2048]{3,2,1,0:T(8,128)}), f32[8,6,8,2048]{3,2,1,0:T(8,128)S(1)}, u32[]{:S(2)}, u32[]{:S(2)}) async-start(f32[8,6,8,2048]{3,2,1,0:T(8,128)} %shard_map.186), calls=%async_computation | async-start | bytes 6291456 | tf_op jit(solution)/shard_map/all_to_all | solution.py:607
  19.1 0.1 copy.25.col_ref
  19.3 2.5 %shard_map.187 = (f32[192,2048]{1,0:T(8,128)}, f32[128,2048]{1,0:T(8,128)}) custom-call(s32[1,512]{1,0:T(1,128)S(1)} %get-tuple-element.42.where1_ref, s32[1,512]{1,0:T(1,128)S(1)} %get-tuple-element.41.where2_ref, f32[2,512]{1,0:T(2,128)S(1)} %convert_multiply_fusion.amount_ref, s32[512,1]{1,0:T(8,128)S(1)} %copy.25.col_ref), custom_call_target="tpu_custom_call" | custom-call | tf_op jit(solution)/shard_map/pallas_call | solution.py:525
  21.8 36.4 %all-to-all-done.msg_ref = f32[8,6,8,2048]{3,2,1,0:T(8,128)S(1)} async-done(((f32[8,6,8,2048]{3,2,1,0:T(8,128)}), f32[8,6,8,2048]{3,2,1,0:T(8,128)S(1)}, u32[]{:S(2)}, u32[]{:S(2)}) %all-to-all-start) | async-done | bytes 3145760 | tf_op jit(solution)/shard_map/all_to_all | solution.py:607
  58.2 0.0 copy-done.1
  58.2 6.5 %shard_map.188 = (f32[2,8,2048]{2,1,0:T(8,128)}, f32[2,8,2048]{2,1,0:T(8,128)}, f32[2,8,2048]{2,1,0:T(8,128)}, f32[2,8,2048]{2,1,0:T(8,128)}, f32[2,8,2048]{2,1,...) custom-call(s32[1]{0:T(128)} %bitcast.me_ref, ...), custom_call_target="tpu_custom_call" | custom-call | tf_op jit(solution)/shard_map/pallas_call | solution.py:525
  64.7 14.9 %all-to-all-start.1 = ((f32[256,8,128]{2,1,0:T(8,128)}), f32[256,8,128]{2,1,0:T(8,128)S(1)}, u32[]{:S(2)}, u32[]{:S(2)}) async-start(f32[256,8,128]{2,1,0:T(8,128)} %bitcast.52), calls=%async_computation.1 | async-start | bytes 2097152 | tf_op jit(solution)/shard_map/all_to_all | solution.py:617
  79.7 1.9 %broadcast_multiply_fusion = f32[2048,64]{0,1:T(8,128)} fusion(f32[2048,64]{0,1:T(8,128)} %param.23), kind=kLoop, calls=%fused_computation | loop fusion | flops 131072 | bytes 1048576 | tf_op jit(solution)/shard_map/mul | solution.py:596
  81.6 1.8 %reshape.243 = f32[8,8,32,4,16]{2,1,0,4,3:T(8,128)S(1)} reshape(f32[2048,64]{0,1:T(8,128)} %broadcast_multiply_fusion) | data formatting | bytes 1048576 | tf_op jit(solution)/shard_map/reshape | solution.py:596
  83.3 5.3 %copy.24 = f32[8,8,32,4,16]{0,4,3,2,1:T(8,128)} copy(f32[8,8,32,4,16]{2,1,0,4,3:T(8,128)S(1)} %reshape.243) | data formatting | bytes 1048576 | tf_op jit(solution)/shard_map/reshape | solution.py:596
  88.6 6.4 %reshape.244.green_ref = f32[8,128,128]{2,1,0:T(8,128)S(1)} reshape(f32[8,32,4,16,8]{4,3,2,1,0:T(8,128)} %bitcast.48) | data formatting | bytes 1048576 | tf_op jit(solution)/shard_map/reshape | solution.py:597
  95.0 14.6 %all-to-all-done.1 = f32[256,8,128]{2,1,0:T(8,128)S(1)} async-done(((f32[256,8,128]{2,1,0:T(8,128)}), f32[256,8,128]{2,1,0:T(8,128)S(1)}, u32[]{:S(2)}, u32[]{:S(2)}) %all-to-all-start.1) | async-done | bytes 1048608 | tf_op jit(solution)/shard_map/all_to_all | solution.py:617
  109.7 0.0 copy-start.8
  109.7 0.0 copy-start.7
  109.7 0.0 copy-start.6
  109.7 0.0 copy-start.5
  109.7 5.5 %shard_map.189 = f32[256,1024]{1,0:T(8,128)} custom-call(f32[32,8,8,128]{3,2,1,0:T(8,128)S(1)} %bitcast.47, f32[8,128,128]{2,1,0:T(8,128)S(1)} %reshape.244.green_ref, bf16[256,768]{1,0:T(8,128)(2,1)} %constant.98.clone.mid_hbm, bf16[256,768]{1,0:T(8,128)(2,1)} %constant.99.clone.mid_inv_hbm, bf16[768,256]{1,0:T(8,128)(2,1)} %constant.100.clone.inner_hbm, ...), custom_call_target="tpu_custom_call" | custom-call | tf_op jit(solution)/shard_map/pallas_call | solution.py:525
  115.2 5.4 %all-to-all-start.2 = ((f32[32,8,1024]{2,1,0:T(8,128)}), f32[32,8,1024]{2,1,0:T(8,128)S(1)}, u32[]{:S(2)}, u32[]{:S(2)}) async-start(f32[32,8,1024]{2,1,0:T(8,128)} %bitcast.49), calls=%async_computation.2 | async-start | bytes 2097152 | tf_op jit(solution)/shard_map/all_to_all | solution.py:628
  120.6 0.0 copy-done.11
  120.6 1.6 collective-permute-start.2
  122.2 0.7 collective-permute-start.3
  123.0 2.8 %collective-permute-start.4 = (f32[2,8,2048]{2,1,0:T(8,128)S(1)}, f32[2,8,2048]{2,1,0:T(8,128)S(1)}, u32[]{:S(2)}, u32[]{:S(2)}) collective-permute-start(f32[2,8,2048]{2,1,0:T(8,128)S(1)} %copy-done.9), channel_id=1, source_target_pairs={{0,3},{1,4},{2,5},{3,6},{4,7},{5,0},{6,1},{7,2},{8,11},{9,12},{10,... | collective-permute-start | bytes 393224 | tf_op jit(solution)/shard_map/ppermute | solution.py:547
  125.8 2.8 %collective-permute-start.5 = (f32[2,8,2048]{2,1,0:T(8,128)S(1)}, f32[2,8,2048]{2,1,0:T(8,128)S(1)}, u32[]{:S(2)}, u32[]{:S(2)}) collective-permute-start(f32[2,8,2048]{2,1,0:T(8,128)S(1)} %copy-done.8), channel_id=1, source_target_pairs={{0,4},{1,5},{2,6},{3,7},{4,0},{5,1},{6,2},{7,3},{8,12},{9,13},{10,... | collective-permute-start | bytes 393224 | tf_op jit(solution)/shard_map/ppermute | solution.py:547
  128.6 2.8 %collective-permute-start.6 = (f32[2,8,2048]{2,1,0:T(8,128)S(1)}, f32[2,8,2048]{2,1,0:T(8,128)S(1)}, u32[]{:S(2)}, u32[]{:S(2)}) collective-permute-start(f32[2,8,2048]{2,1,0:T(8,128)S(1)} %copy-done.7), channel_id=1, source_target_pairs={{0,5},{1,6},{2,7},{3,0},{4,1},{5,2},{6,3},{7,4},{8,13},{9,14},{10,... | collective-permute-start | bytes 393224 | tf_op jit(solution)/shard_map/ppermute | solution.py:547
  131.5 3.9 %collective-permute-done.2.rest_1_ = f32[2,8,2048]{2,1,0:T(8,128)S(1)} collective-permute-done((f32[2,8,2048]{2,1,0:T(8,128)S(1)}, f32[2,8,2048]{2,1,0:T(8,128)S(1)}, u32[]{:S(2)}, u32[]{:S(2)}) %collective-permute-start.2) | collective-permute-done | bytes 131104 | tf_op jit(solution)/shard_map/ppermute | solution.py:547
  135.4 0.0 collective-permute-start.7
  135.4 0.0 collective-permute-done.3.rest_2_
  135.4 0.1 collective-permute-start.8
  135.5 3.4 %shard_map.190.inv_hbm = f32[2,64,2048]{2,1,0:T(8,128)} custom-call(f32[16]{0:T(128)} %asig_hbm.1, s32[2,64,2048]{2,1,0:T(8,128)} %label_hbm.5), custom_call_target="tpu_custom_call" | custom-call | tf_op jit(solution)/shard_map/pallas_call | solution.py:525
  138.9 0.0 collective-permute-done.4.rest_3_
  138.9 0.0 collective-permute-done.5.rest_4_
  138.9 4.7 %collective-permute-done.6.rest_5_ = f32[2,8,2048]{2,1,0:T(8,128)S(1)} collective-permute-done((f32[2,8,2048]{2,1,0:T(8,128)S(1)}, f32[2,8,2048]{2,1,0:T(8,128)S(1)}, u32[]{:S(2)}, u32[]{:S(2)}) %collective-permute-start.6) | collective-permute-done | bytes 131104 | tf_op jit(solution)/shard_map/ppermute | solution.py:547
  143.6 0.0 collective-permute-done.7.rest_6_
  143.6 2.6 %collective-permute-done.8.rest_7_ = f32[2,8,2048]{2,1,0:T(8,128)S(1)} collective-permute-done((f32[2,8,2048]{2,1,0:T(8,128)S(1)}, f32[2,8,2048]{2,1,0:T(8,128)S(1)}, u32[]{:S(2)}, u32[]{:S(2)}) %collective-permute-start.8) | collective-permute-done | bytes 131104 | tf_op jit(solution)/shard_map/ppermute | solution.py:547
  146.2 3.5 %all-to-all-done.2 = f32[32,8,1024]{2,1,0:T(8,128)S(1)} async-done(((f32[32,8,1024]{2,1,0:T(8,128)}), f32[32,8,1024]{2,1,0:T(8,128)S(1)}, u32[]{:S(2)}, u32[]{:S(2)}) %all-to-all-start.2) | async-done | bytes 1048608 | tf_op jit(solution)/shard_map/all_to_all | solution.py:628
  149.6 4.3 %shard_map.191 = (f32[2,64,2048]{2,1,0:T(8,128)}, f32[2,64,2048]{2,1,0:T(8,128)}, f32[8,64,256]{2,1,0:T(8,128)}) custom-call(s32[1]{0:T(128)} %bitcast.me_ref, f32[2]{0:T(128)S(1)} %add_multiply_fusion.weight_ref, f32[256,1024]{1,0:T(8,128)S(1)} %bitcast.46, f32[2,64,2048]{2,1,0:T(8,128)} %shard_map.190.inv_hbm, f32[2,64,2048]{2,1,0:T(8,128)} %seis_hbm.1, ...), custom_call_target="tpu_custom_call" | custom-call | tf_op jit(solution)/shard_map/pallas_call | solution.py:525
  153.9 15.9 %all_to_all.20.part_ref = f32[8,64,256]{2,1,0:T(8,128)S(1)} all-to-all(f32[8,64,256]{2,1,0:T(8,128)} %get-tuple-element.40), channel_id=1, replica_groups=mesh['slab'=32,'depth'=8] {'depth'}, dimensions={0} | all-to-all | bytes 1048576 | tf_op jit(solution)/shard_map/all_to_all | solution.py:640
  169.8 0.7 shard_map.192
  (19 shorter events, 0.1 us)
Async XLA Ops:
  2.1 9.6 %collective-permute-start = (f32[2,2,8,2048]{3,2,1,0:T(8,128)S(1)}, f32[2,2,8,2048]{3,2,1,0:T(8,128)S(1)}, u32[]{:S(2)}, u32[]{:S(2)}) collective-permute-start(f32[2,2,8,2048]{3,2,1,0:T(8,128)S(1)} %get-tuple-element.24), channel_id=1, source_target_pairs={{0,8},{8,16},{16,24},{24,32},{32,40},{40,48},{48,56},{56,64},{64,7... | collective-permute-start | bytes 786440 | tf_op jit(solution)/shard_map/ppermute | solution.py:543
  4.0 7.7 %collective-permute-start.1 = (f32[2,2,8,2048]{3,2,1,0:T(8,128)S(1)}, f32[2,2,8,2048]{3,2,1,0:T(8,128)S(1)}, u32[]{:S(2)}, u32[]{:S(2)}) collective-permute-start(f32[2,2,8,2048]{3,2,1,0:T(8,128)S(1)} %get-tuple-element.25), channel_id=1, source_target_pairs={{8,0},{16,8},{24,16},{32,24},{40,32},{48,40},{56,48},{64,56},{72,6... | collective-permute-start | bytes 786440 | tf_op jit(solution)/shard_map/ppermute | solution.py:543
  12.8 6.2 %copy-start.3 = (s32[512,3]{0,1:T(4,128)S(1)}, s32[512,3]{0,1:T(4,128)}, u32[]{:S(2)}) copy-start(s32[512,3]{0,1:T(4,128)} %param.21) | copy-start | bytes 18436
  12.8 6.4 %copy-start.4 = (s32[2,512]{1,0:T(2,128)S(1)}, s32[2,512]{1,0:T(2,128)}, u32[]{:S(2)}) copy-start(s32[2,512]{1,0:T(2,128)} %param.22) | copy-start | bytes 12292
  12.9 45.3 %copy-start.1 = (f32[2,16,128]{2,1,0:T(8,128)S(1)}, f32[2,16,128]{2,1,0:T(8,128)}, u32[]{:S(2)}) copy-start(f32[2,16,128]{2,1,0:T(8,128)} %constant.102.clone.twist_ref) | copy-start | bytes 49156
  12.9 45.3 %all-to-all-start = ((f32[8,6,8,2048]{3,2,1,0:T(8,128)}), f32[8,6,8,2048]{3,2,1,0:T(8,128)S(1)}, u32[]{:S(2)}, u32[]{:S(2)}) async-start(f32[8,6,8,2048]{3,2,1,0:T(8,128)} %shard_map.186), calls=%async_computation | async-start | bytes 6291456 | tf_op jit(solution)/shard_map/all_to_all | solution.py:607
  64.7 44.9 %all-to-all-start.1 = ((f32[256,8,128]{2,1,0:T(8,128)}), f32[256,8,128]{2,1,0:T(8,128)S(1)}, u32[]{:S(2)}, u32[]{:S(2)}) async-start(f32[256,8,128]{2,1,0:T(8,128)} %bitcast.52), calls=%async_computation.1 | async-start | bytes 2097152 | tf_op jit(solution)/shard_map/all_to_all | solution.py:617
  88.6 21.0 %copy-start.2 = (f32[2,8,128]{2,1,0:T(8,128)S(1)}, f32[2,8,128]{2,1,0:T(8,128)}, u32[]{:S(2)}) copy-start(f32[2,8,128]{2,1,0:T(8,128)} %constant.104.clone.in_ref) | copy-start | bytes 24580
  109.7 11.0 %copy-start.11 = (f32[2,8,2048]{2,1,0:T(8,128)S(1)}, f32[2,8,2048]{2,1,0:T(8,128)}, u32[]{:S(2)}) copy-start(f32[2,8,2048]{2,1,0:T(8,128)} %get-tuple-element.31) | copy-start | bytes 393220
  109.7 12.6 %copy-start.10 = (f32[2,8,2048]{2,1,0:T(8,128)S(1)}, f32[2,8,2048]{2,1,0:T(8,128)}, u32[]{:S(2)}) copy-start(f32[2,8,2048]{2,1,0:T(8,128)} %get-tuple-element.32) | copy-start | bytes 393220
  109.7 13.3 %copy-start.9 = (f32[2,8,2048]{2,1,0:T(8,128)S(1)}, f32[2,8,2048]{2,1,0:T(8,128)}, u32[]{:S(2)}) copy-start(f32[2,8,2048]{2,1,0:T(8,128)} %get-tuple-element.33) | copy-start | bytes 393220
  109.7 16.1 %copy-start.8 = (f32[2,8,2048]{2,1,0:T(8,128)S(1)}, f32[2,8,2048]{2,1,0:T(8,128)}, u32[]{:S(2)}) copy-start(f32[2,8,2048]{2,1,0:T(8,128)} %get-tuple-element.34) | copy-start | bytes 393220
  109.7 19.0 %copy-start.7 = (f32[2,8,2048]{2,1,0:T(8,128)S(1)}, f32[2,8,2048]{2,1,0:T(8,128)}, u32[]{:S(2)}) copy-start(f32[2,8,2048]{2,1,0:T(8,128)} %get-tuple-element.35) | copy-start | bytes 393220
  109.7 25.7 %copy-start.6 = (f32[2,8,2048]{2,1,0:T(8,128)S(1)}, f32[2,8,2048]{2,1,0:T(8,128)}, u32[]{:S(2)}) copy-start(f32[2,8,2048]{2,1,0:T(8,128)} %get-tuple-element.36) | copy-start | bytes 393220
  109.7 25.7 %copy-start.5 = (f32[2,8,2048]{2,1,0:T(8,128)S(1)}, f32[2,8,2048]{2,1,0:T(8,128)}, u32[]{:S(2)}) copy-start(f32[2,8,2048]{2,1,0:T(8,128)} %get-tuple-element.37) | copy-start | bytes 393220
  115.2 34.4 %copy-start = (f32[2,8,2048]{2,1,0:T(8,128)S(1)}, f32[2,8,2048]{2,1,0:T(8,128)}, u32[]{:S(2)}) copy-start(f32[2,8,2048]{2,1,0:T(8,128)} %get-tuple-element.30.rest_0_) | copy-start | bytes 393220
  115.2 34.4 %all-to-all-start.2 = ((f32[32,8,1024]{2,1,0:T(8,128)}), f32[32,8,1024]{2,1,0:T(8,128)S(1)}, u32[]{:S(2)}, u32[]{:S(2)}) async-start(f32[32,8,1024]{2,1,0:T(8,128)} %bitcast.49), calls=%async_computation.2 | async-start | bytes 2097152 | tf_op jit(solution)/shard_map/all_to_all | solution.py:628
  120.6 14.7 %collective-permute-start.2 = (f32[2,8,2048]{2,1,0:T(8,128)S(1)}, f32[2,8,2048]{2,1,0:T(8,128)S(1)}, u32[]{:S(2)}, u32[]{:S(2)}) collective-permute-start(f32[2,8,2048]{2,1,0:T(8,128)S(1)} %copy-done.11), channel_id=1, source_target_pairs={{0,1},{1,2},{2,3},{3,4},{4,5},{5,6},{6,7},{7,0},{8,9},{9,10},{10,1... | collective-permute-start | bytes 393224 | tf_op jit(solution)/shard_map/ppermute | solution.py:547
  122.2 13.1 %collective-permute-start.3 = (f32[2,8,2048]{2,1,0:T(8,128)S(1)}, f32[2,8,2048]{2,1,0:T(8,128)S(1)}, u32[]{:S(2)}, u32[]{:S(2)}) collective-permute-start(f32[2,8,2048]{2,1,0:T(8,128)S(1)} %copy-done.10), channel_id=1, source_target_pairs={{0,2},{1,3},{2,4},{3,5},{4,6},{5,7},{6,0},{7,1},{8,10},{9,11},{10,... | collective-permute-start | bytes 393224 | tf_op jit(solution)/shard_map/ppermute | solution.py:547
  123.0 15.9 %collective-permute-start.4 = (f32[2,8,2048]{2,1,0:T(8,128)S(1)}, f32[2,8,2048]{2,1,0:T(8,128)S(1)}, u32[]{:S(2)}, u32[]{:S(2)}) collective-permute-start(f32[2,8,2048]{2,1,0:T(8,128)S(1)} %copy-done.9), channel_id=1, source_target_pairs={{0,3},{1,4},{2,5},{3,6},{4,7},{5,0},{6,1},{7,2},{8,11},{9,12},{10,... | collective-permute-start | bytes 393224 | tf_op jit(solution)/shard_map/ppermute | solution.py:547
  125.8 13.1 %collective-permute-start.5 = (f32[2,8,2048]{2,1,0:T(8,128)S(1)}, f32[2,8,2048]{2,1,0:T(8,128)S(1)}, u32[]{:S(2)}, u32[]{:S(2)}) collective-permute-start(f32[2,8,2048]{2,1,0:T(8,128)S(1)} %copy-done.8), channel_id=1, source_target_pairs={{0,4},{1,5},{2,6},{3,7},{4,0},{5,1},{6,2},{7,3},{8,12},{9,13},{10,... | collective-permute-start | bytes 393224 | tf_op jit(solution)/shard_map/ppermute | solution.py:547
  128.6 15.0 %collective-permute-start.6 = (f32[2,8,2048]{2,1,0:T(8,128)S(1)}, f32[2,8,2048]{2,1,0:T(8,128)S(1)}, u32[]{:S(2)}, u32[]{:S(2)}) collective-permute-start(f32[2,8,2048]{2,1,0:T(8,128)S(1)} %copy-done.7), channel_id=1, source_target_pairs={{0,5},{1,6},{2,7},{3,0},{4,1},{5,2},{6,3},{7,4},{8,13},{9,14},{10,... | collective-permute-start | bytes 393224 | tf_op jit(solution)/shard_map/ppermute | solution.py:547
  135.4 8.2 %collective-permute-start.7 = (f32[2,8,2048]{2,1,0:T(8,128)S(1)}, f32[2,8,2048]{2,1,0:T(8,128)S(1)}, u32[]{:S(2)}, u32[]{:S(2)}) collective-permute-start(f32[2,8,2048]{2,1,0:T(8,128)S(1)} %copy-done.6), channel_id=1, source_target_pairs={{0,6},{1,7},{2,0},{3,1},{4,2},{5,3},{6,4},{7,5},{8,14},{9,15},{10,... | collective-permute-start | bytes 393224 | tf_op jit(solution)/shard_map/ppermute | solution.py:547
  135.4 10.8 %collective-permute-start.8 = (f32[2,8,2048]{2,1,0:T(8,128)S(1)}, f32[2,8,2048]{2,1,0:T(8,128)S(1)}, u32[]{:S(2)}, u32[]{:S(2)}) collective-permute-start(f32[2,8,2048]{2,1,0:T(8,128)S(1)} %copy-done.5), channel_id=1, source_target_pairs={{0,7},{1,0},{2,1},{3,2},{4,3},{5,4},{6,5},{7,6},{8,15},{9,8},{10,9... | collective-permute-start | bytes 393224 | tf_op jit(solution)/shard_map/ppermute | solution.py:547

commit v4 on v3

--- a/solution.py
+++ b/solution.py
@@ -21,6 +21,8 @@
 N = 2048
 ROWS = N // SLABS
 TILES = N // LANES
+HALF = N // 2
+HALVES = TILES // 2
 FREQS = LANES // SLABS
 STEP = SLABS * FREQS
 F32 = jnp.float32
@@ -184,7 +186,7 @@
 
 def lookup_kernel(perm_hbm, label_hbm, p_hbm, root_out, p_out, msg_hbm, perm_ref, label, sems, msg_sems):
     table = start(perm_hbm, perm_ref, sems.at[8])
-    loads = [start(p_hbm.at[:, rows_of(d), :], p_out.at[:, rows_of(d), :], msg_sems.at[2, d]) for d in range(DEPTHS)]
+    loads = [start(p_hbm.at[:, rows_of(d), :], p_out.at[:, rows_of(d), :], msg_sems.at[4, d]) for d in range(DEPTHS)]
     copies = []
 
     def work(zone, at):
@@ -192,8 +194,10 @@
 
     def done(d):
         loads[d].wait()
-        copies.append(start(p_out.at[:, rows_of(d), :], msg_hbm.at[d, 0:2], msg_sems.at[1, d]))
-        copies.append(start(root_out.at[:, rows_of(d), :], msg_hbm.at[d, 3:5], msg_sems.at[0, d]))
+        for h in range(2):
+            at = slice(h * HALF, (h + 1) * HALF)
+            copies.append(start(p_out.at[:, rows_of(d), at], msg_hbm.at[d, h * 2 : h * 2 + 2], msg_sems.at[h, d]))
+            copies.append(start(root_out.at[:, rows_of(d), at], msg_hbm.at[d, h * 2 + 4 : h * 2 + 6], msg_sems.at[2 + h, d]))
 
     table.wait()
     each_part(label_hbm, label, sems, work, done)
@@ -234,16 +238,24 @@
 
 def pack_kernel(p_ref, q_ref, before_ref, after_ref, msg_hbm, out_hbm, side_ref, sems):
     row = lax.broadcasted_iota(jnp.int32, (8, N), 0)
+    half_row = lax.broadcasted_iota(jnp.int32, (8, HALF), 0) % 4
     copies = []
     for d in range(DEPTHS):
+        both = []
         for v, ref in enumerate((p_ref, q_ref)):
             sides = []
             for l in range(2):
                 prev = ref[l, d * 8 - 8 : d * 8, :] if d else before_ref[v, l]
                 then = ref[l, d * 8 + 8 : d * 8 + 16, :] if d < DEPTHS - 1 else after_ref[v, l]
                 sides.append(jnp.where(row < 4, then, prev))
-            side_ref[d, v] = jnp.where((row < 2) | (row >= 6), sides[0], pltpu.roll(sides[1], 4, 0))
-            copies.append(start(side_ref.at[d, v], out_hbm.at[d, v * 3 + 2], sems.at[v, d]))
+            both.append(jnp.where((row < 2) | (row >= 6), sides[0], pltpu.roll(sides[1], 4, 0)))
+        out_p, out_q = [jnp.where((row == 0) | (row == 4), pltpu.roll(x, 7, 0), pltpu.roll(x, 1, 0)) for x in both]
+        both.append(out_q * (out_p - both[0]))
+        for v, x in enumerate(both):
+            side_ref[d, v] = jnp.where(
+                (half_row == 0) | (half_row == 3), x[:, :HALF], pltpu.roll(x[:, HALF:], 2, 0)
+            )
+        copies.append(start(side_ref.at[d], out_hbm.at[d, 8:11], sems.at[d]))
     for copy in copies:
         copy.wait()
 
@@ -277,10 +289,10 @@
     return up0 + down0, up1 + down1
 
 
-def of_side_rows(main0, main1, side, row):
-    up = jnp.where(row == 0, pltpu.roll(main0, 1, 0), jnp.where(row == 4, pltpu.roll(main1, 5, 0), pltpu.roll(side, 1, 0)))
-    down = jnp.where(row == 7, pltpu.roll(main0, 7, 0), jnp.where(row == 3, pltpu.roll(main1, 3, 0), pltpu.roll(side, 7, 0)))
-    return up + down
+def of_side_rows(main0, main1, row):
+    of0 = jnp.where(row == 0, pltpu.roll(main0, 1, 0), pltpu.roll(main0, 7, 0))
+    of1 = jnp.where(row == 4, pltpu.roll(main1, 5, 0), pltpu.roll(main1, 3, 0))
+    return jnp.where((row == 0) | (row == 7), of0, of1)
 
 
 def tile(c):
@@ -301,32 +313,45 @@
     lane = lax.broadcasted_iota(jnp.int32, (8, LANES), 1)
     of_second = (row >= 2) & (row < 6)
 
+    def main(d, v, l, c):
+        return msg_ref[d, v * 4 + c // HALVES * 2 + l, :, tile(c % HALVES)]
+
+    def side(d, v, c):
+        found = msg_ref[d, 8 + v, :, tile(c % HALVES)]
+        return found if c < HALVES else pltpu.roll(found, 6, 0)
+
     def first(d, carry):
         below, above = jnp.maximum(d - 1, 0), jnp.minimum(d + 1, DEPTHS - 1)
         has_below, has_above = (d > 0).astype(F32), (d < DEPTHS - 1).astype(F32)
         pltpu.make_async_copy(src1_hbm.at[d], src1_ref.at[d], sems.at[3, d]).wait()
-        q = [Tiles(lambda c, i=i: msg_ref[d, 3 + i, :, tile(c)]) for i in range(3)]
-        p = [Tiles(lambda c, i=i: msg_ref[d, i, :, tile(c)]) for i in range(3)]
+
+        def three(v):
+            return [Tiles(lambda c, l=l: main(d, v, l, c)) for l in range(2)] + [Tiles(lambda c: side(d, v, c))]
+
+        p, q = three(0), three(1)
         u = [Tiles(lambda c, i=i: q[i][c] * p[i][c]) for i in range(3)]
         for c in range(TILES):
             at = tile(c)
-            q_below = [msg_ref[below, 3 + i, :, at] * has_below for i in (1, 2)]
-            q_above = [msg_ref[above, 3 + i, :, at] * has_above for i in (0, 2)]
-            u_below = [x * msg_ref[below, i, :, at] for x, i in zip(q_below, (1, 2))]
-            u_above = [x * msg_ref[above, i, :, at] for x, i in zip(q_above, (0, 2))]
+            q_below = [main(below, 1, 1, c) * has_below, side(below, 1, c) * has_below]
+            q_above = [main(above, 1, 0, c) * has_above, side(above, 1, c) * has_above]
+            u_below = [q_below[0] * main(below, 0, 1, c), q_below[1] * side(below, 0, c)]
+            u_above = [q_above[0] * main(above, 0, 0, c), q_above[1] * side(above, 0, c)]
             sums = []
             for own, low, high in ((q, q_below, q_above), (u, u_below, u_above)):
-                x0, x1, side = own[0][c], own[1][c], own[2][c]
-                sum0, sum1 = of_rows(x0, x1, side, row)
-                depth = pltpu.roll(side + jnp.where(of_second, low[1], high[1]), 4, 0)
+                x0, x1, x2 = own[0][c], own[1][c], own[2][c]
+                sum0, sum1 = of_rows(x0, x1, x2, row)
+                depth = pltpu.roll(x2 + jnp.where(of_second, low[1], high[1]), 4, 0)
                 sums.append((
                     sum0 + own[0].beside(c, lane) + (low[0] + x1),
                     sum1 + own[1].beside(c, lane) + (x0 + high[0]),
-                    of_side_rows(x0, x1, side, row) + own[2].beside(c, lane) + depth,
+                    of_side_rows(x0, x1, row) + own[2].beside(c, lane) + depth,
                 ))
             for i in range(3):
                 s, t = sums[0][i], sums[1][i]
-                new = p[i][c] + (conduct * q[i][c]) * (t - p[i][c] * s) + src1_ref[d, i, :, at]
+                gain = t - p[i][c] * s
+                if i == 2:
+                    gain = gain + side(d, 2, c)
+                new = p[i][c] + (conduct * q[i][c]) * gain + src1_ref[d, i, :, at]
                 w_ref[d + 1, i, :, at] = q[i][c] * new
                 if i < 2:
                     s_ref[d, i, :, at] = s
@@ -349,7 +374,7 @@
             for l, t in ((0, t0), (1, t1)):
                 p = p_ref[d, l, :, at]
                 new_ref[k, l, :, at] = (
-                    p + (conduct * msg_ref[d, 3 + l, :, at]) * (t - p * s_ref[d, l, :, at]) + src2_ref[d, l, :, at]
+                    p + (conduct * main(d, 1, l, c)) * (t - p * s_ref[d, l, :, at]) + src2_ref[d, l, :, at]
                 )
         spectrum_of_rows(new_ref.at[k], twist_ref, mid_ref, d)
         return carry
@@ -567,8 +592,8 @@
         lookup_kernel,
         8,
         ((HBM, perm_table), (HBM, zone_labels), (HBM, pressure)),
-        [(VMEM, block)] * 2 + [(HBM, (DEPTHS, 6, 8, N))],
-        [table, buf(*block, dtype=jnp.int32), DMA((9,)), DMA((3, 8))],
+        [(VMEM, block)] * 2 + [(HBM, (DEPTHS, 11, 8, HALF))],
+        [table, buf(*block, dtype=jnp.int32), DMA((9,)), DMA((5, 8))],
     )
     (inv,) = call(
         strength_kernel,
@@ -600,8 +625,8 @@
         pack_kernel,
         8,
         ((VMEM, p_copy), (VMEM, root), (VMEM, before), (VMEM, after), (HBM, msg)),
-        [(HBM, (DEPTHS, 6, 8, N))],
-        [buf(DEPTHS, *rows), DMA((2, 8))],
+        [(HBM, (DEPTHS, 11, 8, HALF))],
+        [buf(DEPTHS, 3, 8, HALF), DMA((8,))],
         {4: 0},
     )
     msg = lax.all_to_all(msg, "depth", 0, 0, tiled=True)

time: 171 us -> 168 us (0.982)
    all_to_all x1, waiting for transfers between devices: 36.4 us -> 33.8 us  [shards(): msg = lax.all_to_all(msg, 'depth', 0, 0, tiled=True)]
where the time goes in v4:
time: 168 us
  waiting for transfers between devices  64.2 us (38%)
  starting transfers between devices  42.6 us (25%)
  Pallas kernels  29.5 us (18%)
  blocking collectives  15.9 us (9%)
  local copies, waits for them, and re-layouts  13.6 us (8%)
    all_to_all x1, waiting for transfers between devices, shards(): msg = lax.all_to_all(msg, 'depth', 0, 0, tiled=True)  33.8 us
    pallas_call x9, Pallas kernels, call(): pl.pallas_call(kernel, out_shape=[HBM(shape, F32) if space is HBM else ve...  29.5 us
    all_to_all x1, blocking collectives, shards(): rate = lax.all_to_all(rate, 'depth', 0, 0, tiled=True)  15.9 us
    all_to_all x1, waiting for transfers between devices, shards(): lax.all_to_all(spec.reshape(SLABS * DEPTHS, 8, LANES), ('slab', 'depth'),...  15.7 us
    all_to_all x1, starting transfers between devices, shards(): lax.all_to_all(spec.reshape(SLABS * DEPTHS, 8, LANES), ('slab', 'depth'),...  14.6 us
    ppermute x7, waiting for transfers between devices, rotate(): lax.ppermute(v, 'depth', [(i, (i + k) % DEPTHS) for i in range(DEPTHS)])  11.2 us
    ppermute x7, starting transfers between devices, rotate(): lax.ppermute(v, 'depth', [(i, (i + k) % DEPTHS) for i in range(DEPTHS)])  10.9 us
    reshape x2, local copies, waits for them, and re-layouts, shards(): (green_spectrum * (1.0 / (N * N))).reshape(8, 8, SLABS, FREQS, TILES)  7.01 us
  transfers between devices with their start and end apart: 12, of which 6 were waited for; matrix products, arithmetic and copies ran while one was open for 9% of the time, Pallas kernels for 6%

profile of v4, /device:TPU:2, one launch (start us, length us, event | category | flops | bytes accessed | tf_op | source)
XLA Modules:
  0.0 167.6 jit_solution(15231008289699039225)
XLA Ops:
  0.6 1.4 shard_map.185
  2.1 1.9 %collective-permute-start = (f32[2,2,8,2048]{3,2,1,0:T(8,128)S(1)}, f32[2,2,8,2048]{3,2,1,0:T(8,128)S(1)}, u32[]{:S(2)}, u32[]{:S(2)}) collective-permute-start(f32[2,2,8,2048]{3,2,1,0:T(8,128)S(1)} %get-tuple-element.24), channel_id=1, source_target_pairs={{0,8},{8,16},{16,24},{24,32},{32,40},{40,48},{48,56},{56,64},{64,7... | collective-permute-start | bytes 786440 | tf_op jit(solution)/shard_map/ppermute | solution.py:568
  4.0 3.6 %collective-permute-start.1 = (f32[2,2,8,2048]{3,2,1,0:T(8,128)S(1)}, f32[2,2,8,2048]{3,2,1,0:T(8,128)S(1)}, u32[]{:S(2)}, u32[]{:S(2)}) collective-permute-start(f32[2,2,8,2048]{3,2,1,0:T(8,128)S(1)} %get-tuple-element.25), channel_id=1, source_target_pairs={{8,0},{16,8},{24,16},{32,24},{40,32},{48,40},{56,48},{64,56},{72,6... | collective-permute-start | bytes 786440 | tf_op jit(solution)/shard_map/ppermute | solution.py:568
  7.6 4.2 %shard_map.184 = (f32[2,64,2048]{2,1,0:T(8,128)S(1)}, f32[2,64,2048]{2,1,0:T(8,128)S(1)}, f32[8,11,8,1024]{3,2,1,0:T(8,128)}) custom-call(f32[16]{0:T(128)} %perm_hbm.3, s32[2,64,2048]{2,1,0:T(8,128)} %label_hbm.5, f32[2,64,2048]{2,1,0:T(8,128)} %p_hbm.3), custom_call_target="tpu_custom_call" | custom-call | tf_op jit(solution)/shard_map/pallas_call | solution.py:550
  11.8 0.0 collective-permute-done.before_ref
  11.9 0.0 collective-permute-done.1.after_ref
  11.9 1.1 shard_map.186
  12.9 0.0 copy-start.4
  13.0 0.0 copy-start.5
  13.0 0.0 copy-start.1
  13.0 6.2 %all-to-all-start = ((f32[8,11,8,1024]{3,2,1,0:T(8,128)}), f32[8,11,8,1024]{3,2,1,0:T(8,128)S(1)}, u32[]{:S(2)}, u32[]{:S(2)}) async-start(f32[8,11,8,1024]{3,2,1,0:T(8,128)} %shard_map.186), calls=%async_computation | async-start | bytes 5767168 | tf_op jit(solution)/shard_map/all_to_all | solution.py:632
  19.2 0.0 copy-done.4
  19.2 0.1 copy.25.col_ref
  19.3 0.0 copy-done.5
  19.4 2.5 %shard_map.187 = (f32[192,2048]{1,0:T(8,128)}, f32[128,2048]{1,0:T(8,128)}) custom-call(s32[1,512]{1,0:T(1,128)S(1)} %get-tuple-element.42.where1_ref, s32[1,512]{1,0:T(1,128)S(1)} %get-tuple-element.41.where2_ref, f32[2,512]{1,0:T(2,128)S(1)} %convert_multiply_fusion.amount_ref, s32[512,1]{1,0:T(8,128)S(1)} %copy.25.col_ref), custom_call_target="tpu_custom_call" | custom-call | tf_op jit(solution)/shard_map/pallas_call | solution.py:550
  21.9 33.8 %all-to-all-done.msg_ref = f32[8,11,8,1024]{3,2,1,0:T(8,128)S(1)} async-done(((f32[8,11,8,1024]{3,2,1,0:T(8,128)}), f32[8,11,8,1024]{3,2,1,0:T(8,128)S(1)}, u32[]{:S(2)}, u32[]{:S(2)}) %all-to-all-start) | async-done | bytes 2883616 | tf_op jit(solution)/shard_map/all_to_all | solution.py:632
  55.7 0.0 copy-done.1
  55.7 6.6 %shard_map.188 = (f32[2,8,2048]{2,1,0:T(8,128)}, f32[2,8,2048]{2,1,0:T(8,128)}, f32[2,8,2048]{2,1,0:T(8,128)}, f32[2,8,2048]{2,1,0:T(8,128)}, f32[2,8,2048]{2,1,...) custom-call(s32[1]{0:T(128)} %bitcast.me_ref, ...), custom_call_target="tpu_custom_call" | custom-call | tf_op jit(solution)/shard_map/pallas_call | solution.py:550
  62.3 14.6 %all-to-all-start.1 = ((f32[256,8,128]{2,1,0:T(8,128)}), f32[256,8,128]{2,1,0:T(8,128)S(1)}, u32[]{:S(2)}, u32[]{:S(2)}) async-start(f32[256,8,128]{2,1,0:T(8,128)} %bitcast.51), calls=%async_computation.1 | async-start | bytes 2097152 | tf_op jit(solution)/shard_map/all_to_all | solution.py:642
  76.8 0.8 broadcast_multiply_fusion
  77.7 1.8 %reshape.243 = f32[8,8,32,4,16]{2,1,0,4,3:T(8,128)S(1)} reshape(f32[2048,64]{0,1:T(8,128)} %broadcast_multiply_fusion) | data formatting | bytes 1048576 | tf_op jit(solution)/shard_map/reshape | solution.py:621
  79.5 5.2 %copy.24 = f32[8,8,32,4,16]{0,4,3,2,1:T(8,128)} copy(f32[8,8,32,4,16]{2,1,0,4,3:T(8,128)S(1)} %reshape.243) | data formatting | bytes 1048576 | tf_op jit(solution)/shard_map/reshape | solution.py:621
  84.7 6.4 %reshape.244.green_ref = f32[8,128,128]{2,1,0:T(8,128)S(1)} reshape(f32[8,32,4,16,8]{4,3,2,1,0:T(8,128)} %bitcast.48) | data formatting | bytes 1048576 | tf_op jit(solution)/shard_map/reshape | solution.py:622
  91.1 15.7 %all-to-all-done.1 = f32[256,8,128]{2,1,0:T(8,128)S(1)} async-done(((f32[256,8,128]{2,1,0:T(8,128)}), f32[256,8,128]{2,1,0:T(8,128)S(1)}, u32[]{:S(2)}, u32[]{:S(2)}) %all-to-all-start.1) | async-done | bytes 1048608 | tf_op jit(solution)/shard_map/all_to_all | solution.py:642
  106.9 5.5 %shard_map.189 = f32[256,1024]{1,0:T(8,128)} custom-call(f32[32,8,8,128]{3,2,1,0:T(8,128)S(1)} %bitcast.47, f32[8,128,128]{2,1,0:T(8,128)S(1)} %reshape.244.green_ref, bf16[256,768]{1,0:T(8,128)(2,1)} %constant.98.clone.mid_hbm, bf16[256,768]{1,0:T(8,128)(2,1)} %constant.99.clone.mid_inv_hbm, bf16[768,256]{1,0:T(8,128)(2,1)} %constant.100.clone.inner_hbm, ...), custom_call_target="tpu_custom_call" | custom-call | tf_op jit(solution)/shard_map/pallas_call | solution.py:550
  112.4 5.4 %all-to-all-start.2 = ((f32[32,8,1024]{2,1,0:T(8,128)}), f32[32,8,1024]{2,1,0:T(8,128)S(1)}, u32[]{:S(2)}, u32[]{:S(2)}) async-start(f32[32,8,1024]{2,1,0:T(8,128)} %bitcast.49), calls=%async_computation.2 | async-start | bytes 2097152 | tf_op jit(solution)/shard_map/all_to_all | solution.py:653
  117.8 0.0 copy-done.12
  117.8 1.6 collective-permute-start.2
  119.4 0.7 collective-permute-start.3
  120.1 2.8 %collective-permute-start.4 = (f32[2,8,2048]{2,1,0:T(8,128)S(1)}, f32[2,8,2048]{2,1,0:T(8,128)S(1)}, u32[]{:S(2)}, u32[]{:S(2)}) collective-permute-start(f32[2,8,2048]{2,1,0:T(8,128)S(1)} %copy-done.10), channel_id=1, source_target_pairs={{0,3},{1,4},{2,5},{3,6},{4,7},{5,0},{6,1},{7,2},{8,11},{9,12},{10,... | collective-permute-start | bytes 393224 | tf_op jit(solution)/shard_map/ppermute | solution.py:572
  123.0 0.0 copy-done.9
  123.0 2.8 %collective-permute-start.5 = (f32[2,8,2048]{2,1,0:T(8,128)S(1)}, f32[2,8,2048]{2,1,0:T(8,128)S(1)}, u32[]{:S(2)}, u32[]{:S(2)}) collective-permute-start(f32[2,8,2048]{2,1,0:T(8,128)S(1)} %copy-done.9), channel_id=1, source_target_pairs={{0,4},{1,5},{2,6},{3,7},{4,0},{5,1},{6,2},{7,3},{8,12},{9,13},{10,... | collective-permute-start | bytes 393224 | tf_op jit(solution)/shard_map/ppermute | solution.py:572
  125.8 2.8 %collective-permute-start.6 = (f32[2,8,2048]{2,1,0:T(8,128)S(1)}, f32[2,8,2048]{2,1,0:T(8,128)S(1)}, u32[]{:S(2)}, u32[]{:S(2)}) collective-permute-start(f32[2,8,2048]{2,1,0:T(8,128)S(1)} %copy-done.8), channel_id=1, source_target_pairs={{0,5},{1,6},{2,7},{3,0},{4,1},{5,2},{6,3},{7,4},{8,13},{9,14},{10,... | collective-permute-start | bytes 393224 | tf_op jit(solution)/shard_map/ppermute | solution.py:572
  128.6 3.9 %collective-permute-done.2.rest_1_ = f32[2,8,2048]{2,1,0:T(8,128)S(1)} collective-permute-done((f32[2,8,2048]{2,1,0:T(8,128)S(1)}, f32[2,8,2048]{2,1,0:T(8,128)S(1)}, u32[]{:S(2)}, u32[]{:S(2)}) %collective-permute-start.2) | collective-permute-done | bytes 131104 | tf_op jit(solution)/shard_map/ppermute | solution.py:572
  132.5 0.0 collective-permute-start.7
  132.5 0.0 collective-permute-done.3.rest_2_
  132.5 0.1 collective-permute-start.8
  132.6 3.3 %shard_map.190.inv_hbm = f32[2,64,2048]{2,1,0:T(8,128)} custom-call(f32[16]{0:T(128)} %asig_hbm.1, s32[2,64,2048]{2,1,0:T(8,128)} %label_hbm.5), custom_call_target="tpu_custom_call" | custom-call | tf_op jit(solution)/shard_map/pallas_call | solution.py:550
  136.0 0.0 collective-permute-done.4.rest_3_
  136.0 0.0 collective-permute-done.5.rest_4_
  136.0 4.7 %collective-permute-done.6.rest_5_ = f32[2,8,2048]{2,1,0:T(8,128)S(1)} collective-permute-done((f32[2,8,2048]{2,1,0:T(8,128)S(1)}, f32[2,8,2048]{2,1,0:T(8,128)S(1)}, u32[]{:S(2)}, u32[]{:S(2)}) %collective-permute-start.6) | collective-permute-done | bytes 131104 | tf_op jit(solution)/shard_map/ppermute | solution.py:572
  140.7 0.0 collective-permute-done.7.rest_6_
  140.8 2.6 %collective-permute-done.8.rest_7_ = f32[2,8,2048]{2,1,0:T(8,128)S(1)} collective-permute-done((f32[2,8,2048]{2,1,0:T(8,128)S(1)}, f32[2,8,2048]{2,1,0:T(8,128)S(1)}, u32[]{:S(2)}, u32[]{:S(2)}) %collective-permute-start.8) | collective-permute-done | bytes 131104 | tf_op jit(solution)/shard_map/ppermute | solution.py:572
  143.3 3.5 %all-to-all-done.2 = f32[32,8,1024]{2,1,0:T(8,128)S(1)} async-done(((f32[32,8,1024]{2,1,0:T(8,128)}), f32[32,8,1024]{2,1,0:T(8,128)S(1)}, u32[]{:S(2)}, u32[]{:S(2)}) %all-to-all-start.2) | async-done | bytes 1048608 | tf_op jit(solution)/shard_map/all_to_all | solution.py:653
  146.8 0.0 copy-done
  146.8 4.3 %shard_map.191 = (f32[2,64,2048]{2,1,0:T(8,128)}, f32[2,64,2048]{2,1,0:T(8,128)}, f32[8,64,256]{2,1,0:T(8,128)}) custom-call(s32[1]{0:T(128)} %bitcast.me_ref, f32[2]{0:T(128)S(1)} %add_multiply_fusion.weight_ref, f32[256,1024]{1,0:T(8,128)S(1)} %bitcast.46, f32[2,64,2048]{2,1,0:T(8,128)} %shard_map.190.inv_hbm, f32[2,64,2048]{2,1,0:T(8,128)} %seis_hbm.1, ...), custom_call_target="tpu_custom_call" | custom-call | tf_op jit(solution)/shard_map/pallas_call | solution.py:550
  151.1 15.9 %all_to_all.20.part_ref = f32[8,64,256]{2,1,0:T(8,128)S(1)} all-to-all(f32[8,64,256]{2,1,0:T(8,128)} %get-tuple-element.40), channel_id=1, replica_groups=mesh['slab'=32,'depth'=8] {'depth'}, dimensions={0} | all-to-all | bytes 1048576 | tf_op jit(solution)/shard_map/all_to_all | solution.py:665
  167.0 0.7 shard_map.192
  (21 shorter events, 0.1 us)
Async XLA Ops:
  2.1 9.8 %collective-permute-start = (f32[2,2,8,2048]{3,2,1,0:T(8,128)S(1)}, f32[2,2,8,2048]{3,2,1,0:T(8,128)S(1)}, u32[]{:S(2)}, u32[]{:S(2)}) collective-permute-start(f32[2,2,8,2048]{3,2,1,0:T(8,128)S(1)} %get-tuple-element.24), channel_id=1, source_target_pairs={{0,8},{8,16},{16,24},{24,32},{32,40},{40,48},{48,56},{56,64},{64,7... | collective-permute-start | bytes 786440 | tf_op jit(solution)/shard_map/ppermute | solution.py:568
  4.0 7.9 %collective-permute-start.1 = (f32[2,2,8,2048]{3,2,1,0:T(8,128)S(1)}, f32[2,2,8,2048]{3,2,1,0:T(8,128)S(1)}, u32[]{:S(2)}, u32[]{:S(2)}) collective-permute-start(f32[2,2,8,2048]{3,2,1,0:T(8,128)S(1)} %get-tuple-element.25), channel_id=1, source_target_pairs={{8,0},{16,8},{24,16},{32,24},{40,32},{48,40},{56,48},{64,56},{72,6... | collective-permute-start | bytes 786440 | tf_op jit(solution)/shard_map/ppermute | solution.py:568
  12.9 6.2 %copy-start.4 = (s32[512,3]{0,1:T(4,128)S(1)}, s32[512,3]{0,1:T(4,128)}, u32[]{:S(2)}) copy-start(s32[512,3]{0,1:T(4,128)} %param.21) | copy-start | bytes 18436
  13.0 6.4 %copy-start.5 = (s32[2,512]{1,0:T(2,128)S(1)}, s32[2,512]{1,0:T(2,128)}, u32[]{:S(2)}) copy-start(s32[2,512]{1,0:T(2,128)} %param.22) | copy-start | bytes 12292
  13.0 42.7 %copy-start.1 = (f32[2,16,128]{2,1,0:T(8,128)S(1)}, f32[2,16,128]{2,1,0:T(8,128)}, u32[]{:S(2)}) copy-start(f32[2,16,128]{2,1,0:T(8,128)} %constant.102.clone.twist_ref) | copy-start | bytes 49156
  13.0 42.7 %all-to-all-start = ((f32[8,11,8,1024]{3,2,1,0:T(8,128)}), f32[8,11,8,1024]{3,2,1,0:T(8,128)S(1)}, u32[]{:S(2)}, u32[]{:S(2)}) async-start(f32[8,11,8,1024]{3,2,1,0:T(8,128)} %shard_map.186), calls=%async_computation | async-start | bytes 5767168 | tf_op jit(solution)/shard_map/all_to_all | solution.py:632
  55.7 21.2 %copy-start.3 = (f32[2048,64]{0,1:T(8,128)S(1)}, f32[2048,64]{0,1:T(8,128)}, u32[]{:S(2)}) copy-start(f32[2048,64]{0,1:T(8,128)} %param.23) | copy-start | bytes 1572868
  62.3 44.6 %all-to-all-start.1 = ((f32[256,8,128]{2,1,0:T(8,128)}), f32[256,8,128]{2,1,0:T(8,128)S(1)}, u32[]{:S(2)}, u32[]{:S(2)}) async-start(f32[256,8,128]{2,1,0:T(8,128)} %bitcast.51), calls=%async_computation.1 | async-start | bytes 2097152 | tf_op jit(solution)/shard_map/all_to_all | solution.py:642
  84.7 22.1 %copy-start.2 = (f32[2,8,128]{2,1,0:T(8,128)S(1)}, f32[2,8,128]{2,1,0:T(8,128)}, u32[]{:S(2)}) copy-start(f32[2,8,128]{2,1,0:T(8,128)} %constant.104.clone.in_ref) | copy-start | bytes 24580
  106.8 11.0 %copy-start.12 = (f32[2,8,2048]{2,1,0:T(8,128)S(1)}, f32[2,8,2048]{2,1,0:T(8,128)}, u32[]{:S(2)}) copy-start(f32[2,8,2048]{2,1,0:T(8,128)} %get-tuple-element.31) | copy-start | bytes 393220
  106.8 12.6 %copy-start.11 = (f32[2,8,2048]{2,1,0:T(8,128)S(1)}, f32[2,8,2048]{2,1,0:T(8,128)}, u32[]{:S(2)}) copy-start(f32[2,8,2048]{2,1,0:T(8,128)} %get-tuple-element.32) | copy-start | bytes 393220
  106.8 13.3 %copy-start.10 = (f32[2,8,2048]{2,1,0:T(8,128)S(1)}, f32[2,8,2048]{2,1,0:T(8,128)}, u32[]{:S(2)}) copy-start(f32[2,8,2048]{2,1,0:T(8,128)} %get-tuple-element.33) | copy-start | bytes 393220
  106.8 16.1 %copy-start.9 = (f32[2,8,2048]{2,1,0:T(8,128)S(1)}, f32[2,8,2048]{2,1,0:T(8,128)}, u32[]{:S(2)}) copy-start(f32[2,8,2048]{2,1,0:T(8,128)} %get-tuple-element.34) | copy-start | bytes 393220
  106.8 19.0 %copy-start.8 = (f32[2,8,2048]{2,1,0:T(8,128)S(1)}, f32[2,8,2048]{2,1,0:T(8,128)}, u32[]{:S(2)}) copy-start(f32[2,8,2048]{2,1,0:T(8,128)} %get-tuple-element.35) | copy-start | bytes 393220
  106.9 25.7 %copy-start.7 = (f32[2,8,2048]{2,1,0:T(8,128)S(1)}, f32[2,8,2048]{2,1,0:T(8,128)}, u32[]{:S(2)}) copy-start(f32[2,8,2048]{2,1,0:T(8,128)} %get-tuple-element.36) | copy-start | bytes 393220
  106.9 25.7 %copy-start.6 = (f32[2,8,2048]{2,1,0:T(8,128)S(1)}, f32[2,8,2048]{2,1,0:T(8,128)}, u32[]{:S(2)}) copy-start(f32[2,8,2048]{2,1,0:T(8,128)} %get-tuple-element.37) | copy-start | bytes 393220
  112.4 34.4 %copy-start = (f32[2,8,2048]{2,1,0:T(8,128)S(1)}, f32[2,8,2048]{2,1,0:T(8,128)}, u32[]{:S(2)}) copy-start(f32[2,8,2048]{2,1,0:T(8,128)} %get-tuple-element.30.rest_0_) | copy-start | bytes 393220
  112.4 34.4 %all-to-all-start.2 = ((f32[32,8,1024]{2,1,0:T(8,128)}), f32[32,8,1024]{2,1,0:T(8,128)S(1)}, u32[]{:S(2)}, u32[]{:S(2)}) async-start(f32[32,8,1024]{2,1,0:T(8,128)} %bitcast.49), calls=%async_computation.2 | async-start | bytes 2097152 | tf_op jit(solution)/shard_map/all_to_all | solution.py:653
  117.8 14.7 %collective-permute-start.2 = (f32[2,8,2048]{2,1,0:T(8,128)S(1)}, f32[2,8,2048]{2,1,0:T(8,128)S(1)}, u32[]{:S(2)}, u32[]{:S(2)}) collective-permute-start(f32[2,8,2048]{2,1,0:T(8,128)S(1)} %copy-done.12), channel_id=1, source_target_pairs={{0,1},{1,2},{2,3},{3,4},{4,5},{5,6},{6,7},{7,0},{8,9},{9,10},{10,1... | collective-permute-start | bytes 393224 | tf_op jit(solution)/shard_map/ppermute | solution.py:572
  119.4 13.1 %collective-permute-start.3 = (f32[2,8,2048]{2,1,0:T(8,128)S(1)}, f32[2,8,2048]{2,1,0:T(8,128)S(1)}, u32[]{:S(2)}, u32[]{:S(2)}) collective-permute-start(f32[2,8,2048]{2,1,0:T(8,128)S(1)} %copy-done.11), channel_id=1, source_target_pairs={{0,2},{1,3},{2,4},{3,5},{4,6},{5,7},{6,0},{7,1},{8,10},{9,11},{10,... | collective-permute-start | bytes 393224 | tf_op jit(solution)/shard_map/ppermute | solution.py:572
  120.1 15.9 %collective-permute-start.4 = (f32[2,8,2048]{2,1,0:T(8,128)S(1)}, f32[2,8,2048]{2,1,0:T(8,128)S(1)}, u32[]{:S(2)}, u32[]{:S(2)}) collective-permute-start(f32[2,8,2048]{2,1,0:T(8,128)S(1)} %copy-done.10), channel_id=1, source_target_pairs={{0,3},{1,4},{2,5},{3,6},{4,7},{5,0},{6,1},{7,2},{8,11},{9,12},{10,... | collective-permute-start | bytes 393224 | tf_op jit(solution)/shard_map/ppermute | solution.py:572
  123.0 13.1 %collective-permute-start.5 = (f32[2,8,2048]{2,1,0:T(8,128)S(1)}, f32[2,8,2048]{2,1,0:T(8,128)S(1)}, u32[]{:S(2)}, u32[]{:S(2)}) collective-permute-start(f32[2,8,2048]{2,1,0:T(8,128)S(1)} %copy-done.9), channel_id=1, source_target_pairs={{0,4},{1,5},{2,6},{3,7},{4,0},{5,1},{6,2},{7,3},{8,12},{9,13},{10,... | collective-permute-start | bytes 393224 | tf_op jit(solution)/shard_map/ppermute | solution.py:572
  125.8 15.0 %collective-permute-start.6 = (f32[2,8,2048]{2,1,0:T(8,128)S(1)}, f32[2,8,2048]{2,1,0:T(8,128)S(1)}, u32[]{:S(2)}, u32[]{:S(2)}) collective-permute-start(f32[2,8,2048]{2,1,0:T(8,128)S(1)} %copy-done.8), channel_id=1, source_target_pairs={{0,5},{1,6},{2,7},{3,0},{4,1},{5,2},{6,3},{7,4},{8,13},{9,14},{10,... | collective-permute-start | bytes 393224 | tf_op jit(solution)/shard_map/ppermute | solution.py:572
  132.5 8.2 %collective-permute-start.7 = (f32[2,8,2048]{2,1,0:T(8,128)S(1)}, f32[2,8,2048]{2,1,0:T(8,128)S(1)}, u32[]{:S(2)}, u32[]{:S(2)}) collective-permute-start(f32[2,8,2048]{2,1,0:T(8,128)S(1)} %copy-done.7), channel_id=1, source_target_pairs={{0,6},{1,7},{2,0},{3,1},{4,2},{5,3},{6,4},{7,5},{8,14},{9,15},{10,... | collective-permute-start | bytes 393224 | tf_op jit(solution)/shard_map/ppermute | solution.py:572
  132.5 10.8 %collective-permute-start.8 = (f32[2,8,2048]{2,1,0:T(8,128)S(1)}, f32[2,8,2048]{2,1,0:T(8,128)S(1)}, u32[]{:S(2)}, u32[]{:S(2)}) collective-permute-start(f32[2,8,2048]{2,1,0:T(8,128)S(1)} %copy-done.6), channel_id=1, source_target_pairs={{0,7},{1,0},{2,1},{3,2},{4,3},{5,4},{6,5},{7,6},{8,15},{9,8},{10,9... | collective-permute-start | bytes 393224 | tf_op jit(solution)/shard_map/ppermute | solution.py:572

commit v5 on v4

--- a/solution.py
+++ b/solution.py
@@ -127,11 +127,32 @@
     return out
 
 
-def pick(label, table, bit, base):
-    if bit < 0:
-        return table[base]
-    mask = (label & (1 << bit)) != 0
-    return jnp.where(mask, pick(label, table, bit - 1, base + (1 << bit)), pick(label, table, bit - 1, base))
+def table_tiles(table, change):
+    lane = lax.broadcasted_iota(jnp.int32, (8, LANES), 1)
+    values = [change(jnp.full((8, LANES), table[zone], F32)) for zone in range(16)]
+    found = values[0]
+    for zone in range(1, 16):
+        found = jnp.where(lane == zone, values[zone], found)
+    return values, found
+
+
+def choose(bits, values):
+    if len(values) == 1:
+        return values[0]
+    half = len(values) // 2
+    return jnp.where(bits[-1], choose(bits[:-1], values[half:]), choose(bits[:-1], values[:half]))
+
+
+def pick(label, tiles):
+    values, found = tiles
+    parts = []
+    for c in range(label.shape[1] // LANES):
+        zone = label[:, tile(c)]
+        if c % 8 in (1, 4, 6):
+            parts.append(jnp.take_along_axis(found, zone, axis=1))
+        else:
+            parts.append(choose([(zone & (1 << bit)) != 0 for bit in range(4)], values))
+    return jnp.concatenate(parts, 1)
 
 
 def start(src, dst, sem):
@@ -144,80 +165,81 @@
     return pl.ds(pl.multiple_of(d * 8, 8), 8)
 
 
-def edge_kernel(perm_hbm, p_hbm, label_hbm, first_out, last_out, perm_ref, label, sems):
-    table = start(perm_hbm, perm_ref, sems.at[4])
+def edge_kernel(perm_hbm, p_hbm, label_hbm, first_out, last_out, perm_ref, label, p_ref, sems):
+    load = start(perm_hbm, perm_ref, sems.at[4])
     first, last = slice(0, 8), slice(ROWS - 8, ROWS)
     loads = [
         start(label_hbm.at[:, first, :], label.at[0], sems.at[0]),
         start(label_hbm.at[:, last, :], label.at[1], sems.at[1]),
-        start(p_hbm.at[:, first, :], first_out.at[0], sems.at[2]),
-        start(p_hbm.at[:, last, :], last_out.at[0], sems.at[3]),
+        start(p_hbm.at[:, first, :], p_ref.at[0], sems.at[2]),
+        start(p_hbm.at[:, last, :], p_ref.at[1], sems.at[3]),
     ]
-    table.wait()
+    load.wait()
+    table = table_tiles(perm_ref, jnp.sqrt)
     for copy in loads:
         copy.wait()
+    pair = lax.broadcasted_iota(jnp.int32, (8, N), 0) // 2
+    for i, (out, at) in enumerate(((first_out, 0), (last_out, 3))):
+        values = [p_ref[i, 0], p_ref[i, 1], pick(label[i, 0], table), pick(label[i, 1], table)]
+        packed = values[0]
+        for n in range(1, 4):
+            packed = jnp.where(pair == (at + n) % 4, pltpu.roll(values[n], 2 * n, 0), packed)
+        out[...] = packed
+
+
+def each_part(label_hbm, label, sems, work, done):
+    parts = [pl.ds(g * 2, 2) for g in range(4)]
+    loads = [start(label_hbm.at[:, at], label.at[:, at], sems.at[g]) for g, at in enumerate(parts)]
     width = 1024
-
-    def body(c, carry):
-        cols = pl.ds(pl.multiple_of(c * width, width), width)
-        for l in range(2):
-            first_out[1, l, :, cols] = jnp.sqrt(pick(label[0, l, :, cols], perm_ref, 3, 0))
-            last_out[1, l, :, cols] = jnp.sqrt(pick(label[1, l, :, cols], perm_ref, 3, 0))
-        return carry
-
-    lax.fori_loop(0, N // width, body, 0)
-
-
-def each_part(label_hbm, label, sems, work, done):
-    loads = [start(label_hbm.at[:, rows_of(d), :], label.at[:, rows_of(d), :], sems.at[d]) for d in range(DEPTHS)]
-    width = 1024
-    for d in range(DEPTHS):
-        loads[d].wait()
-
-        def body(c, carry, d=d):
-            cols = pl.ds(pl.multiple_of(c * width, width), width)
+    for g in range(4):
+        loads[g].wait()
+
+        def body(n, carry, g=g):
+            d = g * 2 + n // 2
+            cols = pl.ds(pl.multiple_of(n % 2 * width, width), width)
             for l in range(2):
-                work(label[l, rows_of(d), cols], (l, rows_of(d), cols))
+                work(label[l, d, :, cols], d, l, cols)
             return carry
 
-        lax.fori_loop(0, N // width, body, 0)
-        done(d)
+        lax.fori_loop(0, 4, body, 0)
+        done(g)
 
 
 def lookup_kernel(perm_hbm, label_hbm, p_hbm, root_out, p_out, msg_hbm, perm_ref, label, sems, msg_sems):
     table = start(perm_hbm, perm_ref, sems.at[8])
-    loads = [start(p_hbm.at[:, rows_of(d), :], p_out.at[:, rows_of(d), :], msg_sems.at[4, d]) for d in range(DEPTHS)]
+    loads = [start(p_hbm.at[l], p_out.at[:, l], msg_sems.at[2, l]) for l in range(2)]
     copies = []
 
-    def work(zone, at):
-        root_out[at] = jnp.sqrt(pick(zone, perm_ref, 3, 0))
-
-    def done(d):
-        loads[d].wait()
+    def work(zone, d, l, cols):
+        root_out[d, l, :, cols] = pick(zone, values)
+
+    def done(g):
         for h in range(2):
             at = slice(h * HALF, (h + 1) * HALF)
-            copies.append(start(p_out.at[:, rows_of(d), at], msg_hbm.at[d, h * 2 : h * 2 + 2], msg_sems.at[h, d]))
-            copies.append(start(root_out.at[:, rows_of(d), at], msg_hbm.at[d, h * 2 + 4 : h * 2 + 6], msg_sems.at[2 + h, d]))
+            if g == 0:
+                loads[h].wait()
+            if g == 1:
+                copies.append(start(p_out.at[:, :, :, at], msg_hbm.at[:, h * 2 : h * 2 + 2], msg_sems.at[h, 7]))
+            if g % 2:
+                rows = pl.ds(g * 2 - 2, 4)
+                copies.append(start(root_out.at[rows, :, :, at], msg_hbm.at[rows, h * 2 + 4 : h * 2 + 6], msg_sems.at[h, g]))
 
     table.wait()
+    values = table_tiles(perm_ref, jnp.sqrt)
     each_part(label_hbm, label, sems, work, done)
     for copy in copies:
         copy.wait()
 
 
-def strength_kernel(asig_hbm, label_hbm, inv_hbm, asig_ref, label, inv, sems, inv_sems):
+def strength_kernel(asig_hbm, label_hbm, inv_hbm, asig_ref, label, inv, sems):
     start(asig_hbm, asig_ref, sems.at[8]).wait()
-    copies = []
-
-    def work(zone, at):
-        inv[at] = 1.0 / pick(zone, asig_ref, 3, 0)
-
-    def done(d):
-        copies.append(start(inv.at[:, rows_of(d), :], inv_hbm.at[:, rows_of(d), :], inv_sems.at[d]))
-
-    each_part(label_hbm, label, sems, work, done)
-    for copy in copies:
-        copy.wait()
+    values = table_tiles(asig_ref, lambda x: 1.0 / x)
+
+    def work(zone, d, l, cols):
+        inv[l, rows_of(d), cols] = pick(zone, values)
+
+    each_part(label_hbm, label, sems, work, lambda g: None)
+    start(inv, inv_hbm, sems.at[8]).wait()
 
 
 def wells_kernel(where1_ref, where2_ref, amount_ref, col_ref, out1_ref, out2_ref, both, sems):
@@ -245,8 +267,9 @@
         for v, ref in enumerate((p_ref, q_ref)):
             sides = []
             for l in range(2):
-                prev = ref[l, d * 8 - 8 : d * 8, :] if d else before_ref[v, l]
-                then = ref[l, d * 8 + 8 : d * 8 + 16, :] if d < DEPTHS - 1 else after_ref[v, l]
+                back = (8 - 2 * (2 * v + l)) % 8
+                prev = ref[d - 1, l] if d else pltpu.roll(before_ref[...], back, 0)
+                then = ref[d + 1, l] if d < DEPTHS - 1 else pltpu.roll(after_ref[...], back, 0)
                 sides.append(jnp.where(row < 4, then, prev))
             both.append(jnp.where((row < 2) | (row >= 6), sides[0], pltpu.roll(sides[1], 4, 0)))
         out_p, out_q = [jnp.where((row == 0) | (row == 4), pltpu.roll(x, 7, 0), pltpu.roll(x, 1, 0)) for x in both]
@@ -255,7 +278,9 @@
             side_ref[d, v] = jnp.where(
                 (half_row == 0) | (half_row == 3), x[:, :HALF], pltpu.roll(x[:, HALF:], 2, 0)
             )
-        copies.append(start(side_ref.at[d], out_hbm.at[d, 8:11], sems.at[d]))
+        if d % 4 == 3:
+            done = pl.ds(d - 3, 4)
+            copies.append(start(side_ref.at[done], out_hbm.at[done, 8:11], sems.at[d]))
     for copy in copies:
         copy.wait()
 
@@ -361,9 +386,8 @@
     lax.fori_loop(0, DEPTHS, first, 0)
     src2_load.wait()
 
-    def second(n, carry):
-        k = lax.rem(n + 1, DEPTHS)
-        d = lax.rem(me + k, DEPTHS)
+    def second(d):
+        k = lax.rem(d + DEPTHS - me, DEPTHS)
         w = [Tiles(lambda c, i=i: w_ref[d + 1, i, :, tile(c)]) for i in range(3)]
         for c in range(TILES):
             at = tile(c)
@@ -377,18 +401,27 @@
                     p + (conduct * main(d, 1, l, c)) * (t - p * s_ref[d, l, :, at]) + src2_ref[d, l, :, at]
                 )
         spectrum_of_rows(new_ref.at[k], twist_ref, mid_ref, d)
-        return carry
-
-    lax.fori_loop(0, DEPTHS, second, 0)
-    copies = [start(new_ref.at[k], outs[k], sems.at[1, k]) for k in range(DEPTHS)]
-    fwd_load.wait()
-    for c in range(4):
+
+    copies = []
+
+    def transform(c):
         part = triple(mid_ref[c * 256 : (c + 1) * 256, :], 1)
         block = lax.dot_general(fwd_ref[...], part, (((1,), (1,)), ((), ())), preferred_element_type=F32)
         for h in range(2):
             at = c * 2 + h
             spec_out[:, at] = block[:, h * 128 : (h + 1) * 128].reshape(SLABS, 8, 128)
-            copies.append(start(spec_out.at[:, at], spec_hbm.at[:, at], sems.at[2, at]))
+        at = pl.ds(c * 2, 2)
+        copies.append(start(spec_out.at[:, at], spec_hbm.at[:, at], sems.at[2, c]))
+
+    second(0)
+    second(1)
+    fwd_load.wait()
+    for d in range(2, DEPTHS, 2):
+        transform(d // 2 - 1)
+        second(d)
+        second(d + 1)
+    transform(DEPTHS // 2 - 1)
+    copies.extend(start(new_ref.at[k], outs[k], sems.at[1, k]) for k in range(DEPTHS))
     for copy in copies:
         copy.wait()
 
@@ -399,7 +432,7 @@
         if k:
             cos, sin = twist_ref[0, k : k + 1, :], twist_ref[1, k : k + 1, :]
             re, im = re * cos - im * sin, re * sin + im * cos
-        at = pl.ds(pl.multiple_of(d * 128 + k * 8, 8), 8)
+        at = slice(d * 128 + k * 8, d * 128 + k * 8 + 8)
         mid_ref[at, 0:128] = re
         mid_ref[at, 128:256] = im
 
@@ -443,17 +476,18 @@
 
 def middle_kernel(
     spec_ref, green_ref, mid_hbm, mid_inv_hbm, inner_hbm, inner_inv_hbm, col_hbm, in_ref, out_hbm,
-    work, out_ref, mid_ref, mid_inv_ref, inner_ref, inner_inv_ref, col_ref, sems,
+    work, out_ref, mid_ref, mid_inv_ref, inner_ref, inner_inv_ref, col_ref, split_ref, sems,
 ):
     pairs = (
         (mid_hbm, mid_ref), (col_hbm, col_ref), (inner_hbm, inner_ref), (inner_inv_hbm, inner_inv_ref),
         (mid_inv_hbm, mid_inv_ref),
     )
     loads = [start(src, dst, sems.at[i]) for i, (src, dst) in enumerate(pairs)]
+    for d in range(DEPTHS):
+        split_ref[:, d * 128 : (d + 1) * 128] = triple(spec_ref[:, d].reshape(256, 128), 0)
     loads[0].wait()
     for d in range(0, DEPTHS, 2):
-        part = jnp.concatenate([spec_ref[:, d + h].reshape(256, 128) for h in range(2)], 1)
-        spread = matmul(mid_ref[...], triple(part, 0))
+        spread = matmul(mid_ref[...], split_ref[:, d * 128 : (d + 2) * 128])
         for h in range(2):
             work[0, d + h] = spread[0:128, h * 128 : (h + 1) * 128]
             work[1, d + h] = spread[128:256, h * 128 : (h + 1) * 128]
@@ -483,7 +517,7 @@
 def last_kernel(me_ref, weight_ref, spec_ref, inv_hbm, seis_hbm, table_hbm, twist_ref, *rest):
     parts, rest = rest[:DEPTHS], rest[DEPTHS:]
     p_out, state_out, rate_out, rest = rest[0], rest[1], rest[2], rest[3:]
-    p_ref, inv_ref, seis_ref, table_ref, state_ref, rate_ref, mid_ref, sems = rest
+    p_ref, inv_ref, seis_ref, table_ref, state_ref, rate_ref, mid_ref, split_ref, sems = rest
     me = me_ref[0]
     table_load = start(table_hbm, table_ref, sems.at[4, 0])
     loads = [start(inv_hbm, inv_ref, sems.at[4, 1]), start(seis_hbm, seis_ref, sems.at[4, 2])]
@@ -491,10 +525,11 @@
     for k in range(DEPTHS):
         d = lax.rem(me + (DEPTHS - k), DEPTHS)
         loads.append(start(parts[k], p_ref.at[:, rows_of(d), :], sems.at[0, k]))
+    for c in range(4):
+        split_ref[c * 256 : (c + 1) * 256, :] = triple(jnp.transpose(spec_ref[:, c * 256 : (c + 1) * 256]), 1)
     table_load.wait()
     for c in range(4):
-        turned = jnp.transpose(spec_ref[:, c * 256 : (c + 1) * 256])
-        mid_ref[c * 256 : (c + 1) * 256, :] = matmul(triple(turned, 1), table_ref[...])
+        mid_ref[c * 256 : (c + 1) * 256, :] = matmul(split_ref[c * 256 : (c + 1) * 256, :], table_ref[...])
     for copy in loads:
         copy.wait()
     copies.append(start(p_ref, p_out, sems.at[1, 0]))
@@ -520,12 +555,13 @@
                 total = term if total is None else total + term
             rate_ref[n // 2, rows, (n % 2) * 128 : (n % 2) * 128 + 128] = total
         pltpu.make_async_copy(state_ref.at[i], state_out.at[:, rows, :], sems.at[2, i]).start()
+        pltpu.make_async_copy(rate_ref.at[:, rows, :], rate_out.at[:, rows, :], sems.at[3, i]).start()
         return carry
 
     lax.fori_loop(0, DEPTHS, body, 0)
-    copies.append(start(rate_ref, rate_out, sems.at[3, 0]))
     for i in range(DEPTHS):
         pltpu.make_async_copy(state_ref.at[i], state_out.at[:, rows_of(i), :], sems.at[2, i]).wait()
+        pltpu.make_async_copy(rate_ref.at[:, rows_of(i), :], rate_out.at[:, rows_of(i), :], sems.at[3, i]).wait()
     for copy in copies:
         copy.wait()
 
@@ -584,23 +620,24 @@
         edge_kernel,
         4,
         ((HBM, perm_table), (HBM, pressure), (HBM, zone_labels)),
-        [(VMEM, (2,) + rows)] * 2,
-        [table, buf(2, *rows, dtype=jnp.int32), DMA((5,))],
+        [(VMEM, (8, N))] * 2,
+        [table, buf(2, *rows, dtype=jnp.int32), buf(2, *rows), DMA((5,))],
     )
     before, after = shift(last, "slab", 1), shift(first, "slab", -1)
+    zones = zone_labels.reshape(2, DEPTHS, 8, N)
     root, p_copy, msg = call(
         lookup_kernel,
         8,
-        ((HBM, perm_table), (HBM, zone_labels), (HBM, pressure)),
-        [(VMEM, block)] * 2 + [(HBM, (DEPTHS, 11, 8, HALF))],
-        [table, buf(*block, dtype=jnp.int32), DMA((9,)), DMA((5, 8))],
+        ((HBM, perm_table), (HBM, zones), (HBM, pressure.reshape(2, DEPTHS, 8, N))),
+        [(VMEM, (DEPTHS,) + rows)] * 2 + [(HBM, (DEPTHS, 11, 8, HALF))],
+        [table, buf(2, DEPTHS, 8, N, dtype=jnp.int32), DMA((9,)), DMA((3, 8))],
     )
     (inv,) = call(
         strength_kernel,
         8,
-        ((HBM, asig_table), (HBM, zone_labels)),
+        ((HBM, asig_table), (HBM, zones)),
         [(HBM, block)],
-        [table, buf(*block, dtype=jnp.int32), buf(*block), DMA((9,)), DMA((8,))],
+        [table, buf(2, DEPTHS, 8, N, dtype=jnp.int32), buf(*block), DMA((9,))],
     )
 
     layer, offset = well_cells[:, 0], well_cells[:, 1] - (slab * ROWS + depth * 8)
@@ -648,7 +685,7 @@
          (HBM, tab["inner"]), (HBM, tab["inner_inv"]), (HBM, tab["col_twist"]), (VMEM, tab["in_twist"])),
         [(HBM, (256, 1024))],
         [buf(2, DEPTHS, STEP, LANES), buf(256, 1024), buf(256, 768, dtype=BF16), buf(256, 768, dtype=BF16),
-         buf(768, 256, dtype=BF16), buf(768, 256, dtype=BF16), buf(2, 8, STEP, LANES), DMA((12,))],
+         buf(768, 256, dtype=BF16), buf(768, 256, dtype=BF16), buf(2, 8, STEP, LANES), buf(768, 1024, dtype=BF16), DMA((12,))],
     )
     spec = lax.all_to_all(spec.reshape(SLABS, 8, 1024), "slab", 0, 0, tiled=True).reshape(256, 1024)
     layer_pos = (depth * 2 + jnp.arange(2, dtype=jnp.int32)).astype(F32)
@@ -660,7 +697,7 @@
          *[(ANY, v) for v in parts]),
         [(HBM, block)] * 2 + [(HBM, (DEPTHS, ROWS, 2 * LANES))],
         [buf(*block), buf(*block), buf(*block), buf(768, 256, dtype=BF16), buf(8, *rows),
-         buf(DEPTHS, ROWS, 2 * LANES), buf(1024, 256), DMA((5, 8))],
+         buf(DEPTHS, ROWS, 2 * LANES), buf(1024, 256), buf(1024, 768, dtype=BF16), DMA((5, 8))],
     )
     rate = lax.all_to_all(rate, "depth", 0, 0, tiled=True)
     (rate_map,) = call(sum_kernel, 4, [(VMEM, rate)], [(VMEM, (ROWS, 2 * LANES))])

time: 168 us -> 165 us (0.982)
  starting transfers between devices: 42.6 us -> 38.6 us
    all_to_all x1, starting transfers between devices: 14.6 us -> 10.5 us  [shards(): lax.all_to_all(spec.reshape(SLABS * DEPTHS, 8, LANES), ('slab', 'depth'),...]
  transfers between devices with their start and end apart: 12 -> 12, of which waited for: 6 -> 6; matrix products, arithmetic and copies ran while one was open for 9% -> 9% of each run, Pallas kernels for 6% -> 7%
where the time goes in v5:
time: 165 us
  waiting for transfers between devices  64.9 us (39%)
  starting transfers between devices  38.6 us (23%)
  Pallas kernels  29.8 us (18%)
  blocking collectives  15.9 us (10%)
  local copies, waits for them, and re-layouts  13.6 us (8%)
    all_to_all x1, waiting for transfers between devices, shards(): msg = lax.all_to_all(msg, 'depth', 0, 0, tiled=True)  35.2 us
    pallas_call x9, Pallas kernels, call(): pl.pallas_call(kernel, out_shape=[HBM(shape, F32) if space is HBM else ve...  29.8 us
    all_to_all x1, blocking collectives, shards(): rate = lax.all_to_all(rate, 'depth', 0, 0, tiled=True)  15.9 us
    all_to_all x1, waiting for transfers between devices, shards(): lax.all_to_all(spec.reshape(SLABS * DEPTHS, 8, LANES), ('slab', 'depth'),...  15.7 us
    ppermute x7, starting transfers between devices, rotate(): lax.ppermute(v, 'depth', [(i, (i + k) % DEPTHS) for i in range(DEPTHS)])  10.9 us
    all_to_all x1, starting transfers between devices, shards(): lax.all_to_all(spec.reshape(SLABS * DEPTHS, 8, LANES), ('slab', 'depth'),...  10.5 us
    ppermute x7, waiting for transfers between devices, rotate(): lax.ppermute(v, 'depth', [(i, (i + k) % DEPTHS) for i in range(DEPTHS)])  10.5 us
    reshape x2, local copies, waits for them, and re-layouts, shards(): (green_spectrum * (1.0 / (N * N))).reshape(8, 8, SLABS, FREQS, TILES)  7.01 us
  transfers between devices with their start and end apart: 12, of which 6 were waited for; matrix products, arithmetic and copies ran while one was open for 9% of the time, Pallas kernels for 7%

profile of v5, /device:TPU:2, one launch (start us, length us, event | category | flops | bytes accessed | tf_op | source)
XLA Modules:
  0.0 164.5 jit_solution(11312560835476595362)
XLA Ops:
  0.6 1.3 shard_map.185
  1.9 1.9 %collective-permute-start = (f32[8,2048]{1,0:T(8,128)S(1)}, f32[8,2048]{1,0:T(8,128)S(1)}, u32[]{:S(2)}, u32[]{:S(2)}) collective-permute-start(f32[8,2048]{1,0:T(8,128)S(1)} %get-tuple-element.24), channel_id=1, source_target_pairs={{0,8},{8,16},{16,24},{24,32},{32,40},{40,48},{48,56},{56,64},{64,7... | collective-permute-start | bytes 196616 | tf_op jit(solution)/shard_map/ppermute | solution.py:604
  3.9 3.6 %collective-permute-start.1 = (f32[8,2048]{1,0:T(8,128)S(1)}, f32[8,2048]{1,0:T(8,128)S(1)}, u32[]{:S(2)}, u32[]{:S(2)}) collective-permute-start(f32[8,2048]{1,0:T(8,128)S(1)} %get-tuple-element.25), channel_id=1, source_target_pairs={{8,0},{16,8},{24,16},{32,24},{40,32},{48,40},{56,48},{64,56},{72,6... | collective-permute-start | bytes 196616 | tf_op jit(solution)/shard_map/ppermute | solution.py:604
  7.5 4.3 %shard_map.184 = (f32[8,2,8,2048]{3,2,1,0:T(8,128)S(1)}, f32[8,2,8,2048]{3,2,1,0:T(8,128)S(1)}, f32[8,11,8,1024]{3,2,1,0:T(8,128)}) custom-call(f32[16]{0:T(128)} %perm_hbm.3, s32[2,8,8,2048]{3,2,1,0:T(8,128)} %bitcast.51, f32[2,8,8,2048]{3,2,1,0:T(8,128)} %bitcast.53), custom_call_target="tpu_custom_call" | custom-call | tf_op jit(solution)/shard_map/pallas_call | solution.py:586
  11.8 0.0 collective-permute-done.before_ref
  11.8 0.0 collective-permute-done.1.after_ref
  11.8 1.2 shard_map.186
  13.0 0.0 copy-start.4
  13.0 0.0 copy-start.5
  13.0 0.0 copy-start.1
  13.0 6.2 %all-to-all-start = ((f32[8,11,8,1024]{3,2,1,0:T(8,128)}), f32[8,11,8,1024]{3,2,1,0:T(8,128)S(1)}, u32[]{:S(2)}, u32[]{:S(2)}) async-start(f32[8,11,8,1024]{3,2,1,0:T(8,128)} %shard_map.186), calls=%async_computation | async-start | bytes 5767168 | tf_op jit(solution)/shard_map/all_to_all | solution.py:669
  19.2 0.0 copy-done.4
  19.2 0.1 copy.25.col_ref
  19.4 0.0 copy-done.5
  19.5 2.5 %shard_map.187 = (f32[192,2048]{1,0:T(8,128)}, f32[128,2048]{1,0:T(8,128)}) custom-call(s32[1,512]{1,0:T(1,128)S(1)} %get-tuple-element.42.where1_ref, s32[1,512]{1,0:T(1,128)S(1)} %get-tuple-element.41.where2_ref, f32[2,512]{1,0:T(2,128)S(1)} %convert_multiply_fusion.amount_ref, s32[512,1]{1,0:T(8,128)S(1)} %copy.25.col_ref), custom_call_target="tpu_custom_call" | custom-call | tf_op jit(solution)/shard_map/pallas_call | solution.py:586
  22.0 35.2 %all-to-all-done.msg_ref = f32[8,11,8,1024]{3,2,1,0:T(8,128)S(1)} async-done(((f32[8,11,8,1024]{3,2,1,0:T(8,128)}), f32[8,11,8,1024]{3,2,1,0:T(8,128)S(1)}, u32[]{:S(2)}, u32[]{:S(2)}) %all-to-all-start) | async-done | bytes 2883616 | tf_op jit(solution)/shard_map/all_to_all | solution.py:669
  57.1 0.0 copy-done.1
  57.1 6.3 %shard_map.188 = (f32[2,8,2048]{2,1,0:T(8,128)}, f32[2,8,2048]{2,1,0:T(8,128)}, f32[2,8,2048]{2,1,0:T(8,128)}, f32[2,8,2048]{2,1,0:T(8,128)}, f32[2,8,2048]{2,1,...) custom-call(s32[1]{0:T(128)} %bitcast.me_ref, ...), custom_call_target="tpu_custom_call" | custom-call | tf_op jit(solution)/shard_map/pallas_call | solution.py:586
  63.4 10.5 %all-to-all-start.1 = ((f32[256,8,128]{2,1,0:T(8,128)}), f32[256,8,128]{2,1,0:T(8,128)S(1)}, u32[]{:S(2)}, u32[]{:S(2)}) async-start(f32[256,8,128]{2,1,0:T(8,128)} %bitcast.56), calls=%async_computation.1 | async-start | bytes 2097152 | tf_op jit(solution)/shard_map/all_to_all | solution.py:679
  73.9 0.0 copy-done.3
  73.9 0.8 broadcast_multiply_fusion
  74.8 1.8 %reshape.251 = f32[8,8,32,4,16]{2,1,0,4,3:T(8,128)S(1)} reshape(f32[2048,64]{0,1:T(8,128)} %broadcast_multiply_fusion) | data formatting | bytes 1048576 | tf_op jit(solution)/shard_map/reshape | solution.py:658
  76.6 5.2 %copy.24 = f32[8,8,32,4,16]{0,4,3,2,1:T(8,128)} copy(f32[8,8,32,4,16]{2,1,0,4,3:T(8,128)S(1)} %reshape.251) | data formatting | bytes 1048576 | tf_op jit(solution)/shard_map/reshape | solution.py:658
  81.8 6.4 %reshape.252.green_ref = f32[8,128,128]{2,1,0:T(8,128)S(1)} reshape(f32[8,32,4,16,8]{4,3,2,1,0:T(8,128)} %bitcast.50) | data formatting | bytes 1048576 | tf_op jit(solution)/shard_map/reshape | solution.py:659
  88.2 15.7 %all-to-all-done.1 = f32[256,8,128]{2,1,0:T(8,128)S(1)} async-done(((f32[256,8,128]{2,1,0:T(8,128)}), f32[256,8,128]{2,1,0:T(8,128)S(1)}, u32[]{:S(2)}, u32[]{:S(2)}) %all-to-all-start.1) | async-done | bytes 1048608 | tf_op jit(solution)/shard_map/all_to_all | solution.py:679
  104.0 5.5 %shard_map.189 = f32[256,1024]{1,0:T(8,128)} custom-call(f32[32,8,8,128]{3,2,1,0:T(8,128)S(1)} %bitcast.49, f32[8,128,128]{2,1,0:T(8,128)S(1)} %reshape.252.green_ref, bf16[256,768]{1,0:T(8,128)(2,1)} %constant.98.clone.mid_hbm, bf16[256,768]{1,0:T(8,128)(2,1)} %constant.99.clone.mid_inv_hbm, bf16[768,256]{1,0:T(8,128)(2,1)} %constant.100.clone.inner_hbm, ...), custom_call_target="tpu_custom_call" | custom-call | tf_op jit(solution)/shard_map/pallas_call | solution.py:586
  109.5 5.4 %all-to-all-start.2 = ((f32[32,8,1024]{2,1,0:T(8,128)}), f32[32,8,1024]{2,1,0:T(8,128)S(1)}, u32[]{:S(2)}, u32[]{:S(2)}) async-start(f32[32,8,1024]{2,1,0:T(8,128)} %bitcast.54), calls=%async_computation.2 | async-start | bytes 2097152 | tf_op jit(solution)/shard_map/all_to_all | solution.py:690
  114.9 1.6 collective-permute-start.2
  116.5 0.7 collective-permute-start.3
  117.2 2.8 %collective-permute-start.4 = (f32[2,8,2048]{2,1,0:T(8,128)S(1)}, f32[2,8,2048]{2,1,0:T(8,128)S(1)}, u32[]{:S(2)}, u32[]{:S(2)}) collective-permute-start(f32[2,8,2048]{2,1,0:T(8,128)S(1)} %copy-done.10), channel_id=1, source_target_pairs={{0,3},{1,4},{2,5},{3,6},{4,7},{5,0},{6,1},{7,2},{8,11},{9,12},{10,... | collective-permute-start | bytes 393224 | tf_op jit(solution)/shard_map/ppermute | solution.py:608
  120.0 2.8 %collective-permute-start.5 = (f32[2,8,2048]{2,1,0:T(8,128)S(1)}, f32[2,8,2048]{2,1,0:T(8,128)S(1)}, u32[]{:S(2)}, u32[]{:S(2)}) collective-permute-start(f32[2,8,2048]{2,1,0:T(8,128)S(1)} %copy-done.9), channel_id=1, source_target_pairs={{0,4},{1,5},{2,6},{3,7},{4,0},{5,1},{6,2},{7,3},{8,12},{9,13},{10,... | collective-permute-start | bytes 393224 | tf_op jit(solution)/shard_map/ppermute | solution.py:608
  122.9 0.0 copy-done.8
  122.9 2.8 %collective-permute-start.6 = (f32[2,8,2048]{2,1,0:T(8,128)S(1)}, f32[2,8,2048]{2,1,0:T(8,128)S(1)}, u32[]{:S(2)}, u32[]{:S(2)}) collective-permute-start(f32[2,8,2048]{2,1,0:T(8,128)S(1)} %copy-done.8), channel_id=1, source_target_pairs={{0,5},{1,6},{2,7},{3,0},{4,1},{5,2},{6,3},{7,4},{8,13},{9,14},{10,... | collective-permute-start | bytes 393224 | tf_op jit(solution)/shard_map/ppermute | solution.py:608
  125.7 3.9 %collective-permute-done.2.rest_1_ = f32[2,8,2048]{2,1,0:T(8,128)S(1)} collective-permute-done((f32[2,8,2048]{2,1,0:T(8,128)S(1)}, f32[2,8,2048]{2,1,0:T(8,128)S(1)}, u32[]{:S(2)}, u32[]{:S(2)}) %collective-permute-start.2) | collective-permute-done | bytes 131104 | tf_op jit(solution)/shard_map/ppermute | solution.py:608
  129.6 0.0 copy-done.7
  129.6 0.0 collective-permute-start.7
  129.6 0.0 collective-permute-done.3.rest_2_
  129.6 0.1 collective-permute-start.8
  129.7 4.0 %shard_map.190.inv_hbm = f32[2,64,2048]{2,1,0:T(8,128)} custom-call(f32[16]{0:T(128)} %asig_hbm.1, s32[2,8,8,2048]{3,2,1,0:T(8,128)} %bitcast.52), custom_call_target="tpu_custom_call" | custom-call | tf_op jit(solution)/shard_map/pallas_call | solution.py:586
  133.8 0.0 collective-permute-done.4.rest_3_
  133.8 0.0 collective-permute-done.5.rest_4_
  133.8 4.0 %collective-permute-done.6.rest_5_ = f32[2,8,2048]{2,1,0:T(8,128)S(1)} collective-permute-done((f32[2,8,2048]{2,1,0:T(8,128)S(1)}, f32[2,8,2048]{2,1,0:T(8,128)S(1)}, u32[]{:S(2)}, u32[]{:S(2)}) %collective-permute-start.6) | collective-permute-done | bytes 131104 | tf_op jit(solution)/shard_map/ppermute | solution.py:608
  137.8 0.0 collective-permute-done.7.rest_6_
  137.9 2.6 %collective-permute-done.8.rest_7_ = f32[2,8,2048]{2,1,0:T(8,128)S(1)} collective-permute-done((f32[2,8,2048]{2,1,0:T(8,128)S(1)}, f32[2,8,2048]{2,1,0:T(8,128)S(1)}, u32[]{:S(2)}, u32[]{:S(2)}) %collective-permute-start.8) | collective-permute-done | bytes 131104 | tf_op jit(solution)/shard_map/ppermute | solution.py:608
  140.4 3.5 %all-to-all-done.2 = f32[32,8,1024]{2,1,0:T(8,128)S(1)} async-done(((f32[32,8,1024]{2,1,0:T(8,128)}), f32[32,8,1024]{2,1,0:T(8,128)S(1)}, u32[]{:S(2)}, u32[]{:S(2)}) %all-to-all-start.2) | async-done | bytes 1048608 | tf_op jit(solution)/shard_map/all_to_all | solution.py:690
  143.9 4.1 %shard_map.191 = (f32[2,64,2048]{2,1,0:T(8,128)}, f32[2,64,2048]{2,1,0:T(8,128)}, f32[8,64,256]{2,1,0:T(8,128)}) custom-call(s32[1]{0:T(128)} %bitcast.me_ref, f32[2]{0:T(128)S(1)} %add_multiply_fusion.weight_ref, f32[256,1024]{1,0:T(8,128)S(1)} %bitcast.48, f32[2,64,2048]{2,1,0:T(8,128)} %shard_map.190.inv_hbm, f32[2,64,2048]{2,1,0:T(8,128)} %seis_hbm.1, ...), custom_call_target="tpu_custom_call" | custom-call | tf_op jit(solution)/shard_map/pallas_call | solution.py:586
  148.0 15.9 %all_to_all.20.part_ref = f32[8,64,256]{2,1,0:T(8,128)S(1)} all-to-all(f32[8,64,256]{2,1,0:T(8,128)} %get-tuple-element.40), channel_id=1, replica_groups=mesh['slab'=32,'depth'=8] {'depth'}, dimensions={0} | all-to-all | bytes 1048576 | tf_op jit(solution)/shard_map/all_to_all | solution.py:702
  163.9 0.7 shard_map.192
  (21 shorter events, 0.1 us)
Async XLA Ops:
  1.9 9.9 %collective-permute-start = (f32[8,2048]{1,0:T(8,128)S(1)}, f32[8,2048]{1,0:T(8,128)S(1)}, u32[]{:S(2)}, u32[]{:S(2)}) collective-permute-start(f32[8,2048]{1,0:T(8,128)S(1)} %get-tuple-element.24), channel_id=1, source_target_pairs={{0,8},{8,16},{16,24},{24,32},{32,40},{40,48},{48,56},{56,64},{64,7... | collective-permute-start | bytes 196616 | tf_op jit(solution)/shard_map/ppermute | solution.py:604
  3.9 7.9 %collective-permute-start.1 = (f32[8,2048]{1,0:T(8,128)S(1)}, f32[8,2048]{1,0:T(8,128)S(1)}, u32[]{:S(2)}, u32[]{:S(2)}) collective-permute-start(f32[8,2048]{1,0:T(8,128)S(1)} %get-tuple-element.25), channel_id=1, source_target_pairs={{8,0},{16,8},{24,16},{32,24},{40,32},{48,40},{56,48},{64,56},{72,6... | collective-permute-start | bytes 196616 | tf_op jit(solution)/shard_map/ppermute | solution.py:604
  13.0 6.2 %copy-start.4 = (s32[512,3]{0,1:T(4,128)S(1)}, s32[512,3]{0,1:T(4,128)}, u32[]{:S(2)}) copy-start(s32[512,3]{0,1:T(4,128)} %param.21) | copy-start | bytes 18436
  13.0 6.4 %copy-start.5 = (s32[2,512]{1,0:T(2,128)S(1)}, s32[2,512]{1,0:T(2,128)}, u32[]{:S(2)}) copy-start(s32[2,512]{1,0:T(2,128)} %param.22) | copy-start | bytes 12292
  13.0 44.1 %copy-start.1 = (f32[2,16,128]{2,1,0:T(8,128)S(1)}, f32[2,16,128]{2,1,0:T(8,128)}, u32[]{:S(2)}) copy-start(f32[2,16,128]{2,1,0:T(8,128)} %constant.102.clone.twist_ref) | copy-start | bytes 49156
  13.0 44.1 %all-to-all-start = ((f32[8,11,8,1024]{3,2,1,0:T(8,128)}), f32[8,11,8,1024]{3,2,1,0:T(8,128)S(1)}, u32[]{:S(2)}, u32[]{:S(2)}) async-start(f32[8,11,8,1024]{3,2,1,0:T(8,128)} %shard_map.186), calls=%async_computation | async-start | bytes 5767168 | tf_op jit(solution)/shard_map/all_to_all | solution.py:669
  57.1 16.8 %copy-start.3 = (f32[2048,64]{0,1:T(8,128)S(1)}, f32[2048,64]{0,1:T(8,128)}, u32[]{:S(2)}) copy-start(f32[2048,64]{0,1:T(8,128)} %param.23) | copy-start | bytes 1572868
  63.4 40.5 %all-to-all-start.1 = ((f32[256,8,128]{2,1,0:T(8,128)}), f32[256,8,128]{2,1,0:T(8,128)S(1)}, u32[]{:S(2)}, u32[]{:S(2)}) async-start(f32[256,8,128]{2,1,0:T(8,128)} %bitcast.56), calls=%async_computation.1 | async-start | bytes 2097152 | tf_op jit(solution)/shard_map/all_to_all | solution.py:679
  81.8 22.1 %copy-start.2 = (f32[2,8,128]{2,1,0:T(8,128)S(1)}, f32[2,8,128]{2,1,0:T(8,128)}, u32[]{:S(2)}) copy-start(f32[2,8,128]{2,1,0:T(8,128)} %constant.104.clone.in_ref) | copy-start | bytes 24580
  103.9 10.9 %copy-start.12 = (f32[2,8,2048]{2,1,0:T(8,128)S(1)}, f32[2,8,2048]{2,1,0:T(8,128)}, u32[]{:S(2)}) copy-start(f32[2,8,2048]{2,1,0:T(8,128)} %get-tuple-element.31) | copy-start | bytes 393220
  103.9 12.6 %copy-start.11 = (f32[2,8,2048]{2,1,0:T(8,128)S(1)}, f32[2,8,2048]{2,1,0:T(8,128)}, u32[]{:S(2)}) copy-start(f32[2,8,2048]{2,1,0:T(8,128)} %get-tuple-element.32) | copy-start | bytes 393220
  103.9 13.3 %copy-start.10 = (f32[2,8,2048]{2,1,0:T(8,128)S(1)}, f32[2,8,2048]{2,1,0:T(8,128)}, u32[]{:S(2)}) copy-start(f32[2,8,2048]{2,1,0:T(8,128)} %get-tuple-element.33) | copy-start | bytes 393220
  103.9 16.1 %copy-start.9 = (f32[2,8,2048]{2,1,0:T(8,128)S(1)}, f32[2,8,2048]{2,1,0:T(8,128)}, u32[]{:S(2)}) copy-start(f32[2,8,2048]{2,1,0:T(8,128)} %get-tuple-element.34) | copy-start | bytes 393220
  103.9 19.0 %copy-start.8 = (f32[2,8,2048]{2,1,0:T(8,128)S(1)}, f32[2,8,2048]{2,1,0:T(8,128)}, u32[]{:S(2)}) copy-start(f32[2,8,2048]{2,1,0:T(8,128)} %get-tuple-element.35) | copy-start | bytes 393220
  104.0 25.7 %copy-start.7 = (f32[2,8,2048]{2,1,0:T(8,128)S(1)}, f32[2,8,2048]{2,1,0:T(8,128)}, u32[]{:S(2)}) copy-start(f32[2,8,2048]{2,1,0:T(8,128)} %get-tuple-element.36) | copy-start | bytes 393220
  104.0 25.7 %copy-start.6 = (f32[2,8,2048]{2,1,0:T(8,128)S(1)}, f32[2,8,2048]{2,1,0:T(8,128)}, u32[]{:S(2)}) copy-start(f32[2,8,2048]{2,1,0:T(8,128)} %get-tuple-element.37) | copy-start | bytes 393220
  109.5 34.4 %copy-start = (f32[2,8,2048]{2,1,0:T(8,128)S(1)}, f32[2,8,2048]{2,1,0:T(8,128)}, u32[]{:S(2)}) copy-start(f32[2,8,2048]{2,1,0:T(8,128)} %get-tuple-element.30.rest_0_) | copy-start | bytes 393220
  109.5 34.4 %all-to-all-start.2 = ((f32[32,8,1024]{2,1,0:T(8,128)}), f32[32,8,1024]{2,1,0:T(8,128)S(1)}, u32[]{:S(2)}, u32[]{:S(2)}) async-start(f32[32,8,1024]{2,1,0:T(8,128)} %bitcast.54), calls=%async_computation.2 | async-start | bytes 2097152 | tf_op jit(solution)/shard_map/all_to_all | solution.py:690
  114.9 14.8 %collective-permute-start.2 = (f32[2,8,2048]{2,1,0:T(8,128)S(1)}, f32[2,8,2048]{2,1,0:T(8,128)S(1)}, u32[]{:S(2)}, u32[]{:S(2)}) collective-permute-start(f32[2,8,2048]{2,1,0:T(8,128)S(1)} %copy-done.12), channel_id=1, source_target_pairs={{0,1},{1,2},{2,3},{3,4},{4,5},{5,6},{6,7},{7,0},{8,9},{9,10},{10,1... | collective-permute-start | bytes 393224 | tf_op jit(solution)/shard_map/ppermute | solution.py:608
  116.5 13.1 %collective-permute-start.3 = (f32[2,8,2048]{2,1,0:T(8,128)S(1)}, f32[2,8,2048]{2,1,0:T(8,128)S(1)}, u32[]{:S(2)}, u32[]{:S(2)}) collective-permute-start(f32[2,8,2048]{2,1,0:T(8,128)S(1)} %copy-done.11), channel_id=1, source_target_pairs={{0,2},{1,3},{2,4},{3,5},{4,6},{5,7},{6,0},{7,1},{8,10},{9,11},{10,... | collective-permute-start | bytes 393224 | tf_op jit(solution)/shard_map/ppermute | solution.py:608
  117.2 16.6 %collective-permute-start.4 = (f32[2,8,2048]{2,1,0:T(8,128)S(1)}, f32[2,8,2048]{2,1,0:T(8,128)S(1)}, u32[]{:S(2)}, u32[]{:S(2)}) collective-permute-start(f32[2,8,2048]{2,1,0:T(8,128)S(1)} %copy-done.10), channel_id=1, source_target_pairs={{0,3},{1,4},{2,5},{3,6},{4,7},{5,0},{6,1},{7,2},{8,11},{9,12},{10,... | collective-permute-start | bytes 393224 | tf_op jit(solution)/shard_map/ppermute | solution.py:608
  120.0 13.8 %collective-permute-start.5 = (f32[2,8,2048]{2,1,0:T(8,128)S(1)}, f32[2,8,2048]{2,1,0:T(8,128)S(1)}, u32[]{:S(2)}, u32[]{:S(2)}) collective-permute-start(f32[2,8,2048]{2,1,0:T(8,128)S(1)} %copy-done.9), channel_id=1, source_target_pairs={{0,4},{1,5},{2,6},{3,7},{4,0},{5,1},{6,2},{7,3},{8,12},{9,13},{10,... | collective-permute-start | bytes 393224 | tf_op jit(solution)/shard_map/ppermute | solution.py:608
  122.9 15.0 %collective-permute-start.6 = (f32[2,8,2048]{2,1,0:T(8,128)S(1)}, f32[2,8,2048]{2,1,0:T(8,128)S(1)}, u32[]{:S(2)}, u32[]{:S(2)}) collective-permute-start(f32[2,8,2048]{2,1,0:T(8,128)S(1)} %copy-done.8), channel_id=1, source_target_pairs={{0,5},{1,6},{2,7},{3,0},{4,1},{5,2},{6,3},{7,4},{8,13},{9,14},{10,... | collective-permute-start | bytes 393224 | tf_op jit(solution)/shard_map/ppermute | solution.py:608
  129.6 8.2 %collective-permute-start.7 = (f32[2,8,2048]{2,1,0:T(8,128)S(1)}, f32[2,8,2048]{2,1,0:T(8,128)S(1)}, u32[]{:S(2)}, u32[]{:S(2)}) collective-permute-start(f32[2,8,2048]{2,1,0:T(8,128)S(1)} %copy-done.7), channel_id=1, source_target_pairs={{0,6},{1,7},{2,0},{3,1},{4,2},{5,3},{6,4},{7,5},{8,14},{9,15},{10,... | collective-permute-start | bytes 393224 | tf_op jit(solution)/shard_map/ppermute | solution.py:608
  129.6 10.8 %collective-permute-start.8 = (f32[2,8,2048]{2,1,0:T(8,128)S(1)}, f32[2,8,2048]{2,1,0:T(8,128)S(1)}, u32[]{:S(2)}, u32[]{:S(2)}) collective-permute-start(f32[2,8,2048]{2,1,0:T(8,128)S(1)} %copy-done.6), channel_id=1, source_target_pairs={{0,7},{1,0},{2,1},{3,2},{4,3},{5,4},{6,5},{7,6},{8,15},{9,8},{10,9... | collective-permute-start | bytes 393224 | tf_op jit(solution)/shard_map/ppermute | solution.py:608

commit v6 on v5

--- a/solution.py
+++ b/solution.py
@@ -187,9 +187,10 @@
         out[...] = packed
 
 
-def each_part(label_hbm, label, sems, work, done):
+def each_part(label_hbm, label, sems, before, work, done):
     parts = [pl.ds(g * 2, 2) for g in range(4)]
     loads = [start(label_hbm.at[:, at], label.at[:, at], sems.at[g]) for g, at in enumerate(parts)]
+    values = before()
     width = 1024
     for g in range(4):
         loads[g].wait()
@@ -198,7 +199,7 @@
             d = g * 2 + n // 2
             cols = pl.ds(pl.multiple_of(n % 2 * width, width), width)
             for l in range(2):
-                work(label[l, d, :, cols], d, l, cols)
+                work(values, label[l, d, :, cols], d, l, cols)
             return carry
 
         lax.fori_loop(0, 4, body, 0)
@@ -207,38 +208,44 @@
 
 def lookup_kernel(perm_hbm, label_hbm, p_hbm, root_out, p_out, msg_hbm, perm_ref, label, sems, msg_sems):
     table = start(perm_hbm, perm_ref, sems.at[8])
-    loads = [start(p_hbm.at[l], p_out.at[:, l], msg_sems.at[2, l]) for l in range(2)]
-    copies = []
-
-    def work(zone, d, l, cols):
+    loads, copies = [], []
+
+    def work(values, zone, d, l, cols):
         root_out[d, l, :, cols] = pick(zone, values)
 
     def done(g):
+        if g == 1:
+            for copy in loads:
+                copy.wait()
         for h in range(2):
             at = slice(h * HALF, (h + 1) * HALF)
-            if g == 0:
-                loads[h].wait()
             if g == 1:
                 copies.append(start(p_out.at[:, :, :, at], msg_hbm.at[:, h * 2 : h * 2 + 2], msg_sems.at[h, 7]))
             if g % 2:
                 rows = pl.ds(g * 2 - 2, 4)
                 copies.append(start(root_out.at[rows, :, :, at], msg_hbm.at[rows, h * 2 + 4 : h * 2 + 6], msg_sems.at[h, g]))
 
-    table.wait()
-    values = table_tiles(perm_ref, jnp.sqrt)
-    each_part(label_hbm, label, sems, work, done)
+    def before():
+        loads.extend(start(p_hbm.at[l], p_out.at[:, l], msg_sems.at[2, l]) for l in range(2))
+        table.wait()
+        return table_tiles(perm_ref, jnp.sqrt)
+
+    each_part(label_hbm, label, sems, before, work, done)
     for copy in copies:
         copy.wait()
 
 
 def strength_kernel(asig_hbm, label_hbm, inv_hbm, asig_ref, label, inv, sems):
-    start(asig_hbm, asig_ref, sems.at[8]).wait()
-    values = table_tiles(asig_ref, lambda x: 1.0 / x)
-
-    def work(zone, d, l, cols):
+    table = start(asig_hbm, asig_ref, sems.at[8])
+
+    def work(values, zone, d, l, cols):
         inv[l, rows_of(d), cols] = pick(zone, values)
 
-    each_part(label_hbm, label, sems, work, lambda g: None)
+    def before():
+        table.wait()
+        return table_tiles(asig_ref, lambda x: 1.0 / x)
+
+    each_part(label_hbm, label, sems, before, work, lambda g: None)
     start(inv, inv_hbm, sems.at[8]).wait()
 
 

time: 165 us -> 165 us (level)
  transfers between devices with their start and end apart: 12 -> 12, of which waited for: 6 -> 6; matrix products, arithmetic and copies ran while one was open for 9% -> 9% of each run, Pallas kernels for 7% -> 6%
where the time goes in v6:
time: 165 us
  waiting for transfers between devices  65.6 us (40%)
  starting transfers between devices  39.4 us (24%)
  Pallas kernels  28.2 us (17%)
  blocking collectives  15.9 us (10%)
  local copies, waits for them, and re-layouts  13.6 us (8%)
    all_to_all x1, waiting for transfers between devices, shards(): msg = lax.all_to_all(msg, 'depth', 0, 0, tiled=True)  35.2 us
    pallas_call x9, Pallas kernels, call(): pl.pallas_call(kernel, out_shape=[HBM(shape, F32) if space is HBM else ve...  28.2 us
    all_to_all x1, blocking collectives, shards(): rate = lax.all_to_all(rate, 'depth', 0, 0, tiled=True)  15.9 us
    all_to_all x1, waiting for transfers between devices, shards(): lax.all_to_all(spec.reshape(SLABS * DEPTHS, 8, LANES), ('slab', 'depth'),...  15.7 us
    all_to_all x1, starting transfers between devices, shards(): lax.all_to_all(spec.reshape(SLABS * DEPTHS, 8, LANES), ('slab', 'depth'),...  11.4 us
    ppermute x7, waiting for transfers between devices, rotate(): lax.ppermute(v, 'depth', [(i, (i + k) % DEPTHS) for i in range(DEPTHS)])  11.2 us
    ppermute x7, starting transfers between devices, rotate(): lax.ppermute(v, 'depth', [(i, (i + k) % DEPTHS) for i in range(DEPTHS)])  10.9 us
    reshape x2, local copies, waits for them, and re-layouts, shards(): (green_spectrum * (1.0 / (N * N))).reshape(8, 8, SLABS, FREQS, TILES)  7.01 us
  transfers between devices with their start and end apart: 12, of which 6 were waited for; matrix products, arithmetic and copies ran while one was open for 9% of the time, Pallas kernels for 6%

profile of v6, /device:TPU:2, one launch (start us, length us, event | category | flops | bytes accessed | tf_op | source)
XLA Modules:
  0.0 164.5 jit_solution(2100001560613396009)
XLA Ops:
  0.6 1.3 shard_map.185
  1.9 1.9 %collective-permute-start = (f32[8,2048]{1,0:T(8,128)S(1)}, f32[8,2048]{1,0:T(8,128)S(1)}, u32[]{:S(2)}, u32[]{:S(2)}) collective-permute-start(f32[8,2048]{1,0:T(8,128)S(1)} %get-tuple-element.24), channel_id=1, source_target_pairs={{0,8},{8,16},{16,24},{24,32},{32,40},{40,48},{48,56},{56,64},{64,7... | collective-permute-start | bytes 196616 | tf_op jit(solution)/shard_map/ppermute | solution.py:611
  3.9 3.6 %collective-permute-start.1 = (f32[8,2048]{1,0:T(8,128)S(1)}, f32[8,2048]{1,0:T(8,128)S(1)}, u32[]{:S(2)}, u32[]{:S(2)}) collective-permute-start(f32[8,2048]{1,0:T(8,128)S(1)} %get-tuple-element.25), channel_id=1, source_target_pairs={{8,0},{16,8},{24,16},{32,24},{40,32},{48,40},{56,48},{64,56},{72,6... | collective-permute-start | bytes 196616 | tf_op jit(solution)/shard_map/ppermute | solution.py:611
  7.5 3.4 %shard_map.184 = (f32[8,2,8,2048]{3,2,1,0:T(8,128)S(1)}, f32[8,2,8,2048]{3,2,1,0:T(8,128)S(1)}, f32[8,11,8,1024]{3,2,1,0:T(8,128)}) custom-call(f32[16]{0:T(128)} %perm_hbm.3, s32[2,8,8,2048]{3,2,1,0:T(8,128)} %bitcast.51, f32[2,8,8,2048]{3,2,1,0:T(8,128)} %bitcast.53), custom_call_target="tpu_custom_call" | custom-call | tf_op jit(solution)/shard_map/pallas_call | solution.py:593
  10.9 0.0 collective-permute-done.before_ref
  10.9 0.0 collective-permute-done.1.after_ref
  10.9 1.2 shard_map.186
  12.1 0.0 copy-start.4
  12.1 0.0 copy-start.5
  12.1 0.0 copy-start.1
  12.2 6.2 %all-to-all-start = ((f32[8,11,8,1024]{3,2,1,0:T(8,128)}), f32[8,11,8,1024]{3,2,1,0:T(8,128)S(1)}, u32[]{:S(2)}, u32[]{:S(2)}) async-start(f32[8,11,8,1024]{3,2,1,0:T(8,128)} %shard_map.186), calls=%async_computation | async-start | bytes 5767168 | tf_op jit(solution)/shard_map/all_to_all | solution.py:676
  18.3 0.0 copy-done.4
  18.4 0.1 copy.25.col_ref
  18.5 0.0 copy-done.5
  18.6 2.5 %shard_map.187 = (f32[192,2048]{1,0:T(8,128)}, f32[128,2048]{1,0:T(8,128)}) custom-call(s32[1,512]{1,0:T(1,128)S(1)} %get-tuple-element.42.where1_ref, s32[1,512]{1,0:T(1,128)S(1)} %get-tuple-element.41.where2_ref, f32[2,512]{1,0:T(2,128)S(1)} %convert_multiply_fusion.amount_ref, s32[512,1]{1,0:T(8,128)S(1)} %copy.25.col_ref), custom_call_target="tpu_custom_call" | custom-call | tf_op jit(solution)/shard_map/pallas_call | solution.py:593
  21.1 35.2 %all-to-all-done.msg_ref = f32[8,11,8,1024]{3,2,1,0:T(8,128)S(1)} async-done(((f32[8,11,8,1024]{3,2,1,0:T(8,128)}), f32[8,11,8,1024]{3,2,1,0:T(8,128)S(1)}, u32[]{:S(2)}, u32[]{:S(2)}) %all-to-all-start) | async-done | bytes 2883616 | tf_op jit(solution)/shard_map/all_to_all | solution.py:676
  56.3 0.0 copy-done.1
  56.3 6.3 %shard_map.188 = (f32[2,8,2048]{2,1,0:T(8,128)}, f32[2,8,2048]{2,1,0:T(8,128)}, f32[2,8,2048]{2,1,0:T(8,128)}, f32[2,8,2048]{2,1,0:T(8,128)}, f32[2,8,2048]{2,1,...) custom-call(s32[1]{0:T(128)} %bitcast.me_ref, ...), custom_call_target="tpu_custom_call" | custom-call | tf_op jit(solution)/shard_map/pallas_call | solution.py:593
  62.6 11.4 %all-to-all-start.1 = ((f32[256,8,128]{2,1,0:T(8,128)}), f32[256,8,128]{2,1,0:T(8,128)S(1)}, u32[]{:S(2)}, u32[]{:S(2)}) async-start(f32[256,8,128]{2,1,0:T(8,128)} %bitcast.56), calls=%async_computation.1 | async-start | bytes 2097152 | tf_op jit(solution)/shard_map/all_to_all | solution.py:686
  73.9 0.0 copy-done.3
  73.9 0.8 broadcast_multiply_fusion
  74.8 1.8 %reshape.251 = f32[8,8,32,4,16]{2,1,0,4,3:T(8,128)S(1)} reshape(f32[2048,64]{0,1:T(8,128)} %broadcast_multiply_fusion) | data formatting | bytes 1048576 | tf_op jit(solution)/shard_map/reshape | solution.py:665
  76.6 5.2 %copy.24 = f32[8,8,32,4,16]{0,4,3,2,1:T(8,128)} copy(f32[8,8,32,4,16]{2,1,0,4,3:T(8,128)S(1)} %reshape.251) | data formatting | bytes 1048576 | tf_op jit(solution)/shard_map/reshape | solution.py:665
  81.8 6.4 %reshape.252.green_ref = f32[8,128,128]{2,1,0:T(8,128)S(1)} reshape(f32[8,32,4,16,8]{4,3,2,1,0:T(8,128)} %bitcast.50) | data formatting | bytes 1048576 | tf_op jit(solution)/shard_map/reshape | solution.py:666
  88.2 15.7 %all-to-all-done.1 = f32[256,8,128]{2,1,0:T(8,128)S(1)} async-done(((f32[256,8,128]{2,1,0:T(8,128)}), f32[256,8,128]{2,1,0:T(8,128)S(1)}, u32[]{:S(2)}, u32[]{:S(2)}) %all-to-all-start.1) | async-done | bytes 1048608 | tf_op jit(solution)/shard_map/all_to_all | solution.py:686
  104.0 5.5 %shard_map.189 = f32[256,1024]{1,0:T(8,128)} custom-call(f32[32,8,8,128]{3,2,1,0:T(8,128)S(1)} %bitcast.49, f32[8,128,128]{2,1,0:T(8,128)S(1)} %reshape.252.green_ref, bf16[256,768]{1,0:T(8,128)(2,1)} %constant.98.clone.mid_hbm, bf16[256,768]{1,0:T(8,128)(2,1)} %constant.99.clone.mid_inv_hbm, bf16[768,256]{1,0:T(8,128)(2,1)} %constant.100.clone.inner_hbm, ...), custom_call_target="tpu_custom_call" | custom-call | tf_op jit(solution)/shard_map/pallas_call | solution.py:593
  109.5 5.4 %all-to-all-start.2 = ((f32[32,8,1024]{2,1,0:T(8,128)}), f32[32,8,1024]{2,1,0:T(8,128)S(1)}, u32[]{:S(2)}, u32[]{:S(2)}) async-start(f32[32,8,1024]{2,1,0:T(8,128)} %bitcast.54), calls=%async_computation.2 | async-start | bytes 2097152 | tf_op jit(solution)/shard_map/all_to_all | solution.py:697
  114.9 1.6 collective-permute-start.2
  116.5 0.7 collective-permute-start.3
  117.2 2.8 %collective-permute-start.4 = (f32[2,8,2048]{2,1,0:T(8,128)S(1)}, f32[2,8,2048]{2,1,0:T(8,128)S(1)}, u32[]{:S(2)}, u32[]{:S(2)}) collective-permute-start(f32[2,8,2048]{2,1,0:T(8,128)S(1)} %copy-done.10), channel_id=1, source_target_pairs={{0,3},{1,4},{2,5},{3,6},{4,7},{5,0},{6,1},{7,2},{8,11},{9,12},{10,... | collective-permute-start | bytes 393224 | tf_op jit(solution)/shard_map/ppermute | solution.py:615
  120.0 2.8 %collective-permute-start.5 = (f32[2,8,2048]{2,1,0:T(8,128)S(1)}, f32[2,8,2048]{2,1,0:T(8,128)S(1)}, u32[]{:S(2)}, u32[]{:S(2)}) collective-permute-start(f32[2,8,2048]{2,1,0:T(8,128)S(1)} %copy-done.9), channel_id=1, source_target_pairs={{0,4},{1,5},{2,6},{3,7},{4,0},{5,1},{6,2},{7,3},{8,12},{9,13},{10,... | collective-permute-start | bytes 393224 | tf_op jit(solution)/shard_map/ppermute | solution.py:615
  122.9 0.0 copy-done.8
  122.9 2.8 %collective-permute-start.6 = (f32[2,8,2048]{2,1,0:T(8,128)S(1)}, f32[2,8,2048]{2,1,0:T(8,128)S(1)}, u32[]{:S(2)}, u32[]{:S(2)}) collective-permute-start(f32[2,8,2048]{2,1,0:T(8,128)S(1)} %copy-done.8), channel_id=1, source_target_pairs={{0,5},{1,6},{2,7},{3,0},{4,1},{5,2},{6,3},{7,4},{8,13},{9,14},{10,... | collective-permute-start | bytes 393224 | tf_op jit(solution)/shard_map/ppermute | solution.py:615
  125.7 3.9 %collective-permute-done.2.rest_1_ = f32[2,8,2048]{2,1,0:T(8,128)S(1)} collective-permute-done((f32[2,8,2048]{2,1,0:T(8,128)S(1)}, f32[2,8,2048]{2,1,0:T(8,128)S(1)}, u32[]{:S(2)}, u32[]{:S(2)}) %collective-permute-start.2) | collective-permute-done | bytes 131104 | tf_op jit(solution)/shard_map/ppermute | solution.py:615
  129.6 0.0 copy-done.7
  129.6 0.0 collective-permute-start.7
  129.6 0.0 collective-permute-done.3.rest_2_
  129.6 0.1 collective-permute-start.8
  129.7 3.4 %shard_map.190.inv_hbm = f32[2,64,2048]{2,1,0:T(8,128)} custom-call(f32[16]{0:T(128)} %asig_hbm.1, s32[2,8,8,2048]{3,2,1,0:T(8,128)} %bitcast.52), custom_call_target="tpu_custom_call" | custom-call | tf_op jit(solution)/shard_map/pallas_call | solution.py:593
  133.1 0.0 collective-permute-done.4.rest_3_
  133.1 0.0 collective-permute-done.5.rest_4_
  133.1 4.7 %collective-permute-done.6.rest_5_ = f32[2,8,2048]{2,1,0:T(8,128)S(1)} collective-permute-done((f32[2,8,2048]{2,1,0:T(8,128)S(1)}, f32[2,8,2048]{2,1,0:T(8,128)S(1)}, u32[]{:S(2)}, u32[]{:S(2)}) %collective-permute-start.6) | collective-permute-done | bytes 131104 | tf_op jit(solution)/shard_map/ppermute | solution.py:615
  137.8 0.0 collective-permute-done.7.rest_6_
  137.9 2.6 %collective-permute-done.8.rest_7_ = f32[2,8,2048]{2,1,0:T(8,128)S(1)} collective-permute-done((f32[2,8,2048]{2,1,0:T(8,128)S(1)}, f32[2,8,2048]{2,1,0:T(8,128)S(1)}, u32[]{:S(2)}, u32[]{:S(2)}) %collective-permute-start.8) | collective-permute-done | bytes 131104 | tf_op jit(solution)/shard_map/ppermute | solution.py:615
  140.4 3.5 %all-to-all-done.2 = f32[32,8,1024]{2,1,0:T(8,128)S(1)} async-done(((f32[32,8,1024]{2,1,0:T(8,128)}), f32[32,8,1024]{2,1,0:T(8,128)S(1)}, u32[]{:S(2)}, u32[]{:S(2)}) %all-to-all-start.2) | async-done | bytes 1048608 | tf_op jit(solution)/shard_map/all_to_all | solution.py:697
  143.9 4.1 %shard_map.191 = (f32[2,64,2048]{2,1,0:T(8,128)}, f32[2,64,2048]{2,1,0:T(8,128)}, f32[8,64,256]{2,1,0:T(8,128)}) custom-call(s32[1]{0:T(128)} %bitcast.me_ref, f32[2]{0:T(128)S(1)} %add_multiply_fusion.weight_ref, f32[256,1024]{1,0:T(8,128)S(1)} %bitcast.48, f32[2,64,2048]{2,1,0:T(8,128)} %shard_map.190.inv_hbm, f32[2,64,2048]{2,1,0:T(8,128)} %seis_hbm.1, ...), custom_call_target="tpu_custom_call" | custom-call | tf_op jit(solution)/shard_map/pallas_call | solution.py:593
  148.0 15.9 %all_to_all.20.part_ref = f32[8,64,256]{2,1,0:T(8,128)S(1)} all-to-all(f32[8,64,256]{2,1,0:T(8,128)} %get-tuple-element.40), channel_id=1, replica_groups=mesh['slab'=32,'depth'=8] {'depth'}, dimensions={0} | all-to-all | bytes 1048576 | tf_op jit(solution)/shard_map/all_to_all | solution.py:709
  163.9 0.7 shard_map.192
  (21 shorter events, 0.1 us)
Async XLA Ops:
  1.9 9.0 %collective-permute-start = (f32[8,2048]{1,0:T(8,128)S(1)}, f32[8,2048]{1,0:T(8,128)S(1)}, u32[]{:S(2)}, u32[]{:S(2)}) collective-permute-start(f32[8,2048]{1,0:T(8,128)S(1)} %get-tuple-element.24), channel_id=1, source_target_pairs={{0,8},{8,16},{16,24},{24,32},{32,40},{40,48},{48,56},{56,64},{64,7... | collective-permute-start | bytes 196616 | tf_op jit(solution)/shard_map/ppermute | solution.py:611
  3.9 7.1 %collective-permute-start.1 = (f32[8,2048]{1,0:T(8,128)S(1)}, f32[8,2048]{1,0:T(8,128)S(1)}, u32[]{:S(2)}, u32[]{:S(2)}) collective-permute-start(f32[8,2048]{1,0:T(8,128)S(1)} %get-tuple-element.25), channel_id=1, source_target_pairs={{8,0},{16,8},{24,16},{32,24},{40,32},{48,40},{56,48},{64,56},{72,6... | collective-permute-start | bytes 196616 | tf_op jit(solution)/shard_map/ppermute | solution.py:611
  12.1 6.2 %copy-start.4 = (s32[512,3]{0,1:T(4,128)S(1)}, s32[512,3]{0,1:T(4,128)}, u32[]{:S(2)}) copy-start(s32[512,3]{0,1:T(4,128)} %param.21) | copy-start | bytes 18436
  12.1 6.4 %copy-start.5 = (s32[2,512]{1,0:T(2,128)S(1)}, s32[2,512]{1,0:T(2,128)}, u32[]{:S(2)}) copy-start(s32[2,512]{1,0:T(2,128)} %param.22) | copy-start | bytes 12292
  12.1 44.1 %copy-start.1 = (f32[2,16,128]{2,1,0:T(8,128)S(1)}, f32[2,16,128]{2,1,0:T(8,128)}, u32[]{:S(2)}) copy-start(f32[2,16,128]{2,1,0:T(8,128)} %constant.102.clone.twist_ref) | copy-start | bytes 49156
  12.2 44.1 %all-to-all-start = ((f32[8,11,8,1024]{3,2,1,0:T(8,128)}), f32[8,11,8,1024]{3,2,1,0:T(8,128)S(1)}, u32[]{:S(2)}, u32[]{:S(2)}) async-start(f32[8,11,8,1024]{3,2,1,0:T(8,128)} %shard_map.186), calls=%async_computation | async-start | bytes 5767168 | tf_op jit(solution)/shard_map/all_to_all | solution.py:676
  56.3 17.6 %copy-start.3 = (f32[2048,64]{0,1:T(8,128)S(1)}, f32[2048,64]{0,1:T(8,128)}, u32[]{:S(2)}) copy-start(f32[2048,64]{0,1:T(8,128)} %param.23) | copy-start | bytes 1572868
  62.6 41.3 %all-to-all-start.1 = ((f32[256,8,128]{2,1,0:T(8,128)}), f32[256,8,128]{2,1,0:T(8,128)S(1)}, u32[]{:S(2)}, u32[]{:S(2)}) async-start(f32[256,8,128]{2,1,0:T(8,128)} %bitcast.56), calls=%async_computation.1 | async-start | bytes 2097152 | tf_op jit(solution)/shard_map/all_to_all | solution.py:686
  81.8 22.1 %copy-start.2 = (f32[2,8,128]{2,1,0:T(8,128)S(1)}, f32[2,8,128]{2,1,0:T(8,128)}, u32[]{:S(2)}) copy-start(f32[2,8,128]{2,1,0:T(8,128)} %constant.104.clone.in_ref) | copy-start | bytes 24580
  103.9 10.9 %copy-start.12 = (f32[2,8,2048]{2,1,0:T(8,128)S(1)}, f32[2,8,2048]{2,1,0:T(8,128)}, u32[]{:S(2)}) copy-start(f32[2,8,2048]{2,1,0:T(8,128)} %get-tuple-element.31) | copy-start | bytes 393220
  103.9 12.6 %copy-start.11 = (f32[2,8,2048]{2,1,0:T(8,128)S(1)}, f32[2,8,2048]{2,1,0:T(8,128)}, u32[]{:S(2)}) copy-start(f32[2,8,2048]{2,1,0:T(8,128)} %get-tuple-element.32) | copy-start | bytes 393220
  103.9 13.3 %copy-start.10 = (f32[2,8,2048]{2,1,0:T(8,128)S(1)}, f32[2,8,2048]{2,1,0:T(8,128)}, u32[]{:S(2)}) copy-start(f32[2,8,2048]{2,1,0:T(8,128)} %get-tuple-element.33) | copy-start | bytes 393220
  103.9 16.1 %copy-start.9 = (f32[2,8,2048]{2,1,0:T(8,128)S(1)}, f32[2,8,2048]{2,1,0:T(8,128)}, u32[]{:S(2)}) copy-start(f32[2,8,2048]{2,1,0:T(8,128)} %get-tuple-element.34) | copy-start | bytes 393220
  103.9 19.0 %copy-start.8 = (f32[2,8,2048]{2,1,0:T(8,128)S(1)}, f32[2,8,2048]{2,1,0:T(8,128)}, u32[]{:S(2)}) copy-start(f32[2,8,2048]{2,1,0:T(8,128)} %get-tuple-element.35) | copy-start | bytes 393220
  104.0 25.7 %copy-start.7 = (f32[2,8,2048]{2,1,0:T(8,128)S(1)}, f32[2,8,2048]{2,1,0:T(8,128)}, u32[]{:S(2)}) copy-start(f32[2,8,2048]{2,1,0:T(8,128)} %get-tuple-element.36) | copy-start | bytes 393220
  104.0 25.7 %copy-start.6 = (f32[2,8,2048]{2,1,0:T(8,128)S(1)}, f32[2,8,2048]{2,1,0:T(8,128)}, u32[]{:S(2)}) copy-start(f32[2,8,2048]{2,1,0:T(8,128)} %get-tuple-element.37) | copy-start | bytes 393220
  109.5 34.4 %copy-start = (f32[2,8,2048]{2,1,0:T(8,128)S(1)}, f32[2,8,2048]{2,1,0:T(8,128)}, u32[]{:S(2)}) copy-start(f32[2,8,2048]{2,1,0:T(8,128)} %get-tuple-element.30.rest_0_) | copy-start | bytes 393220
  109.5 34.4 %all-to-all-start.2 = ((f32[32,8,1024]{2,1,0:T(8,128)}), f32[32,8,1024]{2,1,0:T(8,128)S(1)}, u32[]{:S(2)}, u32[]{:S(2)}) async-start(f32[32,8,1024]{2,1,0:T(8,128)} %bitcast.54), calls=%async_computation.2 | async-start | bytes 2097152 | tf_op jit(solution)/shard_map/all_to_all | solution.py:697
  114.9 14.8 %collective-permute-start.2 = (f32[2,8,2048]{2,1,0:T(8,128)S(1)}, f32[2,8,2048]{2,1,0:T(8,128)S(1)}, u32[]{:S(2)}, u32[]{:S(2)}) collective-permute-start(f32[2,8,2048]{2,1,0:T(8,128)S(1)} %copy-done.12), channel_id=1, source_target_pairs={{0,1},{1,2},{2,3},{3,4},{4,5},{5,6},{6,7},{7,0},{8,9},{9,10},{10,1... | collective-permute-start | bytes 393224 | tf_op jit(solution)/shard_map/ppermute | solution.py:615
  116.5 13.1 %collective-permute-start.3 = (f32[2,8,2048]{2,1,0:T(8,128)S(1)}, f32[2,8,2048]{2,1,0:T(8,128)S(1)}, u32[]{:S(2)}, u32[]{:S(2)}) collective-permute-start(f32[2,8,2048]{2,1,0:T(8,128)S(1)} %copy-done.11), channel_id=1, source_target_pairs={{0,2},{1,3},{2,4},{3,5},{4,6},{5,7},{6,0},{7,1},{8,10},{9,11},{10,... | collective-permute-start | bytes 393224 | tf_op jit(solution)/shard_map/ppermute | solution.py:615
  117.2 15.9 %collective-permute-start.4 = (f32[2,8,2048]{2,1,0:T(8,128)S(1)}, f32[2,8,2048]{2,1,0:T(8,128)S(1)}, u32[]{:S(2)}, u32[]{:S(2)}) collective-permute-start(f32[2,8,2048]{2,1,0:T(8,128)S(1)} %copy-done.10), channel_id=1, source_target_pairs={{0,3},{1,4},{2,5},{3,6},{4,7},{5,0},{6,1},{7,2},{8,11},{9,12},{10,... | collective-permute-start | bytes 393224 | tf_op jit(solution)/shard_map/ppermute | solution.py:615
  120.0 13.1 %collective-permute-start.5 = (f32[2,8,2048]{2,1,0:T(8,128)S(1)}, f32[2,8,2048]{2,1,0:T(8,128)S(1)}, u32[]{:S(2)}, u32[]{:S(2)}) collective-permute-start(f32[2,8,2048]{2,1,0:T(8,128)S(1)} %copy-done.9), channel_id=1, source_target_pairs={{0,4},{1,5},{2,6},{3,7},{4,0},{5,1},{6,2},{7,3},{8,12},{9,13},{10,... | collective-permute-start | bytes 393224 | tf_op jit(solution)/shard_map/ppermute | solution.py:615
  122.9 15.0 %collective-permute-start.6 = (f32[2,8,2048]{2,1,0:T(8,128)S(1)}, f32[2,8,2048]{2,1,0:T(8,128)S(1)}, u32[]{:S(2)}, u32[]{:S(2)}) collective-permute-start(f32[2,8,2048]{2,1,0:T(8,128)S(1)} %copy-done.8), channel_id=1, source_target_pairs={{0,5},{1,6},{2,7},{3,0},{4,1},{5,2},{6,3},{7,4},{8,13},{9,14},{10,... | collective-permute-start | bytes 393224 | tf_op jit(solution)/shard_map/ppermute | solution.py:615
  129.6 8.2 %collective-permute-start.7 = (f32[2,8,2048]{2,1,0:T(8,128)S(1)}, f32[2,8,2048]{2,1,0:T(8,128)S(1)}, u32[]{:S(2)}, u32[]{:S(2)}) collective-permute-start(f32[2,8,2048]{2,1,0:T(8,128)S(1)} %copy-done.7), channel_id=1, source_target_pairs={{0,6},{1,7},{2,0},{3,1},{4,2},{5,3},{6,4},{7,5},{8,14},{9,15},{10,... | collective-permute-start | bytes 393224 | tf_op jit(solution)/shard_map/ppermute | solution.py:615
  129.6 10.8 %collective-permute-start.8 = (f32[2,8,2048]{2,1,0:T(8,128)S(1)}, f32[2,8,2048]{2,1,0:T(8,128)S(1)}, u32[]{:S(2)}, u32[]{:S(2)}) collective-permute-start(f32[2,8,2048]{2,1,0:T(8,128)S(1)} %copy-done.6), channel_id=1, source_target_pairs={{0,7},{1,0},{2,1},{3,2},{4,3},{5,4},{6,5},{7,6},{8,15},{9,8},{10,9... | collective-permute-start | bytes 393224 | tf_op jit(solution)/shard_map/ppermute | solution.py:615
